TPU v7x, 32 devices: a whole 2x2x4 slice. The times are simulated.
32 devices in a mesh: dom: 32 (over z, y, x, core).
Axes of the slice: x: 2, y: 2, z: 4, core: 2. Of those that a mesh axis runs over, the one named last changes fastest.
Arguments:
- dof_values: float32 [9, 20, 8192], P(None, None, 'dom'), may hold values from -6 to 6
- star_mats: bfloat16 [3, 9, 9, 8192], P(None, None, None, 'dom'), may hold values from -0.1796875 to 0.1796875
- flux_local: bfloat16 [4, 9, 9, 8192], P(None, None, None, 'dom'), may hold values from -0.19921875 to 0.19921875
- flux_neigh: bfloat16 [4, 9, 9, 8192], P(None, None, None, 'dom'), may hold values from -0.19921875 to 0.19921875
- kstiff: float32 [3, 20, 20], replicated, may hold values from -1.25 to 1.25
- flux_minus: float32 [4, 20, 20], replicated, may hold values from -1.25 to 1.25
- flux_plus: float32 [4, 4, 20, 20], replicated, may hold values from -1.25 to 1.25
- neighbour: int32 [4, 8192], P(None, 'dom'), may hold values from 0 to 511, as said below
- neigh_face: int32 [4, 8192], P(None, 'dom'), may hold values from 0 to 3
- cluster: int32 [8192], P('dom'), may hold values from 0 to 1
- send_list: int32 [32, 4, 64], P('dom'), may hold values from 0 to 255
- damage_list: int32 [32, 256], P('dom'), may hold values from 0 to 255, as said below
- damage_count: int32 [32], P('dom'), may hold values from 0 to 256, as said below
- yield_mask: int32 [20, 8192], P(None, 'dom'), may hold values 0 or 1
- cohesion: float32 [8192], P('dom'), may hold values from 0.3 to 3
- to_points: float32 [20, 20], replicated, may hold values from -1.25 to 1.25
- from_points: float32 [20, 20], replicated, may hold values from -1.25 to 1.25
Outputs:
- new_dofs: float32 [9, 20, 8192], P(None, None, 'dom')
Inputs may be any that keep to these rules, and one draw needn't show every extreme that they name: `neighbour`: entries below 256 are elements of the same partition; the entry 256 + j * 64 + i names ghost slot i of offset slot j. `damage_list`: the entries of one partition's row are distinct. `damage_count`: some partition has exactly 256.
All inputs are finite; a program needn't handle non-finite values. No bound on the sum of `yield_mask` on one device may be relied on, other than what follows from the above.
Results may differ from a plain program's by a relative error of at most 0.0003.
Values sent between devices are 32-bit elements; how exact they have to be, the bound alone decides.
No kernel may reach another device: no remote copies, remote signals or barrier semaphores. Data moves between devices by JAX's collectives and lax.ppermute only.
A program may use at most 128 MiB of HBM per device.

v0:
```python
import jax
import jax.numpy as jnp
from jax import lax
from jax.sharding import PartitionSpec as P

NDER = 3
BLK = 128


PRECISE = lax.Precision.HIGHEST
OFFSETS = (1, -1, 2, -2)
FRICTION = 0.6
RELAXATION = 0.5


def from_behind(block, axis, distance):
    devices = range(lax.axis_size(axis))
    route = [(i - distance, i) for i in devices if i - distance in devices]
    return lax.ppermute(block, axis, route)


def star_apply(source, matrix):
    wide = matrix.astype(jnp.float32)
    total = source[0][None, :, :] * wide[0][:, None, :]
    for quantity in range(1, source.shape[0]):
        total = total + source[quantity][None, :, :] * wide[quantity][:, None, :]
    return total


def derivatives(source, star_part, kstiff):
    series = [source]
    for degree in range(NDER - 1):
        latest = series[-1]
        following = jnp.zeros_like(latest)
        for direction in range(3):
            rotated = star_apply(latest, star_part[direction])
            following = following + jnp.einsum(
                "bc,pce->pbe", kstiff[direction], rotated, precision=PRECISE
            )
        series.append(following)
    return series


def taylor(series, time_begin, time_end):
    summed = jnp.zeros_like(series[0])
    divisor = 1.0
    for degree in range(len(series)):
        divisor = divisor * (degree + 1)
        weight_now = (time_end ** (degree + 1) - time_begin ** (degree + 1)) / divisor
        summed = summed + weight_now * series[degree]
    return summed


def volume(integral, star_part, kstiff):
    summed = jnp.zeros_like(integral)
    for direction in range(3):
        rotated = star_apply(integral, star_part[direction])
        summed = summed + jnp.einsum("cb,pce->pbe", kstiff[direction], rotated, precision=PRECISE)
    return summed


def face_values(extended, neighbours):
    return jnp.stack([jnp.take(extended, neighbours[face_id], axis=2) for face_id in range(4)])


def surface(integral, others, neigh_faces, local_flux, neigh_flux, flux_minus, flux_plus):
    summed = jnp.zeros_like(integral)
    for face_id in range(4):
        own_side = star_apply(integral, local_flux[face_id])
        summed = summed + jnp.einsum(
            "bc,pce->pbe", flux_minus[face_id], own_side, precision=PRECISE
        )
        far_side = star_apply(others[face_id], neigh_flux[face_id])
        selector = (
            neigh_faces[face_id][None, :] == jnp.arange(4, dtype=jnp.int32)[:, None]
        ).astype(jnp.float32)
        masked = far_side[None] * selector[:, None, None, :]
        summed = summed + jnp.einsum("hbc,hpce->pbe", flux_plus[face_id], masked, precision=PRECISE)
    return summed


def plastic(stress, strength, plastic_mask, to_points, from_points):
    points = jnp.einsum("nb,qbp->qnp", to_points, stress, precision=PRECISE)
    pressure = (points[0] + points[1] + points[2]) / 3.0
    normal = points[:3] - pressure[None]
    shear_part = points[3:]
    tau_eff = jnp.sqrt(
        0.5 * jnp.sum(normal * normal, axis=0) + jnp.sum(shear_part * shear_part, axis=0)
    )
    yield_limit = jnp.maximum(strength[None, :] - FRICTION * pressure, 0.5 * strength[None, :])
    rate_now = jnp.where(
        plastic_mask > 0.5,
        RELAXATION * (yield_limit / jnp.maximum(tau_eff, yield_limit) - 1.0),
        0.0,
    )
    change = jnp.concatenate([normal, shear_part], axis=0) * rate_now[None]
    return jnp.einsum("bn,qnp->qbp", from_points, change, precision=PRECISE)


def exchange_ghosts(buffer, send_list):
    pieces = []
    for slot_id in range(len(OFFSETS)):
        outgoing = jnp.take(buffer, send_list[0, slot_id], axis=2)
        pieces.append(from_behind(outgoing, "dom", OFFSETS[slot_id]))
    return jnp.concatenate(pieces, axis=2)


def run_blocks(stress, strength, plastic_mask, live_count, to_points, from_points):
    summed = jnp.zeros_like(stress)
    block_count = (live_count + BLK - 1) // BLK

    def one_block(block_id, carried):
        first_row = block_id * BLK
        result_part = plastic(
            lax.dynamic_slice_in_dim(stress, first_row, BLK, 2),
            lax.dynamic_slice_in_dim(strength, first_row, BLK, 0),
            lax.dynamic_slice_in_dim(plastic_mask, first_row, BLK, 1),
            to_points,
            from_points,
        )
        live_slots = (first_row + jnp.arange(BLK, dtype=jnp.int32) < live_count).astype(jnp.float32)
        return lax.dynamic_update_slice_in_dim(
            carried, result_part * live_slots[None, None, :], first_row, 2
        )

    return lax.fori_loop(0, block_count, one_block, summed)


def per_device(
    dof_values,
    star_mats,
    flux_local,
    flux_neigh,
    kstiff,
    flux_minus,
    flux_plus,
    neighbour,
    neigh_face,
    cluster,
    send_list,
    damage_list,
    damage_count,
    yield_mask,
    cohesion,
    to_points,
    from_points,
):
    is_fine = (cluster == 0)[None, None, :]
    first_series = derivatives(dof_values, star_mats, kstiff)
    buffer_one = taylor(first_series, 0.0, 1.0)
    ghost_one = exchange_ghosts(buffer_one, send_list)
    others = face_values(jnp.concatenate([buffer_one, ghost_one], axis=2), neighbour)
    updated = (
        dof_values
        + volume(buffer_one, star_mats, kstiff)
        - surface(buffer_one, others, neigh_face, flux_local, flux_neigh, flux_minus, flux_plus)
    )
    state_one = jnp.where(is_fine, updated, dof_values)
    second_series = derivatives(state_one, star_mats, kstiff)
    buffer_two = jnp.where(
        is_fine, taylor(second_series, 0.0, 1.0), taylor(second_series, 1.0, 2.0)
    )
    ghost_two = exchange_ghosts(buffer_two, send_list)
    summed_buffer = buffer_one + buffer_two
    fine_side = face_values(jnp.concatenate([buffer_two, ghost_two], axis=2), neighbour)
    coarse_side = face_values(
        jnp.concatenate([summed_buffer, ghost_one + ghost_two], axis=2), neighbour
    )
    others = jnp.where(is_fine[None], fine_side, coarse_side)
    integral = jnp.where(is_fine, buffer_two, summed_buffer)
    state_two = (
        state_one
        + volume(integral, star_mats, kstiff)
        - surface(integral, others, neigh_face, flux_local, flux_neigh, flux_minus, flux_plus)
    )
    listing = damage_list[0]
    live_count = damage_count[0]
    stress = jnp.take(state_two[:6], listing, axis=2)
    strength = jnp.take(cohesion, listing)
    plastic_mask = jnp.take(yield_mask, listing, axis=1).astype(jnp.float32)
    correction = run_blocks(stress, strength, plastic_mask, live_count, to_points, from_points)
    return state_two.at[:6, :, listing].add(correction)


def solution(mesh):
    return jax.shard_map(
        per_device,
        mesh=mesh,
        in_specs=(
            P(None, None, "dom"),
            P(None, None, None, "dom"),
            P(None, None, None, "dom"),
            P(None, None, None, "dom"),
            P(),
            P(),
            P(),
            P(None, "dom"),
            P(None, "dom"),
            P("dom"),
            P("dom", None, None),
            P("dom", None),
            P("dom"),
            P(None, "dom"),
            P("dom"),
            P(),
            P(),
        ),
        out_specs=P(None, None, "dom"),
        check_vma=False,
    )
```

profile of v0, /device:TPU:24, one launch (start us, length us, event | category | flops | bytes accessed | tf_op | source)
XLA Modules:
  0.0 1757.9 jit_solution(14036002622855102805)
XLA Ops:
  12.9 5.4 collective-permute-start.1
  23.4 5.7 collective-permute-start.3
  50.3 4.1 copy.185
  54.5 3.1 gather_fusion.7
  59.5 3.0 gather_fusion.8
  69.8 3.1 gather_fusion.9
  80.2 2.9 gather_fusion.10
  111.8 5.4 collective-permute-start.5
  120.6 5.7 collective-permute-start.7
  129.2 3.9 copy.250
  133.2 4.3 gather_fusion.15
  137.4 4.2 gather_fusion.16
  143.0 3.7 copy.258
  146.7 4.3 gather_fusion.19
  150.9 4.3 gather_fusion.20
  155.3 4.3 gather_fusion.17
  159.5 4.3 gather_fusion.21
  163.8 4.3 gather_fusion.18
  168.1 4.3 gather_fusion.22
  172.4 3.6 select_bitcast_fusion.3
  178.6 3.6 select_bitcast_fusion.2
  184.7 3.7 select_bitcast_fusion.1
  191.0 3.7 select_bitcast_fusion
  216.1 1540.3 %while.14 = (s32[]{:T(128)}, f32[9,20,256]{1,2,0:T(8,128)S(1)}, s32[256,2]{0,1:T(2,128)S(1)}, f32[256,6,20]{2,0,1:T(8,128)S(1)}, s32[]{:T(128)}, /*index=5*/s32[3]{0:T(128)S(1)}, s32[1]{0:T(128)}, s32[]{:T(128)}) while((s32[]{:T(128)}, f32[9,20,256]{1,2,0:T(8,128)S(1)}, s32[256,2]{0,1:T(2,128)S(1)}, f32[256,6,20]{2,0,1:T(8,128)S(1)}, s32[]{:T(128)}, ...), condition=%wide.while_cond, body=%wide.while_body.sunk | while | flops 259 | bytes 2563 | solution.py:182
  (2231 shorter events, 1648.5 us)
Async XLA Ops:
  8.9 40.2 %collective-permute-start = (f32[9,20,64]{2,1,0:T(8,128)}, f32[9,20,64]{2,1,0:T(8,128)}, u32[]{:S(2)}, u32[]{:S(2)}) collective-permute-start(f32[9,20,64]{2,1,0:T(8,128)} %select_bitcast_fusion.20), channel_id=1, source_target_pairs={{0,1},{1,2},{2,3},{3,4},{4,5},{5,6},{6,7},{7,8},{8,9},{9,10},{10,1... | collective-permute-start | bytes 138248 | tf_op jit(solution)/shard_map/ppermute | solution.py:19
  12.9 36.2 %collective-permute-start.1 = (f32[9,20,64]{2,1,0:T(8,128)}, f32[9,20,64]{2,1,0:T(8,128)}, u32[]{:S(2)}, u32[]{:S(2)}) collective-permute-start(f32[9,20,64]{2,1,0:T(8,128)} %select_bitcast_fusion.19), channel_id=1, source_target_pairs={{1,0},{2,1},{3,2},{4,3},{5,4},{6,5},{7,6},{8,7},{9,8},{10,9},{11,1... | collective-permute-start | bytes 138248 | tf_op jit(solution)/shard_map/ppermute | solution.py:19
  20.5 28.6 %collective-permute-start.2 = (f32[9,20,64]{2,1,0:T(8,128)}, f32[9,20,64]{2,1,0:T(8,128)}, u32[]{:S(2)}, u32[]{:S(2)}) collective-permute-start(f32[9,20,64]{2,1,0:T(8,128)} %select_bitcast_fusion.18), channel_id=1, source_target_pairs={{0,2},{1,3},{2,4},{3,5},{4,6},{5,7},{6,8},{7,9},{8,10},{9,11},{10,... | collective-permute-start | bytes 138248 | tf_op jit(solution)/shard_map/ppermute | solution.py:19
  23.4 25.7 %collective-permute-start.3 = (f32[9,20,64]{2,1,0:T(8,128)S(1)}, f32[9,20,64]{2,1,0:T(8,128)S(1)}, u32[]{:S(2)}, u32[]{:S(2)}) collective-permute-start(f32[9,20,64]{2,1,0:T(8,128)S(1)} %select_bitcast_fusion.17), channel_id=1, source_target_pairs={{2,0},{3,1},{4,2},{5,3},{6,4},{7,5},{8,6},{9,7},{10,8},{11,9},{12,... | collective-permute-start | bytes 138248 | tf_op jit(solution)/shard_map/ppermute | solution.py:19
  33.2 52.5 %copy-start.9 = (f32[1,4,20,20]{3,1,2,0:T(4,128)}, f32[1,4,20,20]{3,1,2,0:T(4,128)S(1)}, u32[]{:S(2)}) copy-start(f32[1,4,20,20]{3,1,2,0:T(4,128)S(1)} %get-tuple-element.357) | copy-start | bytes 19204
  33.2 53.6 %copy-start.7 = (f32[1,4,20,20]{3,1,2,0:T(4,128)}, f32[1,4,20,20]{3,1,2,0:T(4,128)S(1)}, u32[]{:S(2)}) copy-start(f32[1,4,20,20]{3,1,2,0:T(4,128)S(1)} %get-tuple-element.359) | copy-start | bytes 19204
  33.2 54.7 %copy-start.5 = (f32[1,4,20,20]{3,1,2,0:T(4,128)}, f32[1,4,20,20]{3,1,2,0:T(4,128)S(1)}, u32[]{:S(2)}) copy-start(f32[1,4,20,20]{3,1,2,0:T(4,128)S(1)} %get-tuple-element.358) | copy-start | bytes 19204
  36.2 50.2 %copy-start.109 = (f32[9,256]{1,0:T(8,128)}, f32[9,256]{1,0:T(8,128)S(1)}, u32[]{:S(2)}) copy-start(f32[9,256]{1,0:T(8,128)S(1)} %get-tuple-element.406) | copy-start | bytes 27652
  36.2 50.3 %copy-start.111 = (f32[9,256]{1,0:T(8,128)}, f32[9,256]{1,0:T(8,128)S(1)}, u32[]{:S(2)}) copy-start(f32[9,256]{1,0:T(8,128)S(1)} %get-tuple-element.407) | copy-start | bytes 27652
  36.2 50.3 %copy-start.113 = (f32[9,256]{1,0:T(8,128)}, f32[9,256]{1,0:T(8,128)S(1)}, u32[]{:S(2)}) copy-start(f32[9,256]{1,0:T(8,128)S(1)} %get-tuple-element.408) | copy-start | bytes 27652
  36.2 50.3 %copy-start.115 = (f32[9,256]{1,0:T(8,128)}, f32[9,256]{1,0:T(8,128)S(1)}, u32[]{:S(2)}) copy-start(f32[9,256]{1,0:T(8,128)S(1)} %get-tuple-element.409) | copy-start | bytes 27652
  36.2 50.3 %copy-start.117 = (f32[9,256]{1,0:T(8,128)}, f32[9,256]{1,0:T(8,128)S(1)}, u32[]{:S(2)}) copy-start(f32[9,256]{1,0:T(8,128)S(1)} %get-tuple-element.410) | copy-start | bytes 27652
  36.2 50.3 %copy-start.119 = (f32[9,256]{1,0:T(8,128)}, f32[9,256]{1,0:T(8,128)S(1)}, u32[]{:S(2)}) copy-start(f32[9,256]{1,0:T(8,128)S(1)} %get-tuple-element.411) | copy-start | bytes 27652
  36.2 50.3 %copy-start.121 = (f32[9,256]{1,0:T(8,128)}, f32[9,256]{1,0:T(8,128)S(1)}, u32[]{:S(2)}) copy-start(f32[9,256]{1,0:T(8,128)S(1)} %get-tuple-element.412) | copy-start | bytes 27652
  36.2 50.3 %copy-start.123 = (f32[9,256]{1,0:T(8,128)}, f32[9,256]{1,0:T(8,128)S(1)}, u32[]{:S(2)}) copy-start(f32[9,256]{1,0:T(8,128)S(1)} %get-tuple-element.413) | copy-start | bytes 27652
  36.3 50.4 %copy-start.203 = (f32[4,256]{1,0:T(4,128)}, f32[4,256]{1,0:T(4,128)S(1)}, u32[]{:S(2)}) copy-start(f32[4,256]{1,0:T(4,128)S(1)} %fusion.1012) | copy-start | bytes 12292
  37.6 49.9 %copy-start.91 = (f32[9,256]{1,0:T(8,128)}, f32[9,256]{1,0:T(8,128)S(1)}, u32[]{:S(2)}) copy-start(f32[9,256]{1,0:T(8,128)S(1)} %get-tuple-element.415) | copy-start | bytes 27652
  37.7 50.2 %copy-start.202 = (f32[4,256]{1,0:T(4,128)}, f32[4,256]{1,0:T(4,128)S(1)}, u32[]{:S(2)}) copy-start(f32[4,256]{1,0:T(4,128)S(1)} %fusion.1013) | copy-start | bytes 12292
  42.4 51.9 %copy-start.19 = (f32[9,256]{1,0:T(8,128)}, f32[9,256]{1,0:T(8,128)S(1)}, u32[]{:S(2)}) copy-start(f32[9,256]{1,0:T(8,128)S(1)} %get-tuple-element.361) | copy-start | bytes 27652
  107.9 21.1 %collective-permute-start.4 = (f32[9,20,64]{2,1,0:T(8,128)S(1)}, f32[9,20,64]{2,1,0:T(8,128)S(1)}, u32[]{:S(2)}, u32[]{:S(2)}) collective-permute-start(f32[9,20,64]{2,1,0:T(8,128)S(1)} %select_bitcast_fusion.16), channel_id=1, source_target_pairs={{0,1},{1,2},{2,3},{3,4},{4,5},{5,6},{6,7},{7,8},{8,9},{9,10},{10,1... | collective-permute-start | bytes 138248 | tf_op jit(solution)/shard_map/ppermute | solution.py:19
  111.8 17.2 collective-permute-start.5
  118.5 10.5 collective-permute-start.6
  120.6 8.4 collective-permute-start.7
  215.8 1541.7 %copy-start.1 = (f32[256]{0:T(256)S(1)}, f32[256]{0:T(256)}, u32[]{:S(2)}) copy-start(f32[256]{0:T(256)} %param.37) | copy-start | bytes 3076
  (333 other events, 2458.5 us)
where the time goes:
time: 1790 us; the launch traced here: 1760 us
  other arithmetic  1050 us (59%)
  local copies, waits for them, and re-layouts  633 us (35%)
  starting transfers between devices  30 us (2%)
  matrix products  26.6 us (1%)
    scatter-add x512, other arithmetic  1020 us
    scatter-add x768, local copies, waits for them, and re-layouts  511 us
    gather x12, local copies, waits for them, and re-layouts, face_values(): jnp.take(extended, neighbours[face_id], axis=2)  46.2 us
  transfers between devices with their start and end apart: 8, of which 0 were waited for; matrix products, arithmetic and copies ran while one was open for 2% of the time, Pallas kernels for 0%

commit v1 on v0

v1 whole, which is shorter than its diff:
```python
import jax
import jax.numpy as jnp
from jax import lax
from jax.experimental import pallas as pl
from jax.experimental.pallas import tpu as pltpu
from jax.sharding import PartitionSpec as P

NQ = 9
NB = 20
R = 24
K3 = 3 * R
LANES = 128
FRICTION = 0.6
RELAXATION = 0.5
F32 = jnp.float32
BF16 = jnp.bfloat16


def stack_weights(w):
    w = jnp.pad(w, [(0, 0)] * (w.ndim - 2) + [(0, R - NB), (0, R - NB)])
    high = lax.reduce_precision(w, 8, 7)
    low = w - high
    return jnp.concatenate([high, high, low], axis=-1).astype(BF16)


def stack_values(x):
    high = x.astype(BF16).astype(F32)
    return jnp.concatenate([high, x - high, high], axis=0).astype(BF16)


def dot(a, b):
    return jnp.dot(a, b, preferred_element_type=F32)


def widen(src_ref, dst_ref, base):
    blocks = src_ref.shape[0]

    def one(k, _):
        for q in range(NQ):
            dst_ref[(base + k) * NQ + q] = src_ref[k, q].astype(F32)
        return 0

    lax.fori_loop(0, blocks, one, 0)


def basis_products(weights, x_ref, y_ref, blocks, base=0):
    for q in range(NQ):
        out = dot(weights, stack_values(x_ref[q]))
        for k in range(blocks):
            y_ref[base + k, q] = out[k * R : (k + 1) * R]


def star_sum(y_ref, m_ref, blocks, lanes, start):
    def one(k, acc):
        acc = list(acc)
        for q in range(NQ):
            y = y_ref[k, q, :, lanes]
            for p in range(NQ):
                acc[p] = acc[p] + y * m_ref[k * NQ + q, p : p + 1, lanes]
        return tuple(acc)

    return lax.fori_loop(0, blocks, one, tuple(start))


def each_half(elements, body):
    def one(half, _):
        body(pl.ds(pl.multiple_of(half * LANES, LANES), LANES))
        return 0

    lax.fori_loop(0, elements // LANES, one, 0)


def taylor_buffer(x_ref, first_ref, y_ref, m_ref, wk, weights_at, out_ref):
    elements = x_ref.shape[-1]
    basis_products(wk, x_ref, y_ref, 3)

    def first(lanes):
        acc = star_sum(y_ref, m_ref, 3, lanes, [jnp.zeros((R, LANES), F32)] * NQ)
        for p in range(NQ):
            first_ref[p, :, lanes] = acc[p]

    each_half(elements, first)
    basis_products(wk, first_ref, y_ref, 3)

    def second(lanes):
        acc = star_sum(y_ref, m_ref, 3, lanes, [jnp.zeros((R, LANES), F32)] * NQ)
        w1, w2 = weights_at(lanes)
        for p in range(NQ):
            out_ref[p, :, lanes] = x_ref[p, :, lanes] + (w1 * first_ref[p, :, lanes] + w2 * acc[p])

    each_half(elements, second)


def send_blocks(b_ref, send_ref, near_ref, far_ref):
    elements = b_ref.shape[-1]
    columns = send_ref.shape[-1]
    b = b_ref[...].reshape(NQ * R, elements)
    high = b.astype(BF16)
    low = (b - high.astype(F32)).astype(BF16)
    rows = lax.broadcasted_iota(jnp.int32, (elements, columns), 0)
    hot = jnp.where(rows == send_ref[...], 1.0, 0.0).astype(BF16)
    out = dot(high, hot) + dot(low, hot)
    near_ref[...] = out[:, : columns // 2]
    far_ref[...] = out[:, columns // 2 :]


def far_sides(source, index_ref, face_ref, wf_ref, g_ref, y_ref, base):
    depth = source.shape[-1]
    high = source.astype(BF16)
    low = (source - high.astype(F32)).astype(BF16)
    both = jnp.concatenate([high, low], axis=0)
    rows = lax.broadcasted_iota(jnp.int32, (depth, index_ref.shape[-1]), 0)
    size = NQ * R

    def one(f, _):
        hot = jnp.where(rows == index_ref[pl.ds(f, 1), :], 1.0, 0.0).astype(BF16)
        g_ref[...] = dot(both, hot)
        kind = jnp.broadcast_to(face_ref[pl.ds(f, 1), :], (R, index_ref.shape[-1]))
        w = wf_ref[f]
        for q in range(NQ):
            high_rows = g_ref[q * R : (q + 1) * R]
            low_rows = g_ref[size + q * R : size + (q + 1) * R]
            out = dot(w, jnp.concatenate([high_rows, low_rows, high_rows], axis=0).astype(BF16))
            y_ref[base + f, q] = jnp.where(
                kind < 2,
                jnp.where(kind == 0, out[:R], out[R : 2 * R]),
                jnp.where(kind == 2, out[2 * R : 3 * R], out[3 * R :]),
            )
        return 0

    lax.fori_loop(0, 4, one, 0)


def predict_kernel(dof_ref, star_ref, wk_ref, send_ref, b_ref, near_ref, far_ref, x_ref, first_ref, y_ref, m_ref):
    widen(star_ref, m_ref, 0)
    x_ref[:, NB:, :] = jnp.zeros((NQ, R - NB, x_ref.shape[-1]), F32)
    x_ref[:, :NB, :] = dof_ref[...]
    taylor_buffer(x_ref, first_ref, y_ref, m_ref, wk_ref[...], lambda lanes: (0.5, 1.0 / 6.0), b_ref)
    send_blocks(b_ref, send_ref, near_ref, far_ref)


def local_kernel(
    base_ref, b_ref, star_ref, local_ref, neigh_ref, wv_ref, wf_ref, index_ref, face_ref, out_ref, y_ref, m_ref, g_ref
):
    elements = b_ref.shape[-1]
    rows = base_ref.shape[1]
    widen(star_ref, m_ref, 0)
    widen(local_ref, m_ref, 3)
    widen(neigh_ref, m_ref, 7)
    basis_products(wv_ref[...], b_ref, y_ref, 7)
    far_sides(b_ref[...].reshape(NQ * R, elements), index_ref, face_ref, wf_ref, g_ref, y_ref, 7)

    def body(lanes):
        acc = star_sum(y_ref, m_ref, 11, lanes, [jnp.zeros((R, LANES), F32)] * NQ)
        for p in range(NQ):
            out_ref[p, :, lanes] = acc[p]

    each_half(elements, body)
    out_ref[:, :rows, :] = out_ref[:, :rows, :] + base_ref[...]


def ghost_index(pos_ref, index_ref, ghost_ref, elements, ghosts):
    me, total = pos_ref[0], pos_ref[1]
    core = me % 2
    chip = (me // 2) % 2
    width = 2 * ghosts
    up = jnp.where(chip == 0, width, 2 * width)
    down = jnp.where(chip == 0, 2 * width, width)
    nowhere = -8 * width
    starts = (
        jnp.where(me >= 1, jnp.where(core == 1, 0, down), nowhere),
        jnp.where(me <= total - 2, jnp.where(core == 0, ghosts, up + ghosts), nowhere),
        jnp.where(me >= 2, down + ghosts, nowhere),
        jnp.where(me <= total - 3, up, nowhere),
    )
    index = index_ref[...] - elements
    out = jnp.full(index.shape, -1, jnp.int32)
    for j in range(4):
        inside = (index >= j * ghosts) & (index < (j + 1) * ghosts)
        out = jnp.where(inside, index - j * ghosts + starts[j], out)
    ghost_ref[...] = out


def ghost_part(
    pos_ref, v_ref, near_ref, even_ref, odd_ref, neigh_ref, wf_ref, index_ref, face_ref, ghost_ref, y_ref, m_ref, g_ref, base
):
    elements = v_ref.shape[-1]
    ghost_index(pos_ref, index_ref, ghost_ref, elements, near_ref.shape[-1] // 2)
    widen(neigh_ref, m_ref, base)
    source = jnp.concatenate([near_ref[...], even_ref[...], odd_ref[...]], axis=1)
    far_sides(source, ghost_ref, face_ref, wf_ref, g_ref, y_ref, 0)


def second_kernel(
    pos_ref, v_ref, dof_ref, near_ref, even_ref, odd_ref, star_ref, neigh_ref, wk_ref, wf_ref, index_ref, face_ref,
    cluster_ref, send_ref,
    state_ref, b_ref, near_out, far_out,
    x_ref, first_ref, y_ref, m_ref, mf_ref, g_ref, ghost_ref,
):
    elements = v_ref.shape[-1]
    ghost_part(
        pos_ref, v_ref, near_ref, even_ref, odd_ref, neigh_ref, wf_ref, index_ref, face_ref, ghost_ref, y_ref, mf_ref, g_ref, 0
    )
    widen(star_ref, m_ref, 0)

    def body(lanes):
        acc = star_sum(y_ref, mf_ref, 4, lanes, [v_ref[p, :, lanes] for p in range(NQ)])
        fine = cluster_ref[:, lanes] == 0
        pad = jnp.zeros((R - NB, LANES), F32)
        for p in range(NQ):
            state_ref[p, :, lanes] = acc[p]
            old = jnp.concatenate([dof_ref[p, :, lanes], pad], axis=0)
            x_ref[p, :, lanes] = jnp.where(fine, acc[p], old)

    each_half(elements, body)

    def weights_at(lanes):
        fine = cluster_ref[:, lanes] == 0
        return jnp.where(fine, 0.5, 1.5), jnp.where(fine, 1.0 / 6.0, 7.0 / 6.0)

    taylor_buffer(x_ref, first_ref, y_ref, m_ref, wk_ref[...], weights_at, b_ref)
    send_blocks(b_ref, send_ref, near_out, far_out)


def last_kernel(
    pos_ref, count_ref, v_ref, near_ref, even_ref, odd_ref, neigh_ref, wf_ref, index_ref, face_ref,
    damage_ref, yield_ref, cohesion_ref, wp_ref,
    out_ref,
    x_ref, y_ref, mf_ref, g_ref, ghost_ref, mask_ref,
):
    elements = v_ref.shape[-1]
    ghost_part(
        pos_ref, v_ref, near_ref, even_ref, odd_ref, neigh_ref, wf_ref, index_ref, face_ref, ghost_ref, y_ref, mf_ref, g_ref, 0
    )

    def body(lanes):
        acc = star_sum(y_ref, mf_ref, 4, lanes, [v_ref[p, :, lanes] for p in range(NQ)])
        for p in range(NQ):
            x_ref[p, :, lanes] = acc[p]

    each_half(elements, body)

    slots = damage_ref.shape[-1]
    rows = lax.broadcasted_iota(jnp.int32, (elements, slots), 0)
    slot = lax.broadcasted_iota(jnp.int32, (elements, slots), 1)
    hit = (rows == damage_ref[...]) & (slot < count_ref[0])
    listed = lax.dot_general(
        jnp.ones((8, slots), BF16),
        jnp.where(hit, 1.0, 0.0).astype(BF16),
        (((1,), (1,)), ((), ())),
        preferred_element_type=F32,
    )[0:1]
    mask_ref[NB:, :] = jnp.zeros((R - NB, elements), F32)
    mask_ref[:NB, :] = jnp.where((yield_ref[...] == 1) & (listed > 0.5), 1.0, 0.0)

    points = [dot(wp_ref[0], stack_values(x_ref[q])) for q in range(6)]
    pressure = (points[0] + points[1] + points[2]) / 3.0
    normal = [points[q] - pressure for q in range(3)]
    normal_sum = normal[0] * normal[0] + normal[1] * normal[1] + normal[2] * normal[2]
    shear_sum = points[3] * points[3] + points[4] * points[4] + points[5] * points[5]
    tau = jnp.sqrt(0.5 * normal_sum + shear_sum)
    strength = cohesion_ref[...]
    limit = jnp.maximum(strength - FRICTION * pressure, 0.5 * strength)
    rate = jnp.where(mask_ref[...] > 0.5, RELAXATION * (limit / jnp.maximum(tau, limit) - 1.0), 0.0)
    deviation = normal + points[3:]
    for q in range(6):
        change = dot(wp_ref[1], stack_values(rate * deviation[q]))
        out_ref[q] = (x_ref[q] + change)[:NB]
    for q in range(6, NQ):
        out_ref[q] = x_ref[q, :NB, :]


def spec(shape, dtype=F32):
    return jax.ShapeDtypeStruct(shape, dtype)


VMEM = pl.BlockSpec(memory_space=pltpu.VMEM)
SMEM = pl.BlockSpec(memory_space=pltpu.SMEM)


def call(kernel, inputs, outputs, scratch, smem=0, cost=0):
    return pl.pallas_call(
        kernel,
        out_shape=outputs,
        in_specs=[SMEM] * smem + [VMEM] * (len(inputs) - smem),
        out_specs=jax.tree.map(lambda _: VMEM, outputs),
        scratch_shapes=[pltpu.VMEM(shape, dtype) for shape, dtype in scratch],
        compiler_params=pltpu.CompilerParams(vmem_limit_bytes=40 * 1024 * 1024),
        cost_estimate=pl.CostEstimate(flops=cost, bytes_accessed=1 << 20, transcendentals=0),
    )(*inputs)


def core_swap(total):
    return [(i, i ^ 1) for i in range(total)]


def even_chip_swap(total):
    return [(i, i ^ 2) for i in range(total)]


def odd_chip_swap(total):
    route = [(i, i) for i in (0, 1, total - 2, total - 1)]
    for i in range(2, total - 2, 4):
        for k in (i, i + 1):
            route += [(k, k + 2), (k + 2, k)]
    return route


def exchange(near, far, me, total):
    got = lax.ppermute(near, "dom", core_swap(total))
    left = lax.broadcasted_iota(jnp.int32, got.shape, 1) < got.shape[1] // 2
    forward = left == ((me // 2) % 2 == 0)
    even = lax.ppermute(jnp.where(forward, got, far), "dom", even_chip_swap(total))
    odd = lax.ppermute(jnp.where(forward, far, got), "dom", odd_chip_swap(total))
    return got, even, odd


def per_device(
    dof_values,
    star_mats,
    flux_local,
    flux_neigh,
    kstiff,
    flux_minus,
    flux_plus,
    neighbour,
    neigh_face,
    cluster,
    send_list,
    damage_list,
    damage_count,
    yield_mask,
    cohesion,
    to_points,
    from_points,
):
    elements = dof_values.shape[-1]
    total = lax.axis_size("dom")
    me = lax.axis_index("dom")
    position = jnp.stack([me.astype(jnp.int32), jnp.int32(total)])
    wk = stack_weights(kstiff).reshape(3 * R, K3)
    wv = stack_weights(jnp.concatenate([jnp.swapaxes(kstiff, 1, 2), -flux_minus])).reshape(7 * R, K3)
    wf = stack_weights(-flux_plus).reshape(4, 4 * R, K3)
    wp = stack_weights(jnp.stack([to_points, from_points]))
    send = jnp.concatenate([send_list[0, 0], send_list[0, 1], send_list[0, 3], send_list[0, 2]])[None]
    cluster = cluster[None]
    cohesion = cohesion[None]

    field = spec((NQ, R, elements))
    block = spec((NQ * R, send.shape[-1] // 2))
    x_s = ((NQ, R, elements), F32)
    g_s = ((2 * NQ * R, elements), F32)
    ghost_s = ((4, elements), jnp.int32)

    def y_s(blocks):
        return ((blocks, NQ, R, elements), F32)

    def m_s(blocks):
        return ((blocks * NQ, NQ, elements), F32)

    def local_part(base, buffer):
        return call(
            local_kernel,
            [base, buffer, star_mats, flux_local, flux_neigh, wv, wf, neighbour, neigh_face],
            field,
            [y_s(11), m_s(11), g_s],
            cost=1_000_000_000,
        )

    buffer_one, near, far = call(
        predict_kernel,
        [dof_values, star_mats, wk, send],
        (field, block, block),
        [x_s, x_s, y_s(3), m_s(3)],
    )
    near, even, odd = exchange(near, far, me, total)
    started = local_part(dof_values, buffer_one)
    updated, buffer_two, near, far = call(
        second_kernel,
        [
            position, started, dof_values, near, even, odd, star_mats, flux_neigh, wk, wf, neighbour, neigh_face,
            cluster, send,
        ],
        (field, field, block, block),
        [x_s, x_s, y_s(4), m_s(3), m_s(4), g_s, ghost_s],
        smem=1,
    )
    near, even, odd = exchange(near, far, me, total)
    started = local_part(updated, buffer_two)
    return call(
        last_kernel,
        [
            position, damage_count, started, near, even, odd, flux_neigh, wf, neighbour, neigh_face,
            damage_list, yield_mask, cohesion, wp,
        ],
        spec(dof_values.shape),
        [x_s, y_s(4), m_s(4), g_s, ghost_s, ((R, elements), F32)],
        smem=2,
    )


def solution(mesh):
    return jax.shard_map(
        per_device,
        mesh=mesh,
        in_specs=(
            P(None, None, "dom"),
            P(None, None, None, "dom"),
            P(None, None, None, "dom"),
            P(None, None, None, "dom"),
            P(),
            P(),
            P(),
            P(None, "dom"),
            P(None, "dom"),
            P("dom"),
            P("dom", None, None),
            P("dom", None),
            P("dom"),
            P(None, "dom"),
            P("dom"),
            P(),
            P(),
        ),
        out_specs=P(None, None, "dom"),
        check_vma=False,
    )
```

time: 1790 us -> 43.8 us (0.02); the launches traced: 1760 us -> 43.4 us
  other arithmetic: 1050 us -> 0.76 us
  local copies, waits for them, and re-layouts: 633 us -> 5.05 us
  matrix products: 26.6 us -> 0 us
  starting transfers between devices: 30 us -> 8.89 us
  Pallas kernels: 0 us -> 21 us
    scatter-add x512 -> x0, other arithmetic: 1020 us -> none
    scatter-add x769 -> x0, local copies, waits for them, and re-layouts: 512 us -> none
    gather x31 -> x0, local copies, waits for them, and re-layouts: 62.9 us -> none  [the longest x12 46.2 us: face_values(): jnp.take(extended, neighbours[face_id], axis=2)]
    dot_general x36 -> x0, matrix products: 26.6 us -> none  [the longest x8 8.83 us: surface(): jnp.einsum('bc,pce->pbe', flux_minus[face_id], own_side, precision=PRECISE)]
    ppermute x8 -> x6, starting transfers between devices: 30 us -> 8.89 us  [the longest x2 7.13 us: exchange(): lax.ppermute(jnp.where(forward, far, got), 'dom', odd_chip_swap(total))]
    pallas_call x0 -> x5, Pallas kernels: none -> 21 us  [call(): pl.pallas_call(kernel, out_shape=outputs, in_specs=[SMEM] * smem + [VMEM]...]
    mul x53 -> x0, local copies, waits for them, and re-layouts: 19.6 us -> none  [the longest x32 12.4 us: star_apply(): total = total + source[quantity][None, :, :] * wide[quantity][:, None, :]]
  transfers between devices with their start and end apart: 8 -> 6, of which waited for: 0 -> 3; matrix products, arithmetic and copies ran while one was open for 2% -> 2% of each run, Pallas kernels for 0% -> 20%
where the time goes in v1:
time: 43.8 us; the launch traced here: 43.4 us
  Pallas kernels  21 us (48%)
  starting transfers between devices  8.89 us (20%)
  waiting for transfers between devices  6.74 us (15%)
  local copies, waits for them, and re-layouts  5.05 us (12%)
  between operations  0.97 us (2%)
  other arithmetic  0.76 us (2%)
    pallas_call x5, Pallas kernels, call(): pl.pallas_call(kernel, out_shape=outputs, in_specs=[SMEM] * smem + [VMEM]...  21 us
    ppermute x2, starting transfers between devices, exchange(): lax.ppermute(jnp.where(forward, far, got), 'dom', odd_chip_swap(total))  7.13 us
    ppermute x2, waiting for transfers between devices, exchange(): lax.ppermute(jnp.where(forward, far, got), 'dom', odd_chip_swap(total))  4.89 us
    unnamed x32, local copies, waits for them, and re-layouts  4.18 us
    ppermute x2, starting transfers between devices, exchange(): lax.ppermute(jnp.where(forward, got, far), 'dom', even_chip_swap(total))  1.63 us
    ppermute x2, waiting for transfers between devices, exchange(): got = lax.ppermute(near, 'dom', core_swap(total))  1.27 us
  transfers between devices with their start and end apart: 6, of which 3 were waited for; matrix products, arithmetic and copies ran while one was open for 2% of the time, Pallas kernels for 20%

profile of v1, /device:TPU:24, one launch (start us, length us, event | category | flops | bytes accessed | tf_op | source)
XLA Modules:
  0.0 43.4 jit_solution(6198623023192300187)
XLA Ops:
  0.0 0.8 %slice_bitcast_fusion.3 = (s32[64]{0:T(128)S(1)}, s32[64]{0:T(128)S(1)}, s32[64]{0:T(128)S(1)}, s32[64]{0:T(128)S(1)}) fusion(s32[1,4,64]{2,1,0:T(4,128)} %param.27), kind=kLoop, calls=%fused_computation.33 | loop fusion | bytes 2048 | tf_op jit(solution)/shard_map/squeeze | solution.py:345
  0.8 1.0 %copy.33.star_ref = bf16[3,9,9,256]{3,2,1,0:T(8,128)(2,1)S(1)} copy(bf16[3,9,9,256]{3,0,2,1:T(4,128)(2,1)} %param.18) | data formatting | bytes 248832 | tf_op args[1]
  1.9 0.1 pad_maximum_fusion.2.wk_ref
  2.0 0.1 pad_add_fusion
  2.0 1.7 %shard_map.163 = (f32[9,24,256]{2,1,0:T(8,128)S(1)}, f32[216,128]{1,0:T(8,128)S(1)}, f32[216,128]{1,0:T(8,128)S(1)}) custom-call(f32[9,20,256]{2,1,0:T(8,128)S(1)} %copy-done, bf16[3,9,9,256]{3,2,1,0:T(8,128)(2,1)S(1)} %copy.33.star_ref, bf16[72,72]{1,0:T(8,128)(2,1)S(1)} %pad_maximum_fusion.2.wk_ref, s32[1,256]{1,0:T(1,128)S(1)} %bitcast.21), custom_call_target="tpu_custom_call" | custom-call | bytes 1048576 | tf_op jit(solution)/shard_map/pallas_call | solution.py:282
  3.9 0.1 copy.34
  4.2 0.7 %copy-done.11 = f32[4,20,20]{2,0,1:T(4,128)S(1)} copy-done((f32[4,20,20]{2,0,1:T(4,128)S(1)}, f32[4,20,20]{2,0,1:T(4,128)}, u32[]{:S(2)}) %copy-start.11) | copy-done | bytes 6424
  4.9 0.2 copy-done.7
  5.1 0.9 %copy-done.8 = bf16[4,9,9,256]{3,0,2,1:T(4,128)(2,1)S(1)} copy-done((bf16[4,9,9,256]{3,0,2,1:T(4,128)(2,1)S(1)}, bf16[4,9,9,256]{3,0,2,1:T(4,128)(2,1)}, u32[]{:S(2)}) %copy-start.8) | copy-done | bytes 165912
  6.0 0.1 pad_maximum_fusion.wf_ref
  6.2 0.1 pad_maximum_fusion.1.wv_ref
  6.3 0.6 %copy-done.2 = s32[4,256]{1,0:T(4,128)S(1)} copy-done((s32[4,256]{1,0:T(4,128)S(1)}, s32[4,256]{1,0:T(4,128)}, u32[]{:S(2)}) %copy-start.2) | copy-done | bytes 4120
  6.9 4.3 %shard_map.164.v_ref = f32[9,24,256]{2,1,0:T(8,128)S(1)} custom-call(f32[9,20,256]{2,1,0:T(8,128)S(1)} %copy-done, f32[9,24,256]{2,1,0:T(8,128)S(1)} %get-tuple-element.12.b_ref, bf16[3,9,9,256]{3,2,1,0:T(8,128)(2,1)S(1)} %copy.33.star_ref, bf16[4,9,9,256]{3,2,1,0:T(8,128)(2,1)S(1)} %copy.39.local_ref, bf16[4,9,9,256]{3,2,1,0:T(8,128)(2,1)S(1)} %copy.40.neigh_ref, ...), custom_call_target="tpu_custom_call" | custom-call | flops 1000000000 | bytes 1048576 | tf_op jit(solution)/shard_map/pallas_call | solution.py:282
  11.2 1.6 %collective-permute-start.1 = (f32[216,128]{1,0:T(8,128)S(1)}, f32[216,128]{1,0:T(8,128)S(1)}, u32[]{:S(2)}, u32[]{:S(2)}) collective-permute-start(f32[216,128]{1,0:T(8,128)S(1)} %get-tuple-element.22), channel_id=1, source_target_pairs={{0,2},{1,3},{2,0},{3,1},{4,6},{5,7},{6,4},{7,5},{8,10},{9,11},{10,... | collective-permute-start | bytes 331784 | tf_op jit(solution)/shard_map/ppermute | solution.py:313
  12.8 3.3 %collective-permute-start.2 = (f32[216,128]{1,0:T(8,128)S(1)}, f32[216,128]{1,0:T(8,128)S(1)}, u32[]{:S(2)}, u32[]{:S(2)}) collective-permute-start(f32[216,128]{1,0:T(8,128)S(1)} %get-tuple-element.21), channel_id=1, source_target_pairs={{0,0},{1,1},{30,30},{31,31},{2,4},{4,2},{3,5},{5,3},{6,8},{8,6},{7... | collective-permute-start | bytes 331784 | tf_op jit(solution)/shard_map/ppermute | solution.py:314
  16.1 0.6 %collective-permute-done.1.even_ref = f32[216,128]{1,0:T(8,128)S(1)} collective-permute-done((f32[216,128]{1,0:T(8,128)S(1)}, f32[216,128]{1,0:T(8,128)S(1)}, u32[]{:S(2)}, u32[]{:S(2)}) %collective-permute-start.1) | collective-permute-done | bytes 110624 | tf_op jit(solution)/shard_map/ppermute | solution.py:313
  16.7 4.9 %collective-permute-done.2.odd_ref = f32[216,128]{1,0:T(8,128)S(1)} collective-permute-done((f32[216,128]{1,0:T(8,128)S(1)}, f32[216,128]{1,0:T(8,128)S(1)}, u32[]{:S(2)}, u32[]{:S(2)}) %collective-permute-start.2) | collective-permute-done | bytes 110624 | tf_op jit(solution)/shard_map/ppermute | solution.py:314
  21.6 5.7 %shard_map.165 = (f32[9,24,256]{2,1,0:T(8,128)S(1)}, f32[9,24,256]{2,1,0:T(8,128)S(1)}, f32[216,128]{1,0:T(8,128)S(1)}, f32[216,128]{1,0:T(8,128)S(1)}) custom-call(s32[2]{0:T(128)S(1)} %pad_add_fusion.1.pos_ref, f32[9,24,256]{2,1,0:T(8,128)S(1)} %shard_map.164.v_ref, f32[9,20,256]{2,1,0:T(8,128)S(1)} %copy-done, ...), custom_call_target="tpu_custom_call" | custom-call | bytes 1048576 | tf_op jit(solution)/shard_map/pallas_call | solution.py:282
  27.4 1.3 %collective-permute-done.3.near_ref = f32[216,128]{1,0:T(8,128)S(1)} collective-permute-done((f32[216,128]{1,0:T(8,128)S(1)}, f32[216,128]{1,0:T(8,128)S(1)}, u32[]{:S(2)}, u32[]{:S(2)}) %collective-permute-start.3) | collective-permute-done | bytes 110624 | tf_op jit(solution)/shard_map/ppermute | solution.py:310
  28.8 3.9 %collective-permute-start.5 = (f32[216,128]{1,0:T(8,128)S(1)}, f32[216,128]{1,0:T(8,128)S(1)}, u32[]{:S(2)}, u32[]{:S(2)}) collective-permute-start(f32[216,128]{1,0:T(8,128)S(1)} %get-tuple-element.19), channel_id=1, source_target_pairs={{0,0},{1,1},{30,30},{31,31},{2,4},{4,2},{3,5},{5,3},{6,8},{8,6},{7... | collective-permute-start | bytes 331784 | tf_op jit(solution)/shard_map/ppermute | solution.py:314
  32.7 0.1 pad_maximum_fusion.3.wp_ref
  33.4 4.3 %shard_map.166.v_ref = f32[9,24,256]{2,1,0:T(8,128)S(1)} custom-call(f32[9,24,256]{2,1,0:T(8,128)S(1)} %get-tuple-element.15.base_ref, f32[9,24,256]{2,1,0:T(8,128)S(1)} %get-tuple-element.16.b_ref, bf16[3,9,9,256]{3,2,1,0:T(8,128)(2,1)S(1)} %copy.33.star_ref, bf16[4,9,9,256]{3,2,1,0:T(8,128)(2,1)S(1)} %copy.39.local_ref, ...), custom_call_target="tpu_custom_call" | custom-call | flops 1000000000 | bytes 1048576 | tf_op jit(solution)/shard_map/pallas_call | solution.py:282
  37.8 0.6 %copy-done.5 = s32[1,256]{1,0:T(1,128)S(1)} copy-done((s32[1,256]{1,0:T(1,128)S(1)}, s32[1,256]{1,0:T(1,128)}, u32[]{:S(2)}) %copy-start.5) | copy-done | bytes 1048
  38.4 5.1 %shard_map.167 = f32[9,20,256]{2,1,0:T(8,128)} custom-call(s32[2]{0:T(128)S(1)} %pad_add_fusion.1.pos_ref, s32[1]{0:T(128)S(6)} %copy.48.count_ref, f32[9,24,256]{2,1,0:T(8,128)S(1)} %shard_map.166.v_ref, f32[216,128]{1,0:T(8,128)S(1)} %collective-permute-done.3.near_ref, f32[216,128]{1,0:T(8,128)S(1)} %collective-permute-done.4.even_ref, ...), custom_call_target="tpu_custom_call" | custom-call | bytes 1048576 | tf_op jit(solution)/shard_map/pallas_call | solution.py:282
  (43 shorter events, 0.7 us)
Async XLA Ops:
  0.8 1.0 %copy-start.10 = (f32[3,20,20]{2,1,0:T(8,128)S(1)}, f32[3,20,20]{2,1,0:T(8,128)}, u32[]{:S(2)}) copy-start(f32[3,20,20]{2,1,0:T(8,128)} %param.21) | copy-start | bytes 14404
  0.8 1.2 %copy-start = (f32[9,20,256]{2,1,0:T(8,128)S(1)}, f32[9,20,256]{2,1,0:T(8,128)}, u32[]{:S(2)}) copy-start(f32[9,20,256]{2,1,0:T(8,128)} %dof_ref.3) | copy-start | bytes 552964
  2.0 1.9 %copy-start.9 = (f32[4,4,20,20]{3,1,2,0:T(4,128)S(1)}, f32[4,4,20,20]{3,1,2,0:T(4,128)}, u32[]{:S(2)}) copy-start(f32[4,4,20,20]{3,1,2,0:T(4,128)} %param.23) | copy-start | bytes 76804
  3.8 7.4 %collective-permute-start = (f32[216,128]{1,0:T(8,128)S(1)}, f32[216,128]{1,0:T(8,128)S(1)}, u32[]{:S(2)}, u32[]{:S(2)}) collective-permute-start(f32[216,128]{1,0:T(8,128)S(1)} %get-tuple-element.13), channel_id=1, source_target_pairs={{0,1},{1,0},{2,3},{3,2},{4,5},{5,4},{6,7},{7,6},{8,9},{9,8},{10,11... | collective-permute-start | bytes 331784 | tf_op jit(solution)/shard_map/ppermute | solution.py:310
  4.1 0.8 %copy-start.11 = (f32[4,20,20]{2,0,1:T(4,128)S(1)}, f32[4,20,20]{2,0,1:T(4,128)}, u32[]{:S(2)}) copy-start(f32[4,20,20]{2,0,1:T(4,128)} %param.22) | copy-start | bytes 19204
  4.1 0.9 %copy-start.7 = (bf16[4,9,9,256]{3,0,2,1:T(4,128)(2,1)S(1)}, bf16[4,9,9,256]{3,0,2,1:T(4,128)(2,1)}, u32[]{:S(2)}) copy-start(bf16[4,9,9,256]{3,0,2,1:T(4,128)(2,1)} %param.20) | copy-start | bytes 497668
  5.1 0.9 %copy-start.8 = (bf16[4,9,9,256]{3,0,2,1:T(4,128)(2,1)S(1)}, bf16[4,9,9,256]{3,0,2,1:T(4,128)(2,1)}, u32[]{:S(2)}) copy-start(bf16[4,9,9,256]{3,0,2,1:T(4,128)(2,1)} %param.19) | copy-start | bytes 497668
  6.2 0.7 %copy-start.2 = (s32[4,256]{1,0:T(4,128)S(1)}, s32[4,256]{1,0:T(4,128)}, u32[]{:S(2)}) copy-start(s32[4,256]{1,0:T(4,128)} %index_ref.7) | copy-start | bytes 12292
  6.2 0.7 %copy-start.3 = (s32[4,256]{1,0:T(4,128)S(1)}, s32[4,256]{1,0:T(4,128)}, u32[]{:S(2)}) copy-start(s32[4,256]{1,0:T(4,128)} %face_ref.7) | copy-start | bytes 12292
  11.2 5.5 %collective-permute-start.1 = (f32[216,128]{1,0:T(8,128)S(1)}, f32[216,128]{1,0:T(8,128)S(1)}, u32[]{:S(2)}, u32[]{:S(2)}) collective-permute-start(f32[216,128]{1,0:T(8,128)S(1)} %get-tuple-element.22), channel_id=1, source_target_pairs={{0,2},{1,3},{2,0},{3,1},{4,6},{5,7},{6,4},{7,5},{8,10},{9,11},{10,... | collective-permute-start | bytes 331784 | tf_op jit(solution)/shard_map/ppermute | solution.py:313
  12.8 8.8 %collective-permute-start.2 = (f32[216,128]{1,0:T(8,128)S(1)}, f32[216,128]{1,0:T(8,128)S(1)}, u32[]{:S(2)}, u32[]{:S(2)}) collective-permute-start(f32[216,128]{1,0:T(8,128)S(1)} %get-tuple-element.21), channel_id=1, source_target_pairs={{0,0},{1,1},{30,30},{31,31},{2,4},{4,2},{3,5},{5,3},{6,8},{8,6},{7... | collective-permute-start | bytes 331784 | tf_op jit(solution)/shard_map/ppermute | solution.py:314
  16.1 5.5 %copy-start.4 = (s32[256]{0:T(256)S(1)}, s32[256]{0:T(256)}, u32[]{:S(2)}) copy-start(s32[256]{0:T(256)} %param.26) | copy-start | bytes 3076
  21.6 5.8 %copy-start.12 = (f32[20,20]{1,0:T(8,128)S(1)}, f32[20,20]{1,0:T(8,128)}, u32[]{:S(2)}) copy-start(f32[20,20]{1,0:T(8,128)} %param.33) | copy-start | bytes 4804
  21.6 5.8 %copy-start.13 = (f32[20,20]{1,0:T(8,128)S(1)}, f32[20,20]{1,0:T(8,128)}, u32[]{:S(2)}) copy-start(f32[20,20]{1,0:T(8,128)} %param.32) | copy-start | bytes 4804
  27.3 1.4 %collective-permute-start.3 = (f32[216,128]{1,0:T(8,128)S(1)}, f32[216,128]{1,0:T(8,128)S(1)}, u32[]{:S(2)}, u32[]{:S(2)}) collective-permute-start(f32[216,128]{1,0:T(8,128)S(1)} %get-tuple-element.17), channel_id=1, source_target_pairs={{0,1},{1,0},{2,3},{3,2},{4,5},{5,4},{6,7},{7,6},{8,9},{9,8},{10,11... | collective-permute-start | bytes 331784 | tf_op jit(solution)/shard_map/ppermute | solution.py:310
  28.7 9.0 %collective-permute-start.4 = (f32[216,128]{1,0:T(8,128)S(1)}, f32[216,128]{1,0:T(8,128)S(1)}, u32[]{:S(2)}, u32[]{:S(2)}) collective-permute-start(f32[216,128]{1,0:T(8,128)S(1)} %get-tuple-element.20), channel_id=1, source_target_pairs={{0,2},{1,3},{2,0},{3,1},{4,6},{5,7},{6,4},{7,5},{8,10},{9,11},{10,... | collective-permute-start | bytes 331784 | tf_op jit(solution)/shard_map/ppermute | solution.py:313
  28.8 8.9 %collective-permute-start.5 = (f32[216,128]{1,0:T(8,128)S(1)}, f32[216,128]{1,0:T(8,128)S(1)}, u32[]{:S(2)}, u32[]{:S(2)}) collective-permute-start(f32[216,128]{1,0:T(8,128)S(1)} %get-tuple-element.19), channel_id=1, source_target_pairs={{0,0},{1,1},{30,30},{31,31},{2,4},{4,2},{3,5},{5,3},{6,8},{8,6},{7... | collective-permute-start | bytes 331784 | tf_op jit(solution)/shard_map/ppermute | solution.py:314
  33.4 4.3 %copy-start.1 = (s32[20,256]{1,0:T(8,128)S(1)}, s32[20,256]{1,0:T(8,128)}, u32[]{:S(2)}) copy-start(s32[20,256]{1,0:T(8,128)} %yield_ref.1) | copy-start | bytes 61444
  33.4 4.3 %copy-start.6 = (f32[256]{0:T(256)S(1)}, f32[256]{0:T(256)}, u32[]{:S(2)}) copy-start(f32[256]{0:T(256)} %param.31) | copy-start | bytes 3076
  37.7 0.7 %copy-start.5 = (s32[1,256]{1,0:T(1,128)S(1)}, s32[1,256]{1,0:T(1,128)}, u32[]{:S(2)}) copy-start(s32[1,256]{1,0:T(1,128)} %damage_ref.1) | copy-start | bytes 3076

commit v2 on v1

v2 whole, which is shorter than its diff:
```python
import functools

import jax
import jax.numpy as jnp
from jax import lax
from jax.experimental import pallas as pl
from jax.experimental.pallas import tpu as pltpu
from jax.sharding import PartitionSpec as P

NQ = 9
NB = 20
R = 24
K3 = 3 * R
LANES = 128
FRICTION = 0.6
RELAXATION = 0.5
F32 = jnp.float32
BF16 = jnp.bfloat16


def stack_weights(w):
    w = jnp.pad(w, [(0, 0)] * (w.ndim - 2) + [(0, R - NB), (0, R - NB)])
    high = lax.reduce_precision(w, 8, 7)
    low = w - high
    return jnp.concatenate([high, high, low], axis=-1).astype(BF16)


def stack_values(x):
    high = x.astype(BF16).astype(F32)
    return jnp.concatenate([high, x - high, high], axis=0).astype(BF16)


def dot(a, b):
    return jnp.dot(a, b, preferred_element_type=F32)


def widen(src_ref, dst_ref):
    for q in range(NQ):
        for p in range(NQ):
            dst_ref[q * NQ + p] = src_ref[q, p].astype(F32)


def basis_products(weights, x_ref, y_ref, blocks, base=0):
    for q in range(NQ):
        out = dot(weights, stack_values(x_ref[q]))
        for k in range(blocks):
            y_ref[base + k, q] = out[k * R : (k + 1) * R]


def star_sum(y_ref, m_refs, lanes, start):
    acc = list(start)
    for q in range(NQ):
        k = 0
        for m_ref in m_refs:
            for row in range(m_ref.shape[1]):
                y = y_ref[k, q, :, lanes]
                for p in range(NQ):
                    acc[p] = acc[p] + y * m_ref[q * NQ + p, row : row + 1, lanes]
                k += 1
    return acc


def each_half(elements, body):
    for start in range(0, elements, LANES):
        body(pl.ds(start, LANES))


def taylor_buffer(x_ref, first_ref, y_ref, m_ref, wk, weights_at, out_ref):
    elements = x_ref.shape[-1]
    basis_products(wk, x_ref, y_ref, 3)

    def first(lanes):
        acc = star_sum(y_ref, [m_ref], lanes, [jnp.zeros((R, LANES), F32)] * NQ)
        for p in range(NQ):
            first_ref[p, :, lanes] = acc[p]

    each_half(elements, first)
    basis_products(wk, first_ref, y_ref, 3)

    def second(lanes):
        acc = star_sum(y_ref, [m_ref], lanes, [jnp.zeros((R, LANES), F32)] * NQ)
        w1, w2 = weights_at(lanes)
        for p in range(NQ):
            out_ref[p, :, lanes] = x_ref[p, :, lanes] + (w1 * first_ref[p, :, lanes] + w2 * acc[p])

    each_half(elements, second)


def send_blocks(b_ref, send, near_ref, far_ref):
    elements = b_ref.shape[-1]
    columns = send.shape[-1]
    b = b_ref[...].reshape(NQ * R, elements)
    high = b.astype(BF16)
    low = (b - high.astype(F32)).astype(BF16)
    rows = lax.broadcasted_iota(jnp.int32, (elements, columns), 0).astype(F32)
    hot = jnp.where(rows == send, 1.0, 0.0).astype(BF16)
    out = dot(high, hot) + dot(low, hot)
    near_ref[...] = out[:, : columns // 2]
    far_ref[...] = out[:, columns // 2 :]


def far_sides(source, index, face, wf_ref, y_ref, base):
    high = source.astype(BF16)
    low = (source - high.astype(F32)).astype(BF16)
    both = jnp.concatenate([high, low], axis=0)
    elements = index.shape[-1]
    rows = lax.broadcasted_iota(jnp.int32, (source.shape[-1], elements), 0).astype(F32)
    size = NQ * R
    gathered = []
    for f in range(4):
        hot = jnp.where(rows == index[f : f + 1], 1.0, 0.0).astype(BF16)
        gathered.append(dot(both, hot))
    for f, picked in enumerate(gathered):
        kind = jnp.broadcast_to(face[f : f + 1], (R, elements))
        w = wf_ref[f]
        for q in range(NQ):
            high_rows = picked[q * R : (q + 1) * R]
            low_rows = picked[size + q * R : size + (q + 1) * R]
            out = dot(w, jnp.concatenate([high_rows, low_rows, high_rows], axis=0).astype(BF16))
            y_ref[base + f, q] = jnp.where(
                kind < 2,
                jnp.where(kind == 0, out[:R], out[R : 2 * R]),
                jnp.where(kind == 2, out[2 * R : 3 * R], out[3 * R :]),
            )


def place_weights(w_ref):
    w = w_ref[...]
    high = w.astype(BF16)
    low = (w - high.astype(F32)).astype(BF16)
    row = lax.broadcasted_iota(jnp.int32, (LANES, K3), 0)
    column = lax.broadcasted_iota(jnp.int32, (LANES, K3), 1)
    twice = jnp.where((column == row) | (column == row + R), 1.0, 0.0).astype(BF16)
    once = jnp.where(column == row + 2 * R, 1.0, 0.0).astype(BF16)
    return (dot(high, twice) + dot(low, once)).astype(BF16)


def send_columns(send_ref):
    slots, ghosts = send_ref.shape
    width = slots * ghosts
    row = lax.broadcasted_iota(jnp.int32, (ghosts, width), 0)
    column = lax.broadcasted_iota(jnp.int32, (ghosts, width), 1)
    repeat = jnp.where(column % ghosts == row, 1.0, 0.0).astype(BF16)
    wide = dot(send_ref[...].astype(F32).astype(BF16), repeat)
    slot = lax.broadcasted_iota(jnp.int32, (1, width), 1) // ghosts
    first = jnp.where(slot == 0, wide[0:1], wide[1:2])
    second = jnp.where(slot == 2, wide[3:4], wide[2:3])
    return jnp.where(slot < 2, first, second)


NEIGHBOUR, FACE, CLUSTER, DAMAGE, COUNT, COHESION, SEND, YIELD = 0, 4, 8, 9, 10, 11, 12, 16
ROWS = 40


def predict_kernel(
    dof_ref, star_ref, kstiff_ref, send_ref, index_ref, face_ref, cluster_ref, damage_ref, count_ref, cohesion_ref, yield_ref,
    b_out, near_out, far_out, table_out, wk_out,
    dof_v, star_v, kstiff_v, send_v, index_v, face_v, cluster_v, damage_v, count_v, cohesion_v, yield_v,
    w_ref, x_ref, first_ref, y_ref, m_ref, b_ref, near_ref, far_ref, table_ref, wk_ref, in_sems, out_sems,
):
    sources = [
        kstiff_ref, send_ref.at[0], dof_ref, star_ref, index_ref, face_ref, cluster_ref, damage_ref, count_ref, cohesion_ref, yield_ref
    ]
    targets = [kstiff_v, send_v, dof_v, star_v, index_v, face_v, cluster_v, damage_v, count_v, cohesion_v, yield_v]
    moves = [pltpu.make_async_copy(*pair, in_sems.at[i]) for i, pair in enumerate(zip(sources, targets))]
    for move in moves:
        move.start()
    results = [(b_ref, b_out), (near_ref, near_out), (far_ref, far_out), (table_ref, table_out), (wk_ref, wk_out)]
    writes = [pltpu.make_async_copy(*pair, out_sems.at[i]) for i, pair in enumerate(results)]
    elements = x_ref.shape[-1]
    w_ref[...] = jnp.zeros(w_ref.shape, F32)
    x_ref[:, NB:, :] = jnp.zeros((NQ, R - NB, elements), F32)
    table_ref[...] = jnp.zeros(table_ref.shape, F32)
    for move in moves:
        move.wait()
    for d in range(3):
        w_ref[d * R : d * R + NB, :NB] = kstiff_v[d]
    wk = place_weights(w_ref)
    wk_ref[...] = wk
    x_ref[:, :NB, :] = dof_v[...]
    widen(star_v, m_ref)
    taylor_buffer(x_ref, first_ref, y_ref, m_ref, wk, lambda lanes: (0.5, 1.0 / 6.0), b_ref)
    writes[0].start()
    writes[4].start()
    send = send_columns(send_v)
    send_blocks(b_ref, send, near_ref, far_ref)
    writes[1].start()
    writes[2].start()
    table_ref[NEIGHBOUR : NEIGHBOUR + 4, :] = index_v[...].astype(F32)
    table_ref[FACE : FACE + 4, :] = face_v[...].astype(F32)
    table_ref[CLUSTER : CLUSTER + 1, :] = cluster_v[...].astype(F32)
    table_ref[DAMAGE : DAMAGE + 1, :] = damage_v[...].astype(F32)
    table_ref[COUNT : COUNT + 1, :] = jnp.full((1, elements), count_v[0], jnp.int32).astype(F32)
    table_ref[COHESION : COHESION + 1, :] = cohesion_v[...]
    table_ref[SEND : SEND + 1, :] = send
    table_ref[YIELD : YIELD + NB, :] = yield_v[...].astype(F32)
    writes[3].start()
    for write in writes:
        write.wait()


def local_part(b_ref, wv_ref, wf_ref, table_ref, ms_ref, ml_ref, mn_ref, out_ref, y_ref, start):
    elements = b_ref.shape[-1]
    basis_products(wv_ref[...], b_ref, y_ref, 7)
    source = b_ref[...].reshape(NQ * R, elements)
    far_sides(source, table_ref[NEIGHBOUR : NEIGHBOUR + 4], table_ref[FACE : FACE + 4], wf_ref, y_ref, 7)

    def body(lanes):
        acc = star_sum(y_ref, [ms_ref, ml_ref, mn_ref], lanes, [start(p, lanes) for p in range(NQ)])
        for p in range(NQ):
            out_ref[p, :, lanes] = acc[p]

    each_half(elements, body)


def padded(ref, p, lanes):
    return jnp.concatenate([ref[p, :, lanes], jnp.zeros((R - NB, LANES), F32)], axis=0)


def local_kernel(
    dof_ref, b_ref, star_ref, local_ref, neigh_ref, wv_ref, wf_ref, table_ref, out_ref, ms_ref, ml_ref, mn_ref, mask_ref, y_ref
):
    widen(star_ref, ms_ref)
    widen(local_ref, ml_ref)
    widen(neigh_ref, mn_ref)
    local_part(
        b_ref, wv_ref, wf_ref, table_ref, ms_ref, ml_ref, mn_ref, out_ref, y_ref, lambda p, lanes: padded(dof_ref, p, lanes)
    )
    elements = out_ref.shape[-1]
    rows = lax.broadcasted_iota(jnp.int32, (elements, elements), 0).astype(F32)
    slot = lax.broadcasted_iota(jnp.int32, (1, elements), 1).astype(F32)
    live = jnp.where(slot < table_ref[COUNT : COUNT + 1], table_ref[DAMAGE : DAMAGE + 1], -1.0)
    listed = lax.dot_general(
        jnp.ones((8, elements), BF16),
        jnp.where(rows == live, 1.0, 0.0).astype(BF16),
        (((1,), (1,)), ((), ())),
        preferred_element_type=F32,
    )[0:1]
    mask_ref[...] = jnp.where(listed > 0.5, table_ref[YIELD : YIELD + R], 0.0)


def again_kernel(base_ref, b_ref, wv_ref, wf_ref, table_ref, ms_ref, ml_ref, mn_ref, out_ref, y_ref):
    local_part(b_ref, wv_ref, wf_ref, table_ref, ms_ref, ml_ref, mn_ref, out_ref, y_ref, lambda p, lanes: base_ref[p, :, lanes])


def ghost_source(pos_ref, near_ref, even_ref, odd_ref):
    me, total = pos_ref[0], pos_ref[1]
    core = me % 2
    chip = (me // 2) % 2 == 0
    near, even, odd = near_ref[...], even_ref[...], odd_ref[...]
    up = jnp.where(chip, even, odd)
    down = jnp.where(chip, odd, even)
    half = near.shape[1] // 2
    side = lax.broadcasted_iota(jnp.int32, near.shape, 1) // half
    across = jnp.where(core == 0, down, up)
    one = jnp.where(side == core, across, near)
    two = jnp.where(side == 0, up, down)
    one = jnp.where(jnp.where(side == 0, me - 1, total - 2 - me) >= 0, one, 0.0)
    two = jnp.where(jnp.where(side == 0, total - 3 - me, me - 2) >= 0, two, 0.0)
    return jnp.concatenate([one, two], axis=1)


def ghost_part(pos_ref, near_ref, even_ref, odd_ref, wf_ref, table_ref, y_ref):
    elements = table_ref.shape[-1]
    ghosts = near_ref.shape[-1] // 2
    index = table_ref[NEIGHBOUR : NEIGHBOUR + 4] - elements
    last = jnp.where(index >= 3 * ghosts, index - ghosts, index + ghosts)
    index = jnp.where(index >= 2 * ghosts, last, index)
    source = ghost_source(pos_ref, near_ref, even_ref, odd_ref)
    far_sides(source, index, table_ref[FACE : FACE + 4], wf_ref, y_ref, 0)


def second_kernel(
    pos_ref, v_ref, dof_ref, near_ref, even_ref, odd_ref, wk_ref, wf_ref, table_ref, ms_ref, mn_ref,
    state_ref, b_ref, near_out, far_out,
    x_ref, first_ref, y_ref,
):
    elements = v_ref.shape[-1]
    ghost_part(pos_ref, near_ref, even_ref, odd_ref, wf_ref, table_ref, y_ref)

    def body(lanes):
        acc = star_sum(y_ref, [mn_ref], lanes, [v_ref[p, :, lanes] for p in range(NQ)])
        fine = table_ref[CLUSTER : CLUSTER + 1, lanes] < 0.5
        for p in range(NQ):
            state_ref[p, :, lanes] = acc[p]
            x_ref[p, :, lanes] = jnp.where(fine, acc[p], padded(dof_ref, p, lanes))

    each_half(elements, body)

    def weights_at(lanes):
        fine = table_ref[CLUSTER : CLUSTER + 1, lanes] < 0.5
        return jnp.where(fine, 0.5, 1.5), jnp.where(fine, 1.0 / 6.0, 7.0 / 6.0)

    taylor_buffer(x_ref, first_ref, y_ref, ms_ref, wk_ref[...], weights_at, b_ref)
    send_blocks(b_ref, table_ref[SEND : SEND + 1], near_out, far_out)


def last_kernel(
    pos_ref, v_ref, near_ref, even_ref, odd_ref, wf_ref, table_ref, mn_ref, mask_ref, wp_ref,
    out_ref,
    x_ref, y_ref,
):
    elements = v_ref.shape[-1]
    ghost_part(pos_ref, near_ref, even_ref, odd_ref, wf_ref, table_ref, y_ref)

    def body(lanes):
        acc = star_sum(y_ref, [mn_ref], lanes, [v_ref[p, :, lanes] for p in range(NQ)])
        for p in range(NQ):
            x_ref[p, :, lanes] = acc[p]

    each_half(elements, body)

    points = [dot(wp_ref[0], stack_values(x_ref[q])) for q in range(6)]
    pressure = (points[0] + points[1] + points[2]) / 3.0
    normal = [points[q] - pressure for q in range(3)]
    normal_sum = normal[0] * normal[0] + normal[1] * normal[1] + normal[2] * normal[2]
    shear_sum = points[3] * points[3] + points[4] * points[4] + points[5] * points[5]
    tau = jnp.sqrt(0.5 * normal_sum + shear_sum)
    strength = table_ref[COHESION : COHESION + 1]
    limit = jnp.maximum(strength - FRICTION * pressure, 0.5 * strength)
    rate = jnp.where(mask_ref[...] > 0.5, RELAXATION * (limit / jnp.maximum(tau, limit) - 1.0), 0.0)
    deviation = normal + points[3:]
    for q in range(6):
        change = dot(wp_ref[1], stack_values(rate * deviation[q]))
        out_ref[q] = (x_ref[q] + change)[:NB]
    for q in range(6, NQ):
        out_ref[q] = x_ref[q, :NB, :]


def spec(shape, dtype=F32):
    return jax.ShapeDtypeStruct(shape, dtype)


VMEM = pl.BlockSpec(memory_space=pltpu.VMEM)
SMEM = pl.BlockSpec(memory_space=pltpu.SMEM)
HBM = pl.BlockSpec(memory_space=pltpu.HBM)


def call(kernel, inputs, outputs, scratch, smem=0, cost=0, space=VMEM, grant=40):
    out_space = space if space is HBM else VMEM
    return pl.pallas_call(
        kernel,
        out_shape=outputs,
        in_specs=[SMEM] * smem + [space] * (len(inputs) - smem),
        out_specs=jax.tree.map(lambda _: out_space, outputs),
        scratch_shapes=[pltpu.VMEM(*one) if isinstance(one, tuple) else one for one in scratch],
        compiler_params=pltpu.CompilerParams(vmem_limit_bytes=grant * 1024 * 1024),
        cost_estimate=pl.CostEstimate(flops=cost, bytes_accessed=1 << 20, transcendentals=0),
    )(*inputs)


def core_swap(total):
    return [(i, i ^ 1) for i in range(total)]


def even_chip_swap(total):
    return [(i, i ^ 2) for i in range(total)]


def odd_chip_swap(total):
    route = [(i, i) for i in (0, 1, total - 2, total - 1)]
    for i in range(2, total - 2, 4):
        for k in (i, i + 1):
            route += [(k, k + 2), (k + 2, k)]
    return route


def exchange(near, far, me, total, beside):
    got = lax.ppermute(near, "dom", core_swap(total))
    left = lax.broadcasted_iota(jnp.int32, got.shape, 1) < got.shape[1] // 2
    forward = left == ((me // 2) % 2 == 0)
    to_even, to_odd = jnp.where(forward, got, far), jnp.where(forward, far, got)
    beside, to_even, to_odd = lax.optimization_barrier((beside, to_even, to_odd))
    even = lax.ppermute(to_even, "dom", even_chip_swap(total))
    odd = lax.ppermute(to_odd, "dom", odd_chip_swap(total))
    return got, even, odd, beside


def per_device(
    dof_values,
    star_mats,
    flux_local,
    flux_neigh,
    kstiff,
    flux_minus,
    flux_plus,
    neighbour,
    neigh_face,
    cluster,
    send_list,
    damage_list,
    damage_count,
    yield_mask,
    cohesion,
    to_points,
    from_points,
):
    elements = dof_values.shape[-1]
    total = lax.axis_size("dom")
    me = lax.axis_index("dom")
    position = jnp.stack([me.astype(jnp.int32), jnp.int32(total)])
    ghosts = send_list.shape[-1]

    field = spec((NQ, R, elements))
    block = spec((NQ * R, 2 * ghosts))
    x_s = (field.shape, F32)

    def y_s(blocks):
        return ((blocks, NQ, R, elements), F32)

    def m_o(blocks):
        return spec((NQ * NQ, blocks, elements))

    star = jnp.transpose(star_mats, (1, 2, 0, 3))
    own = jnp.transpose(flux_local, (1, 2, 0, 3))
    other = jnp.transpose(flux_neigh, (1, 2, 0, 3))
    inputs = [
        dof_values, star, kstiff, send_list, neighbour, neigh_face, cluster[None], damage_list, damage_count, cohesion[None], yield_mask
    ]
    held = [(one.shape, one.dtype) for one in inputs]
    held[3] = (send_list.shape[1:], send_list.dtype)
    held[8] = pltpu.SMEM(damage_count.shape, damage_count.dtype)
    outputs = [field, block, block, spec((ROWS, elements)), spec((3 * R, K3), BF16)]
    buffer_one, near, far, table, wk = call(
        predict_kernel,
        inputs,
        outputs,
        held
        + [((3 * R, LANES), F32), x_s, x_s, y_s(3), (m_o(3).shape, F32)]
        + [(one.shape, one.dtype) for one in outputs]
        + [pltpu.SemaphoreType.DMA((len(inputs),)), pltpu.SemaphoreType.DMA((len(outputs),))],
        space=HBM,
        grant=60,
    )
    wv = stack_weights(jnp.concatenate([jnp.swapaxes(kstiff, 1, 2), -flux_minus])).reshape(7 * R, K3)
    wf = stack_weights(-flux_plus).reshape(4, 4 * R, K3)
    wp = stack_weights(jnp.stack([to_points, from_points]))

    near, even, odd, buffer_one = exchange(near, far, me, total, buffer_one)
    started, ms, ml, mn, mask = call(
        local_kernel,
        [dof_values, buffer_one, star, own, other, wv, wf, table],
        (field, m_o(3), m_o(4), m_o(4), spec((R, elements))),
        [y_s(11)],
        cost=1_000_000_000,
    )
    updated, buffer_two, near, far = call(
        second_kernel,
        [position, started, dof_values, near, even, odd, wk, wf, table, ms, mn],
        (field, field, block, block),
        [x_s, x_s, y_s(4)],
        smem=1,
    )
    near, even, odd, buffer_two = exchange(near, far, me, total, buffer_two)
    started = call(
        again_kernel,
        [updated, buffer_two, wv, wf, table, ms, ml, mn],
        field,
        [y_s(11)],
        cost=1_000_000_000,
    )
    return call(
        last_kernel,
        [position, started, near, even, odd, wf, table, mn, mask, wp],
        spec(dof_values.shape),
        [x_s, y_s(4)],
        smem=1,
    )


def solution(mesh):
    return jax.shard_map(
        per_device,
        mesh=mesh,
        in_specs=(
            P(None, None, "dom"),
            P(None, None, None, "dom"),
            P(None, None, None, "dom"),
            P(None, None, None, "dom"),
            P(),
            P(),
            P(),
            P(None, "dom"),
            P(None, "dom"),
            P("dom"),
            P("dom", None, None),
            P("dom", None),
            P("dom"),
            P(None, "dom"),
            P("dom"),
            P(),
            P(),
        ),
        out_specs=P(None, None, "dom"),
        check_vma=False,
    )
```

time: 43.8 us -> 34.1 us (0.78)
  Pallas kernels: 21 us -> 16.3 us
  local copies, waits for them, and re-layouts: 5.05 us -> 2.15 us
  waiting for transfers between devices: 6.74 us -> 4.76 us
    pallas_call x5, Pallas kernels: 21 us -> 16.3 us  [call(): pl.pallas_call(kernel, out_shape=outputs, in_specs=[SMEM] * smem + [space...]
    unnamed x32 -> x27, local copies, waits for them, and re-layouts: 4.18 us -> 2.11 us
    ppermute x4, waiting for transfers between devices: 5.48 us -> 3.49 us  [the longest x2 3.48 us: exchange(): odd = lax.ppermute(to_odd, 'dom', odd_chip_swap(total))]
    squeeze x1 -> x0, local copies, waits for them, and re-layouts: 0.83 us -> none  [per_device(): send_list[0, 0]]
  transfers between devices with their start and end apart: 6 -> 6, of which waited for: 3 -> 3; matrix products, arithmetic and copies ran while one was open for 2% -> 2% of each run, Pallas kernels for 20% -> 18%
where the time goes in v2:
time: 34.1 us; the launch traced here: 33.8 us
  Pallas kernels  16.3 us (48%)
  starting transfers between devices  9.08 us (27%)
  waiting for transfers between devices  4.76 us (14%)
  local copies, waits for them, and re-layouts  2.15 us (6%)
  between operations  0.95 us (3%)
  other arithmetic  0.58 us (2%)
    pallas_call x5, Pallas kernels, call(): pl.pallas_call(kernel, out_shape=outputs, in_specs=[SMEM] * smem + [space...  16.3 us
    ppermute x2, starting transfers between devices, exchange(): odd = lax.ppermute(to_odd, 'dom', odd_chip_swap(total))  7.3 us
    ppermute x2, waiting for transfers between devices, exchange(): odd = lax.ppermute(to_odd, 'dom', odd_chip_swap(total))  3.48 us
    unnamed x27, local copies, waits for them, and re-layouts  2.11 us
    ppermute x2, starting transfers between devices, exchange(): even = lax.ppermute(to_even, 'dom', even_chip_swap(total))  1.63 us
    ppermute x2, waiting for transfers between devices, exchange(): got = lax.ppermute(near, 'dom', core_swap(total))  1.27 us
  transfers between devices with their start and end apart: 6, of which 3 were waited for; matrix products, arithmetic and copies ran while one was open for 2% of the time, Pallas kernels for 18%

profile of v2, /device:TPU:24, one launch (start us, length us, event | category | flops | bytes accessed | tf_op | source)
XLA Modules:
  0.0 33.8 jit_solution(12190795542062130950)
XLA Ops:
  0.7 3.5 %shard_map.163 = (f32[9,24,256]{2,1,0:T(8,128)}, f32[216,128]{1,0:T(8,128)}, f32[216,128]{1,0:T(8,128)}, f32[40,256]{1,0:T(8,128)}, bf16[72,72]{1,0:T(8,128)(2,1)}) custom-call(f32[9,20,256]{2,1,0:T(8,128)} %dof_ref.5, bf16[9,9,3,256]{3,2,1,0:T(4,128)(2,1)} %bitcast.13, f32[3,20,20]{2,1,0:T(8,128)} %kstiff_ref.1, s32[1,4,64]{2,1,0:T(4,128)} %send_ref.1, ...), custom_call_target="tpu_custom_call" | custom-call | bytes 1048576 | tf_op jit(solution)/shard_map/pallas_call | solution.py:341
  4.2 0.1 collective-permute-start
  4.3 0.7 %copy-done.8 = f32[3,20,20]{2,1,0:T(8,128)S(1)} copy-done((f32[3,20,20]{2,1,0:T(8,128)S(1)}, f32[3,20,20]{2,1,0:T(8,128)}, u32[]{:S(2)}) %copy-start.8) | copy-done | bytes 4824
  5.0 0.1 copy.23
  5.1 0.1 reduce-precision_convert_fusion
  5.3 0.7 %copy-done.10 = f32[4,20,20]{2,0,1:T(4,128)S(1)} copy-done((f32[4,20,20]{2,0,1:T(4,128)S(1)}, f32[4,20,20]{2,0,1:T(4,128)}, u32[]{:S(2)}) %copy-start.10) | copy-done | bytes 6424
  6.0 0.0 copy-start.5
  6.1 0.1 pad_maximum_fusion.wf_ref
  6.2 0.1 pad_maximum_fusion.1.wv_ref
  6.4 0.6 %copy-done.9 = f32[216,128]{1,0:T(8,128)S(1)} copy-done((f32[216,128]{1,0:T(8,128)S(1)}, f32[216,128]{1,0:T(8,128)}, u32[]{:S(2)}) %copy-start.9) | copy-done | bytes 110616
  6.9 1.6 %collective-permute-start.1 = (f32[216,128]{1,0:T(8,128)S(1)}, f32[216,128]{1,0:T(8,128)S(1)}, u32[]{:S(2)}, u32[]{:S(2)}) collective-permute-start(f32[216,128]{1,0:T(8,128)S(1)} %get-tuple-element.31), channel_id=1, source_target_pairs={{0,2},{1,3},{2,0},{3,1},{4,6},{5,7},{6,4},{7,5},{8,10},{9,11},{10,... | collective-permute-start | bytes 331784 | tf_op jit(solution)/shard_map/ppermute | solution.py:374
  8.5 3.3 %collective-permute-start.2 = (f32[216,128]{1,0:T(8,128)S(1)}, f32[216,128]{1,0:T(8,128)S(1)}, u32[]{:S(2)}, u32[]{:S(2)}) collective-permute-start(f32[216,128]{1,0:T(8,128)S(1)} %get-tuple-element.32), channel_id=1, source_target_pairs={{0,0},{1,1},{30,30},{31,31},{2,4},{4,2},{3,5},{5,3},{6,8},{8,6},{7... | collective-permute-start | bytes 331784 | tf_op jit(solution)/shard_map/ppermute | solution.py:375
  11.8 0.1 pad_add_fusion.pos_ref
  11.9 3.2 %shard_map.164 = (f32[9,24,256]{2,1,0:T(8,128)S(1)}, f32[81,3,256]{2,1,0:T(4,128)S(1)}, f32[81,4,256]{2,1,0:T(4,128)S(1)}, f32[81,4,256]{2,1,0:T(4,128)S(1)}, f32[24,256]{1,0:T(8,128)S(1)}) custom-call(f32[9,20,256]{2,1,0:T(8,128)S(1)} %copy-done, f32[9,24,256]{2,1,0:T(8,128)S(1)} %copy-done.4, bf16[9,9,3,256]{3,2,1,0:T(4,128)(2,1)S(1)} %bitcast.14, ...), custom_call_target="tpu_custom_call" | custom-call | flops 1000000000 | bytes 1048576 | tf_op jit(solution)/shard_map/pallas_call | solution.py:341
  15.1 1.9 %collective-permute-done.2.odd_ref = f32[216,128]{1,0:T(8,128)S(1)} collective-permute-done((f32[216,128]{1,0:T(8,128)S(1)}, f32[216,128]{1,0:T(8,128)S(1)}, u32[]{:S(2)}, u32[]{:S(2)}) %collective-permute-start.2) | collective-permute-done | bytes 110624 | tf_op jit(solution)/shard_map/ppermute | solution.py:375
  16.9 3.5 %shard_map.165 = (f32[9,24,256]{2,1,0:T(8,128)S(1)}, f32[9,24,256]{2,1,0:T(8,128)S(1)}, f32[216,128]{1,0:T(8,128)S(1)}, f32[216,128]{1,0:T(8,128)S(1)}) custom-call(s32[2]{0:T(128)S(1)} %pad_add_fusion.pos_ref, f32[9,24,256]{2,1,0:T(8,128)S(1)} %get-tuple-element.30.v_ref, f32[9,20,256]{2,1,0:T(8,128)S(1)} %copy-done, ...), custom_call_target="tpu_custom_call" | custom-call | bytes 1048576 | tf_op jit(solution)/shard_map/pallas_call | solution.py:341
  20.4 0.1 collective-permute-start.3
  20.5 1.3 %collective-permute-done.3.near_ref = f32[216,128]{1,0:T(8,128)S(1)} collective-permute-done((f32[216,128]{1,0:T(8,128)S(1)}, f32[216,128]{1,0:T(8,128)S(1)}, u32[]{:S(2)}, u32[]{:S(2)}) %collective-permute-start.3) | collective-permute-done | bytes 110624 | tf_op jit(solution)/shard_map/ppermute | solution.py:369
  21.8 0.1 collective-permute-start.4
  21.9 4.0 %collective-permute-start.5 = (f32[216,128]{1,0:T(8,128)S(1)}, f32[216,128]{1,0:T(8,128)S(1)}, u32[]{:S(2)}, u32[]{:S(2)}) collective-permute-start(f32[216,128]{1,0:T(8,128)S(1)} %get-tuple-element.43), channel_id=1, source_target_pairs={{0,0},{1,1},{30,30},{31,31},{2,4},{4,2},{3,5},{5,3},{6,8},{8,6},{7... | collective-permute-start | bytes 331784 | tf_op jit(solution)/shard_map/ppermute | solution.py:375
  25.9 0.1 pad_maximum_fusion.2.wp_ref
  26.0 3.0 %shard_map.166.v_ref = f32[9,24,256]{2,1,0:T(8,128)S(1)} custom-call(f32[9,24,256]{2,1,0:T(8,128)S(1)} %get-tuple-element.36.base_ref, f32[9,24,256]{2,1,0:T(8,128)S(1)} %get-tuple-element.40.b_ref, bf16[168,72]{1,0:T(8,128)(2,1)S(1)} %pad_maximum_fusion.1.wv_ref, bf16[4,96,72]{2,1,0:T(8,128)(2,1)S(1)} %pad_maximum_fusion.wf_ref, f32[40,256]{1,0:T(8,128)S(1)} %copy-done.2, ...), custom_call_target="tpu_custom_call" | custom-call | flops 1000000000 | bytes 1048576 | tf_op jit(solution)/shard_map/pallas_call | solution.py:341
  29.1 1.6 %collective-permute-done.5.odd_ref = f32[216,128]{1,0:T(8,128)S(1)} collective-permute-done((f32[216,128]{1,0:T(8,128)S(1)}, f32[216,128]{1,0:T(8,128)S(1)}, u32[]{:S(2)}, u32[]{:S(2)}) %collective-permute-start.5) | collective-permute-done | bytes 110624 | tf_op jit(solution)/shard_map/ppermute | solution.py:375
  30.7 3.1 %shard_map.167 = f32[9,20,256]{2,1,0:T(8,128)} custom-call(s32[2]{0:T(128)S(1)} %pad_add_fusion.pos_ref, f32[9,24,256]{2,1,0:T(8,128)S(1)} %shard_map.166.v_ref, f32[216,128]{1,0:T(8,128)S(1)} %collective-permute-done.3.near_ref, f32[216,128]{1,0:T(8,128)S(1)} %collective-permute-done.4.even_ref, f32[216,128]{1,0:T(8,128)S(1)} %collective-permute-done.5.odd_ref, ...), custom_call_target="tpu_custom_call" | custom-call | bytes 1048576 | tf_op jit(solution)/shard_map/pallas_call | solution.py:341
  (34 shorter events, 0.2 us)
Async XLA Ops:
  0.7 4.4 %copy-start.7 = (f32[4,4,20,20]{3,1,2,0:T(4,128)S(1)}, f32[4,4,20,20]{3,1,2,0:T(4,128)}, u32[]{:S(2)}) copy-start(f32[4,4,20,20]{3,1,2,0:T(4,128)} %param.23) | copy-start | bytes 76804
  4.2 0.8 %copy-start.8 = (f32[3,20,20]{2,1,0:T(8,128)S(1)}, f32[3,20,20]{2,1,0:T(8,128)}, u32[]{:S(2)}) copy-start(f32[3,20,20]{2,1,0:T(8,128)} %kstiff_ref.1) | copy-start | bytes 14404
  4.2 2.1 %collective-permute-start = (f32[216,128]{1,0:T(8,128)}, f32[216,128]{1,0:T(8,128)S(1)}, u32[]{:S(2)}, u32[]{:S(2)}) collective-permute-start(f32[216,128]{1,0:T(8,128)} %get-tuple-element.26), channel_id=1, source_target_pairs={{0,1},{1,0},{2,3},{3,2},{4,5},{5,4},{6,7},{7,6},{8,9},{9,8},{10,11... | collective-permute-start | bytes 331784 | tf_op jit(solution)/shard_map/ppermute | solution.py:369
  5.2 0.8 %copy-start.10 = (f32[4,20,20]{2,0,1:T(4,128)S(1)}, f32[4,20,20]{2,0,1:T(4,128)}, u32[]{:S(2)}) copy-start(f32[4,20,20]{2,0,1:T(4,128)} %param.22) | copy-start | bytes 19204
  6.0 0.9 %copy-start.9 = (f32[216,128]{1,0:T(8,128)S(1)}, f32[216,128]{1,0:T(8,128)}, u32[]{:S(2)}) copy-start(f32[216,128]{1,0:T(8,128)} %get-tuple-element.27) | copy-start | bytes 331780
  6.0 5.8 %copy-start.5 = (bf16[4,9,9,256]{3,0,2,1:T(4,128)(2,1)S(1)}, bf16[4,9,9,256]{3,0,2,1:T(4,128)(2,1)}, u32[]{:S(2)}) copy-start(bf16[4,9,9,256]{3,0,2,1:T(4,128)(2,1)} %param.19) | copy-start | bytes 497668
  6.0 5.8 %copy-start.6 = (bf16[4,9,9,256]{3,0,2,1:T(4,128)(2,1)S(1)}, bf16[4,9,9,256]{3,0,2,1:T(4,128)(2,1)}, u32[]{:S(2)}) copy-start(bf16[4,9,9,256]{3,0,2,1:T(4,128)(2,1)} %param.20) | copy-start | bytes 497668
  6.2 5.7 %copy-start.4 = (f32[9,24,256]{2,1,0:T(8,128)S(1)}, f32[9,24,256]{2,1,0:T(8,128)}, u32[]{:S(2)}) copy-start(f32[9,24,256]{2,1,0:T(8,128)} %get-tuple-element.28.b_ref) | copy-start | bytes 663556
  6.9 5.0 %copy-start = (f32[9,20,256]{2,1,0:T(8,128)S(1)}, f32[9,20,256]{2,1,0:T(8,128)}, u32[]{:S(2)}) copy-start(f32[9,20,256]{2,1,0:T(8,128)} %dof_ref.5) | copy-start | bytes 552964
  6.9 5.0 %copy-start.1 = (bf16[3,9,9,256]{3,0,2,1:T(4,128)(2,1)S(1)}, bf16[3,9,9,256]{3,0,2,1:T(4,128)(2,1)}, u32[]{:S(2)}) copy-start(bf16[3,9,9,256]{3,0,2,1:T(4,128)(2,1)} %param.18) | copy-start | bytes 373252
  6.9 5.0 %copy-start.2 = (f32[40,256]{1,0:T(8,128)S(1)}, f32[40,256]{1,0:T(8,128)}, u32[]{:S(2)}) copy-start(f32[40,256]{1,0:T(8,128)} %get-tuple-element.29.table_ref) | copy-start | bytes 122884
  6.9 8.1 %collective-permute-start.1 = (f32[216,128]{1,0:T(8,128)S(1)}, f32[216,128]{1,0:T(8,128)S(1)}, u32[]{:S(2)}, u32[]{:S(2)}) collective-permute-start(f32[216,128]{1,0:T(8,128)S(1)} %get-tuple-element.31), channel_id=1, source_target_pairs={{0,2},{1,3},{2,0},{3,1},{4,6},{5,7},{6,4},{7,5},{8,10},{9,11},{10,... | collective-permute-start | bytes 331784 | tf_op jit(solution)/shard_map/ppermute | solution.py:374
  8.5 8.4 %collective-permute-start.2 = (f32[216,128]{1,0:T(8,128)S(1)}, f32[216,128]{1,0:T(8,128)S(1)}, u32[]{:S(2)}, u32[]{:S(2)}) collective-permute-start(f32[216,128]{1,0:T(8,128)S(1)} %get-tuple-element.32), channel_id=1, source_target_pairs={{0,0},{1,1},{30,30},{31,31},{2,4},{4,2},{3,5},{5,3},{6,8},{8,6},{7... | collective-permute-start | bytes 331784 | tf_op jit(solution)/shard_map/ppermute | solution.py:375
  11.9 5.0 %copy-start.3 = (bf16[72,72]{1,0:T(8,128)(2,1)S(1)}, bf16[72,72]{1,0:T(8,128)(2,1)}, u32[]{:S(2)}) copy-start(bf16[72,72]{1,0:T(8,128)(2,1)} %get-tuple-element.33.wk_ref) | copy-start | bytes 31108
  16.9 3.6 %copy-start.11 = (f32[20,20]{1,0:T(8,128)S(1)}, f32[20,20]{1,0:T(8,128)}, u32[]{:S(2)}) copy-start(f32[20,20]{1,0:T(8,128)} %param.33) | copy-start | bytes 4804
  16.9 3.6 %copy-start.12 = (f32[20,20]{1,0:T(8,128)S(1)}, f32[20,20]{1,0:T(8,128)}, u32[]{:S(2)}) copy-start(f32[20,20]{1,0:T(8,128)} %param.32) | copy-start | bytes 4804
  20.4 1.4 %collective-permute-start.3 = (f32[216,128]{1,0:T(8,128)S(1)}, f32[216,128]{1,0:T(8,128)S(1)}, u32[]{:S(2)}, u32[]{:S(2)}) collective-permute-start(f32[216,128]{1,0:T(8,128)S(1)} %get-tuple-element.38), channel_id=1, source_target_pairs={{0,1},{1,0},{2,3},{3,2},{4,5},{5,4},{6,7},{7,6},{8,9},{9,8},{10,11... | collective-permute-start | bytes 331784 | tf_op jit(solution)/shard_map/ppermute | solution.py:369
  21.8 7.3 %collective-permute-start.4 = (f32[216,128]{1,0:T(8,128)S(1)}, f32[216,128]{1,0:T(8,128)S(1)}, u32[]{:S(2)}, u32[]{:S(2)}) collective-permute-start(f32[216,128]{1,0:T(8,128)S(1)} %get-tuple-element.42), channel_id=1, source_target_pairs={{0,2},{1,3},{2,0},{3,1},{4,6},{5,7},{6,4},{7,5},{8,10},{9,11},{10,... | collective-permute-start | bytes 331784 | tf_op jit(solution)/shard_map/ppermute | solution.py:374
  21.9 8.8 %collective-permute-start.5 = (f32[216,128]{1,0:T(8,128)S(1)}, f32[216,128]{1,0:T(8,128)S(1)}, u32[]{:S(2)}, u32[]{:S(2)}) collective-permute-start(f32[216,128]{1,0:T(8,128)S(1)} %get-tuple-element.43), channel_id=1, source_target_pairs={{0,0},{1,1},{30,30},{31,31},{2,4},{4,2},{3,5},{5,3},{6,8},{8,6},{7... | collective-permute-start | bytes 331784 | tf_op jit(solution)/shard_map/ppermute | solution.py:375

commit v3 on v2

v3 whole, which is shorter than its diff:
```python
import jax
import jax.numpy as jnp
from jax import lax
from jax.experimental import pallas as pl
from jax.experimental.pallas import tpu as pltpu
from jax.sharding import PartitionSpec as P

NQ = 9
NB = 20
R = 24
K3 = 3 * R
LANES = 128
FRICTION = 0.6
RELAXATION = 0.5
F32 = jnp.float32
BF16 = jnp.bfloat16


def stack_values(x):
    high = x.astype(BF16).astype(F32)
    return jnp.concatenate([high, x - high, high], axis=0).astype(BF16)


def dot(a, b):
    return jnp.dot(a, b, preferred_element_type=F32)


def widen(src_ref, dst_ref):
    for q in range(NQ):
        for p in range(NQ):
            dst_ref[q * NQ + p] = src_ref[q, p].astype(F32)


def basis_products(weights, x_ref, y_ref, blocks, base=0):
    for q in range(NQ):
        out = dot(weights, stack_values(x_ref[q]))
        for k in range(blocks):
            y_ref[base + k, q] = out[k * R : (k + 1) * R]


def star_sum(y_ref, m_refs, lanes, start):
    acc = list(start)
    for q in range(NQ):
        k = 0
        for m_ref in m_refs:
            for row in range(m_ref.shape[1]):
                y = y_ref[k, q, :, lanes]
                for p in range(NQ):
                    acc[p] = acc[p] + y * m_ref[q * NQ + p, row : row + 1, lanes]
                k += 1
    return acc


def each_half(elements, body):
    for start in range(0, elements, LANES):
        body(pl.ds(start, LANES))


def taylor_buffer(x_ref, first_ref, y_ref, m_ref, wk, weights_at, out_ref):
    elements = x_ref.shape[-1]
    basis_products(wk, x_ref, y_ref, 3)

    def first(lanes):
        acc = star_sum(y_ref, [m_ref], lanes, [jnp.zeros((R, LANES), F32)] * NQ)
        for p in range(NQ):
            first_ref[p, :, lanes] = acc[p]

    each_half(elements, first)
    basis_products(wk, first_ref, y_ref, 3)

    def second(lanes):
        acc = star_sum(y_ref, [m_ref], lanes, [jnp.zeros((R, LANES), F32)] * NQ)
        w1, w2 = weights_at(lanes)
        for p in range(NQ):
            out_ref[p, :, lanes] = x_ref[p, :, lanes] + (w1 * first_ref[p, :, lanes] + w2 * acc[p])

    each_half(elements, second)


def send_blocks(b_ref, send, near_ref, far_ref):
    elements = b_ref.shape[-1]
    columns = send.shape[-1]
    b = b_ref[...].reshape(NQ * R, elements)
    high = b.astype(BF16)
    low = (b - high.astype(F32)).astype(BF16)
    rows = lax.broadcasted_iota(jnp.int32, (elements, columns), 0).astype(F32)
    hot = jnp.where(rows == send, 1.0, 0.0).astype(BF16)
    out = dot(high, hot) + dot(low, hot)
    for q in range(NQ):
        near_ref[q * NB : (q + 1) * NB] = out[q * R : q * R + NB, : columns // 2]
        far_ref[q * NB : (q + 1) * NB] = out[q * R : q * R + NB, columns // 2 :]


def far_sides(source, index, face, w_ref, y_ref, base):
    high = source.astype(BF16)
    low = (source - high.astype(F32)).astype(BF16)
    both = jnp.concatenate([high, low], axis=0)
    elements = index.shape[-1]
    rows = lax.broadcasted_iota(jnp.int32, (source.shape[-1], elements), 0).astype(F32)
    size = NQ * R
    gathered = []
    for f in range(4):
        hot = jnp.where(rows == index[f : f + 1], 1.0, 0.0).astype(BF16)
        gathered.append(dot(both, hot))
    for f, picked in enumerate(gathered):
        kind = jnp.broadcast_to(face[f : f + 1], (R, elements))
        w = w_ref[W_FAR + 4 * f * R : W_FAR + 4 * (f + 1) * R]
        for q in range(NQ):
            high_rows = picked[q * R : (q + 1) * R]
            low_rows = picked[size + q * R : size + (q + 1) * R]
            out = dot(w, jnp.concatenate([high_rows, low_rows, high_rows], axis=0).astype(BF16))
            y_ref[base + f, q] = jnp.where(
                kind < 2,
                jnp.where(kind == 0, out[:R], out[R : 2 * R]),
                jnp.where(kind == 2, out[2 * R : 3 * R], out[3 * R :]),
            )


def place_kernel(twice_ref, once_ref):
    row = lax.broadcasted_iota(jnp.int32, twice_ref.shape, 0)
    column = lax.broadcasted_iota(jnp.int32, twice_ref.shape, 1)
    twice_ref[...] = jnp.where((column == row) | (column == row + R), 1.0, 0.0).astype(BF16)
    once_ref[...] = jnp.where(column == row + 2 * R, 1.0, 0.0).astype(BF16)


def place_weights(w, twice_ref, once_ref):
    high = w.astype(BF16)
    low = (w - high.astype(F32)).astype(BF16)
    return (dot(high, twice_ref[...]) + dot(low, once_ref[...])).astype(BF16)


W_OWN, W_FAR, W_POINTS, W_ROWS = 0, 7 * R, 23 * R, 25 * R


def fill_stiffness(w_ref, kstiff_ref):
    w_ref[...] = jnp.zeros(w_ref.shape, F32)
    for d in range(3):
        w_ref[d * R : d * R + NB, :NB] = kstiff_ref[d]


def fill_weights(w_ref, kstiff_ref, minus_ref, plus_ref, to_ref, from_ref):
    fill_stiffness(w_ref, kstiff_ref)
    row = lax.broadcasted_iota(jnp.int32, (R, LANES), 0)
    column = lax.broadcasted_iota(jnp.int32, (R, LANES), 1)
    same = jnp.where(row == column, 1.0, 0.0).astype(BF16)
    stiff = w_ref[: 3 * R]
    high = stiff.astype(BF16)
    low = (stiff - high.astype(F32)).astype(BF16)
    turned = [
        lax.dot_general(same, part, (((1,), (1,)), ((), ())), preferred_element_type=F32) for part in (high, low)
    ]
    turned = turned[0] + turned[1]
    for d in range(3):
        w_ref[W_OWN + d * R : W_OWN + (d + 1) * R, :R] = turned[:, d * R : (d + 1) * R]
    for f in range(4):
        start = W_OWN + (3 + f) * R
        w_ref[start : start + NB, :NB] = -minus_ref[:, f, :]
        for h in range(4):
            start = W_FAR + (4 * f + h) * R
            w_ref[start : start + NB, :NB] = -plus_ref[f, :, h, :]
    w_ref[W_POINTS : W_POINTS + NB, :NB] = to_ref[...]
    w_ref[W_POINTS + R : W_POINTS + R + NB, :NB] = from_ref[...]


def send_columns(send_ref):
    slots, ghosts = send_ref.shape
    width = slots * ghosts
    row = lax.broadcasted_iota(jnp.int32, (ghosts, width), 0)
    column = lax.broadcasted_iota(jnp.int32, (ghosts, width), 1)
    repeat = jnp.where(column % ghosts == row, 1.0, 0.0).astype(BF16)
    wide = dot(send_ref[...].astype(F32).astype(BF16), repeat)
    slot = lax.broadcasted_iota(jnp.int32, (1, width), 1) // ghosts
    first = jnp.where(slot == 0, wide[0:1], wide[1:2])
    second = jnp.where(slot == 2, wide[3:4], wide[2:3])
    return jnp.where(slot < 2, first, second)


NEIGHBOUR, FACE, CLUSTER, DAMAGE, COUNT, COHESION, SEND, YIELD = 0, 4, 8, 9, 10, 11, 12, 16
ROWS = 40


def predict_kernel(
    dof_ref, star_ref, kstiff_ref, send_ref, twice_ref, once_ref,
    b_ref, near_ref, far_ref, m_ref, wk_ref, send_out,
    w_ref, x_ref, first_ref, y_ref,
):
    fill_stiffness(w_ref, kstiff_ref)
    wk_ref[...] = place_weights(w_ref[...], twice_ref, once_ref)
    x_ref[:, NB:, :] = jnp.zeros((NQ, R - NB, x_ref.shape[-1]), F32)
    x_ref[:, :NB, :] = dof_ref[...]
    widen(star_ref, m_ref)
    taylor_buffer(x_ref, first_ref, y_ref, m_ref, wk_ref[...], lambda lanes: (0.5, 1.0 / 6.0), b_ref)
    send = send_columns(send_ref.at[0])
    send_out[...] = send
    send_blocks(b_ref, send, near_ref, far_ref)


NEIGHBOUR, FACE, CLUSTER, DAMAGE, COHESION, YIELD = 0, 4, 8, 9, 10, 16
ROWS = 40


def fill_table(table_ref, index_ref, face_ref, cluster_ref, damage_ref, count_ref, cohesion_ref, yield_ref):
    elements = table_ref.shape[-1]
    table_ref[...] = jnp.zeros(table_ref.shape, F32)
    table_ref[NEIGHBOUR : NEIGHBOUR + 4, :] = index_ref[...].astype(F32)
    table_ref[FACE : FACE + 4, :] = face_ref[...].astype(F32)
    table_ref[CLUSTER : CLUSTER + 1, :] = cluster_ref[...].astype(F32)
    slot = lax.broadcasted_iota(jnp.int32, (1, elements), 1)
    count = jnp.broadcast_to(count_ref[...], (1, elements))
    table_ref[DAMAGE : DAMAGE + 1, :] = jnp.where(slot < count, damage_ref[...], -1).astype(F32)
    table_ref[COHESION : COHESION + 1, :] = cohesion_ref[...]
    table_ref[YIELD : YIELD + NB, :] = yield_ref[...].astype(F32)


def local_part(b_ref, w_ref, table_ref, ms_ref, ml_ref, mn_ref, out_ref, y_ref, start):
    elements = b_ref.shape[-1]
    basis_products(w_ref[W_OWN:W_FAR], b_ref, y_ref, 7)
    source = b_ref[...].reshape(NQ * R, elements)
    far_sides(source, table_ref[NEIGHBOUR : NEIGHBOUR + 4], table_ref[FACE : FACE + 4], w_ref, y_ref, 7)

    def body(lanes):
        acc = star_sum(y_ref, [ms_ref, ml_ref, mn_ref], lanes, [start(p, lanes) for p in range(NQ)])
        for p in range(NQ):
            out_ref[p, :, lanes] = acc[p]

    each_half(elements, body)


def padded(ref, p, lanes):
    return jnp.concatenate([ref[p, :, lanes], jnp.zeros((R - NB, LANES), F32)], axis=0)


def local_kernel(
    dof_ref, b_ref, ms_ref, local_ref, neigh_ref,
    kstiff_ref, minus_ref, plus_ref, to_ref, from_ref, twice_ref, once_ref,
    index_ref, face_ref, cluster_ref, damage_ref, count_ref, cohesion_ref, yield_ref,
    out_ref, ml_ref, mn_ref, mask_ref, table_ref, weights_ref,
    w_ref, y_ref,
):
    fill_weights(w_ref, kstiff_ref, minus_ref, plus_ref, to_ref, from_ref)
    weights_ref[...] = place_weights(w_ref[...], twice_ref, once_ref)
    fill_table(table_ref, index_ref, face_ref, cluster_ref, damage_ref, count_ref, cohesion_ref, yield_ref)
    widen(local_ref, ml_ref)
    widen(neigh_ref, mn_ref)
    local_part(
        b_ref, weights_ref, table_ref, ms_ref, ml_ref, mn_ref, out_ref, y_ref, lambda p, lanes: padded(dof_ref, p, lanes)
    )
    elements = out_ref.shape[-1]
    rows = lax.broadcasted_iota(jnp.int32, (elements, elements), 0).astype(F32)
    listed = lax.dot_general(
        jnp.ones((8, elements), BF16),
        jnp.where(rows == table_ref[DAMAGE : DAMAGE + 1], 1.0, 0.0).astype(BF16),
        (((1,), (1,)), ((), ())),
        preferred_element_type=F32,
    )[0:1]
    mask_ref[...] = jnp.where(listed > 0.5, table_ref[YIELD : YIELD + R], 0.0)


def again_kernel(base_ref, b_ref, w_ref, table_ref, ms_ref, ml_ref, mn_ref, out_ref, y_ref):
    local_part(b_ref, w_ref, table_ref, ms_ref, ml_ref, mn_ref, out_ref, y_ref, lambda p, lanes: base_ref[p, :, lanes])


def ghost_source(near_ref, even_ref, odd_ref):
    me, total = lax.axis_index("dom"), lax.axis_size("dom")
    core = me % 2
    chip = (me // 2) % 2 == 0
    near, even, odd = near_ref[...], even_ref[...], odd_ref[...]
    up = jnp.where(chip, even, odd)
    down = jnp.where(chip, odd, even)
    half = near.shape[1] // 2
    side = lax.broadcasted_iota(jnp.int32, near.shape, 1) // half
    across = jnp.where(core == 0, down, up)
    one = jnp.where(side == core, across, near)
    two = jnp.where(side == 0, up, down)
    one = jnp.where(jnp.where(side == 0, me - 1, total - 2 - me) >= 0, one, 0.0)
    two = jnp.where(jnp.where(side == 0, total - 3 - me, me - 2) >= 0, two, 0.0)
    pad = jnp.zeros((R - NB, 2 * near.shape[1]), F32)
    both = jnp.concatenate([one, two], axis=1)
    return jnp.concatenate([piece for q in range(NQ) for piece in (both[q * NB : (q + 1) * NB], pad)], axis=0)


def ghost_part(near_ref, even_ref, odd_ref, w_ref, table_ref, y_ref):
    elements = table_ref.shape[-1]
    ghosts = near_ref.shape[-1] // 2
    index = table_ref[NEIGHBOUR : NEIGHBOUR + 4] - elements
    last = jnp.where(index >= 3 * ghosts, index - ghosts, index + ghosts)
    index = jnp.where(index >= 2 * ghosts, last, index)
    source = ghost_source(near_ref, even_ref, odd_ref)
    far_sides(source, index, table_ref[FACE : FACE + 4], w_ref, y_ref, 0)


def second_kernel(
    v_ref, dof_ref, near_ref, even_ref, odd_ref, wk_ref, send_ref, w_ref, table_ref, ms_ref, mn_ref,
    state_ref, b_ref, near_out, far_out,
    x_ref, first_ref, y_ref,
):
    elements = v_ref.shape[-1]
    ghost_part(near_ref, even_ref, odd_ref, w_ref, table_ref, y_ref)

    def body(lanes):
        acc = star_sum(y_ref, [mn_ref], lanes, [v_ref[p, :, lanes] for p in range(NQ)])
        fine = table_ref[CLUSTER : CLUSTER + 1, lanes] < 0.5
        for p in range(NQ):
            state_ref[p, :, lanes] = acc[p]
            x_ref[p, :, lanes] = jnp.where(fine, acc[p], padded(dof_ref, p, lanes))

    each_half(elements, body)

    def weights_at(lanes):
        fine = table_ref[CLUSTER : CLUSTER + 1, lanes] < 0.5
        return jnp.where(fine, 0.5, 1.5), jnp.where(fine, 1.0 / 6.0, 7.0 / 6.0)

    taylor_buffer(x_ref, first_ref, y_ref, ms_ref, wk_ref[...], weights_at, b_ref)
    send_blocks(b_ref, send_ref[...], near_out, far_out)


def last_kernel(
    v_ref, near_ref, even_ref, odd_ref, w_ref, table_ref, mn_ref, mask_ref,
    result_ref,
    x_ref, y_ref, out_ref, sems,
):
    writes = [pltpu.make_async_copy(out_ref.at[q], result_ref.at[q], sems.at[q]) for q in range(NQ)]
    elements = v_ref.shape[-1]
    ghost_part(near_ref, even_ref, odd_ref, w_ref, table_ref, y_ref)

    def body(lanes):
        acc = star_sum(y_ref, [mn_ref], lanes, [v_ref[p, :, lanes] for p in range(NQ)])
        for p in range(NQ):
            x_ref[p, :, lanes] = acc[p]

    each_half(elements, body)

    for q in range(6, NQ):
        out_ref[q] = x_ref[q, :NB, :]
        writes[q].start()
    points = [dot(w_ref[W_POINTS : W_POINTS + R], stack_values(x_ref[q])) for q in range(6)]
    pressure = (points[0] + points[1] + points[2]) / 3.0
    normal = [points[q] - pressure for q in range(3)]
    normal_sum = normal[0] * normal[0] + normal[1] * normal[1] + normal[2] * normal[2]
    shear_sum = points[3] * points[3] + points[4] * points[4] + points[5] * points[5]
    tau = jnp.sqrt(0.5 * normal_sum + shear_sum)
    strength = table_ref[COHESION : COHESION + 1]
    limit = jnp.maximum(strength - FRICTION * pressure, 0.5 * strength)
    rate = jnp.where(mask_ref[...] > 0.5, RELAXATION * (limit / jnp.maximum(tau, limit) - 1.0), 0.0)
    deviation = normal + points[3:]
    for q in range(6):
        change = dot(w_ref[W_POINTS + R : W_ROWS], stack_values(rate * deviation[q]))
        out_ref[q] = (x_ref[q] + change)[:NB]
        writes[q].start()
    for write in writes:
        write.wait()


def spec(shape, dtype=F32):
    return jax.ShapeDtypeStruct(shape, dtype)


VMEM = pl.BlockSpec(memory_space=pltpu.VMEM)
HBM = pl.BlockSpec(memory_space=pltpu.HBM)


def call(kernel, inputs, outputs, scratch, cost=0, out_space=VMEM):
    return pl.pallas_call(
        kernel,
        out_shape=outputs,
        in_specs=[VMEM] * len(inputs),
        out_specs=jax.tree.map(lambda _: out_space, outputs),
        scratch_shapes=[pltpu.VMEM(*one) if isinstance(one, tuple) else one for one in scratch],
        compiler_params=pltpu.CompilerParams(vmem_limit_bytes=40 * 1024 * 1024),
        cost_estimate=pl.CostEstimate(flops=cost, bytes_accessed=1 << 20, transcendentals=0),
    )(*inputs)


def core_swap(total):
    return [(i, i ^ 1) for i in range(total)]


def even_chip_swap(total):
    return [(i, i ^ 2) for i in range(total)]


def odd_chip_swap(total):
    route = [(i, i) for i in (0, 1, total - 2, total - 1)]
    for i in range(2, total - 2, 4):
        for k in (i, i + 1):
            route += [(k, k + 2), (k + 2, k)]
    return route


def exchange(near, far, me, total, beside):
    got = lax.ppermute(near, "dom", core_swap(total))
    left = lax.broadcasted_iota(jnp.int32, got.shape, 1) < got.shape[1] // 2
    forward = left == ((me // 2) % 2 == 0)
    to_even, to_odd = jnp.where(forward, got, far), jnp.where(forward, far, got)
    beside, to_even, to_odd = lax.optimization_barrier((beside, to_even, to_odd))
    even = lax.ppermute(to_even, "dom", even_chip_swap(total))
    odd = lax.ppermute(to_odd, "dom", odd_chip_swap(total))
    return got, even, odd, beside


def per_device(
    dof_values,
    star_mats,
    flux_local,
    flux_neigh,
    kstiff,
    flux_minus,
    flux_plus,
    neighbour,
    neigh_face,
    cluster,
    send_list,
    damage_list,
    damage_count,
    yield_mask,
    cohesion,
    to_points,
    from_points,
):
    elements = dof_values.shape[-1]
    total = lax.axis_size("dom")
    me = lax.axis_index("dom")
    ghosts = send_list.shape[-1]

    field = spec((NQ, R, elements))
    block = spec((NQ * NB, 2 * ghosts))
    x_s = (field.shape, F32)

    def y_s(blocks):
        return ((blocks, NQ, R, elements), F32)

    def m_o(blocks):
        return spec((NQ * NQ, blocks, elements))

    star = jnp.transpose(star_mats, (1, 2, 0, 3))
    own = jnp.transpose(flux_local, (1, 2, 0, 3))
    other = jnp.transpose(flux_neigh, (1, 2, 0, 3))
    minus = jnp.transpose(flux_minus, (1, 0, 2))
    plus = jnp.transpose(flux_plus, (0, 2, 1, 3))

    place = spec((LANES, K3), BF16)
    twice, once = call(place_kernel, [], (place, place), [], cost=4_000_000_000)
    buffer_one, near, far, ms, wk, send = call(
        predict_kernel,
        [dof_values, star, kstiff, send_list, twice, once],
        (field, block, block, m_o(3), spec((3 * R, K3), BF16), spec((1, 4 * ghosts))),
        [((3 * R, LANES), F32), x_s, x_s, y_s(3)],
    )
    near, even, odd, buffer_one = exchange(near, far, me, total, buffer_one)
    started, ml, mn, mask, table, weights = call(
        local_kernel,
        [
            dof_values, buffer_one, ms, own, other,
            kstiff, minus, plus, to_points, from_points, twice, once,
            neighbour, neigh_face, cluster[None], damage_list, damage_count[None], cohesion[None], yield_mask,
        ],
        (field, m_o(4), m_o(4), spec((R, elements)), spec((ROWS, elements)), spec((W_ROWS, K3), BF16)),
        [((W_ROWS, LANES), F32), y_s(11)],
        cost=1_000_000_000,
    )
    updated, buffer_two, near, far = call(
        second_kernel,
        [started, dof_values, near, even, odd, wk, send, weights, table, ms, mn],
        (field, field, block, block),
        [x_s, x_s, y_s(4)],
    )
    near, even, odd, buffer_two = exchange(near, far, me, total, buffer_two)
    started = call(
        again_kernel,
        [updated, buffer_two, weights, table, ms, ml, mn],
        field,
        [y_s(11)],
        cost=1_000_000_000,
    )
    return call(
        last_kernel,
        [started, near, even, odd, weights, table, mn, mask],
        spec(dof_values.shape),
        [x_s, y_s(4), (dof_values.shape, F32), pltpu.SemaphoreType.DMA((NQ,))],
        out_space=HBM,
    )


def solution(mesh):
    return jax.shard_map(
        per_device,
        mesh=mesh,
        in_specs=(
            P(None, None, "dom"),
            P(None, None, None, "dom"),
            P(None, None, None, "dom"),
            P(None, None, None, "dom"),
            P(),
            P(),
            P(),
            P(None, "dom"),
            P(None, "dom"),
            P("dom"),
            P("dom", None, None),
            P("dom", None),
            P("dom"),
            P(None, "dom"),
            P("dom"),
            P(),
            P(),
        ),
        out_specs=P(None, None, "dom"),
        check_vma=False,
    )
```

time: 34.1 us -> 30.5 us (0.89)
  Pallas kernels: 16.3 us -> 13.8 us
  other arithmetic: 0.58 us -> 0.04 us
  local copies, waits for them, and re-layouts: 2.15 us -> 1.62 us
    pallas_call x5 -> x6, Pallas kernels: 16.3 us -> 13.8 us  [call(): pl.pallas_call(kernel, out_shape=outputs, in_specs=[VMEM] * len(inputs),...]
    ppermute x2, starting transfers between devices: 7.3 us -> 6.42 us  [exchange(): odd = lax.ppermute(to_odd, 'dom', odd_chip_swap(total))]
    ppermute x2, starting transfers between devices: 1.63 us -> 2.52 us  [exchange(): even = lax.ppermute(to_even, 'dom', even_chip_swap(total))]
    ppermute x2, waiting for transfers between devices: 3.48 us -> 2.78 us  [exchange(): odd = lax.ppermute(to_odd, 'dom', odd_chip_swap(total))]
    ppermute x2, waiting for transfers between devices: 1.27 us -> 1.87 us  [exchange(): got = lax.ppermute(near, 'dom', core_swap(total))]
    unnamed x27 -> x32, local copies, waits for them, and re-layouts: 2.11 us -> 1.62 us
  transfers between devices with their start and end apart: 6 -> 6, of which waited for: 3 -> 4; matrix products, arithmetic and copies ran while one was open for 2% -> 0% of each run, Pallas kernels for 18% -> 22%
where the time goes in v3:
time: 30.5 us; the launch traced here: 30.3 us
  Pallas kernels  13.8 us (45%)
  starting transfers between devices  9.08 us (30%)
  waiting for transfers between devices  4.66 us (15%)
  local copies, waits for them, and re-layouts  1.62 us (5%)
  between operations  1.09 us (4%)
    pallas_call x6, Pallas kernels, call(): pl.pallas_call(kernel, out_shape=outputs, in_specs=[VMEM] * len(inputs),...  13.8 us
    ppermute x2, starting transfers between devices, exchange(): odd = lax.ppermute(to_odd, 'dom', odd_chip_swap(total))  6.42 us
    ppermute x2, waiting for transfers between devices, exchange(): odd = lax.ppermute(to_odd, 'dom', odd_chip_swap(total))  2.78 us
    ppermute x2, starting transfers between devices, exchange(): even = lax.ppermute(to_even, 'dom', even_chip_swap(total))  2.52 us
    ppermute x2, waiting for transfers between devices, exchange(): got = lax.ppermute(near, 'dom', core_swap(total))  1.87 us
    unnamed x32, local copies, waits for them, and re-layouts  1.62 us
  transfers between devices with their start and end apart: 6, of which 4 were waited for; matrix products, arithmetic and copies ran while one was open for 0% of the time, Pallas kernels for 22%

profile of v3, /device:TPU:24, one launch (start us, length us, event | category | flops | bytes accessed | tf_op | source)
XLA Modules:
  0.0 30.3 jit_solution(12372918630178355663)
XLA Ops:
  0.0 0.0 copy-start.3
  0.1 0.9 %copy-done = f32[9,20,256]{2,1,0:T(8,128)S(1)} copy-done((f32[9,20,256]{2,1,0:T(8,128)S(1)}, f32[9,20,256]{2,1,0:T(8,128)}, u32[]{:S(2)}) %copy-start) | copy-done | bytes 184344
  0.9 0.1 copy-done.1
  1.1 0.0 copy-start.11
  1.1 0.0 copy-start.12
  1.1 0.0 copy-start.14
  1.1 0.0 copy-start.15
  1.1 1.7 %shard_map.164 = (f32[9,24,256]{2,1,0:T(8,128)S(1)}, f32[180,128]{1,0:T(8,128)S(1)}, f32[180,128]{1,0:T(8,128)S(1)}, f32[81,3,256]{2,1,0:T(4,128)S(1)}, bf16[72,...) custom-call(f32[9,20,256]{2,1,0:T(8,128)S(1)} %copy-done, bf16[9,9,3,256]{3,2,1,0:T(4,128)(2,1)S(1)} %bitcast.9, ...), custom_call_target="tpu_custom_call" | custom-call | bytes 1048576 | tf_op jit(solution)/shard_map/pallas_call | solution.py:363
  2.8 0.1 collective-permute-start
  3.6 0.6 %collective-permute-done.near_ref = f32[180,128]{1,0:T(8,128)S(1)} collective-permute-done((f32[180,128]{1,0:T(8,128)S(1)}, f32[180,128]{1,0:T(8,128)S(1)}, u32[]{:S(2)}, u32[]{:S(2)}) %collective-permute-start) | collective-permute-done | bytes 92192 | tf_op jit(solution)/shard_map/ppermute | solution.py:391
  4.2 1.6 %collective-permute-start.1 = (f32[180,128]{1,0:T(8,128)S(1)}, f32[180,128]{1,0:T(8,128)S(1)}, u32[]{:S(2)}, u32[]{:S(2)}) collective-permute-start(f32[180,128]{1,0:T(8,128)S(1)} %get-tuple-element.37), channel_id=1, source_target_pairs={{0,2},{1,3},{2,0},{3,1},{4,6},{5,7},{6,4},{7,5},{8,10},{9,11},{10,... | collective-permute-start | bytes 276488 | tf_op jit(solution)/shard_map/ppermute | solution.py:396
  5.8 3.3 %collective-permute-start.2 = (f32[180,128]{1,0:T(8,128)S(1)}, f32[180,128]{1,0:T(8,128)S(1)}, u32[]{:S(2)}, u32[]{:S(2)}) collective-permute-start(f32[180,128]{1,0:T(8,128)S(1)} %get-tuple-element.38), channel_id=1, source_target_pairs={{0,0},{1,1},{30,30},{31,31},{2,4},{4,2},{3,5},{5,3},{6,8},{8,6},{7... | collective-permute-start | bytes 276488 | tf_op jit(solution)/shard_map/ppermute | solution.py:397
  9.1 0.0 copy-start.13
  9.2 0.6 %copy-done.13 = s32[256]{0:T(256)S(1)} copy-done((s32[256]{0:T(256)S(1)}, s32[256]{0:T(256)}, u32[]{:S(2)}) %copy-start.13) | copy-done | bytes 1048
  9.8 3.6 %shard_map.165 = (f32[9,24,256]{2,1,0:T(8,128)S(1)}, f32[81,4,256]{2,1,0:T(4,128)S(1)}, f32[81,4,256]{2,1,0:T(4,128)S(1)}, f32[24,256]{1,0:T(8,128)S(1)}, f32[40...) custom-call(f32[9,20,256]{2,1,0:T(8,128)S(1)} %copy-done, f32[9,24,256]{2,1,0:T(8,128)S(1)} %get-tuple-element.34.b_ref, ...), custom_call_target="tpu_custom_call" | custom-call | flops 1000000000 | bytes 1048576 | tf_op jit(solution)/shard_map/pallas_call | solution.py:363
  13.3 0.7 %collective-permute-done.2.odd_ref = f32[180,128]{1,0:T(8,128)S(1)} collective-permute-done((f32[180,128]{1,0:T(8,128)S(1)}, f32[180,128]{1,0:T(8,128)S(1)}, u32[]{:S(2)}, u32[]{:S(2)}) %collective-permute-start.2) | collective-permute-done | bytes 92192 | tf_op jit(solution)/shard_map/ppermute | solution.py:397
  14.0 2.9 %shard_map.166 = (f32[9,24,256]{2,1,0:T(8,128)S(1)}, f32[9,24,256]{2,1,0:T(8,128)S(1)}, f32[180,128]{1,0:T(8,128)S(1)}, f32[180,128]{1,0:T(8,128)S(1)}) custom-call(f32[9,24,256]{2,1,0:T(8,128)S(1)} %get-tuple-element.36.v_ref, f32[9,20,256]{2,1,0:T(8,128)S(1)} %copy-done, f32[180,128]{1,0:T(8,128)S(1)} %collective-permute-done.near_ref, ...), custom_call_target="tpu_custom_call" | custom-call | bytes 1048576 | tf_op jit(solution)/shard_map/pallas_call | solution.py:363
  17.0 0.1 collective-permute-start.3
  17.0 1.3 %collective-permute-done.3.near_ref = f32[180,128]{1,0:T(8,128)S(1)} collective-permute-done((f32[180,128]{1,0:T(8,128)S(1)}, f32[180,128]{1,0:T(8,128)S(1)}, u32[]{:S(2)}, u32[]{:S(2)}) %collective-permute-start.3) | collective-permute-done | bytes 92192 | tf_op jit(solution)/shard_map/ppermute | solution.py:391
  18.4 1.0 %collective-permute-start.4 = (f32[180,128]{1,0:T(8,128)S(1)}, f32[180,128]{1,0:T(8,128)S(1)}, u32[]{:S(2)}, u32[]{:S(2)}) collective-permute-start(f32[180,128]{1,0:T(8,128)S(1)} %get-tuple-element.50), channel_id=1, source_target_pairs={{0,2},{1,3},{2,0},{3,1},{4,6},{5,7},{6,4},{7,5},{8,10},{9,11},{10,... | collective-permute-start | bytes 276488 | tf_op jit(solution)/shard_map/ppermute | solution.py:396
  19.3 3.1 %collective-permute-start.5 = (f32[180,128]{1,0:T(8,128)S(1)}, f32[180,128]{1,0:T(8,128)S(1)}, u32[]{:S(2)}, u32[]{:S(2)}) collective-permute-start(f32[180,128]{1,0:T(8,128)S(1)} %get-tuple-element.51), channel_id=1, source_target_pairs={{0,0},{1,1},{30,30},{31,31},{2,4},{4,2},{3,5},{5,3},{6,8},{8,6},{7... | collective-permute-start | bytes 276488 | tf_op jit(solution)/shard_map/ppermute | solution.py:397
  22.5 3.0 %shard_map.167.v_ref = f32[9,24,256]{2,1,0:T(8,128)S(1)} custom-call(f32[9,24,256]{2,1,0:T(8,128)S(1)} %get-tuple-element.44.base_ref, f32[9,24,256]{2,1,0:T(8,128)S(1)} %get-tuple-element.48.b_ref, bf16[600,72]{1,0:T(8,128)(2,1)S(1)} %get-tuple-element.41.w_ref, f32[40,256]{1,0:T(8,128)S(1)} %get-tuple-element.42.table_ref, ...), custom_call_target="tpu_custom_call" | custom-call | flops 1000000000 | bytes 1048576 | tf_op jit(solution)/shard_map/pallas_call | solution.py:363
  25.5 2.1 %collective-permute-done.5.odd_ref = f32[180,128]{1,0:T(8,128)S(1)} collective-permute-done((f32[180,128]{1,0:T(8,128)S(1)}, f32[180,128]{1,0:T(8,128)S(1)}, u32[]{:S(2)}, u32[]{:S(2)}) %collective-permute-start.5) | collective-permute-done | bytes 92192 | tf_op jit(solution)/shard_map/ppermute | solution.py:397
  27.6 2.6 %shard_map.168 = f32[9,20,256]{2,1,0:T(8,128)} custom-call(f32[9,24,256]{2,1,0:T(8,128)S(1)} %shard_map.167.v_ref, f32[180,128]{1,0:T(8,128)S(1)} %collective-permute-done.3.near_ref, f32[180,128]{1,0:T(8,128)S(1)} %collective-permute-done.4.even_ref, f32[180,128]{1,0:T(8,128)S(1)} %collective-permute-done.5.odd_ref, ...), custom_call_target="tpu_custom_call" | custom-call | bytes 1048576 | tf_op jit(solution)/shard_map/pallas_call | solution.py:363
  (29 shorter events, 0.1 us)
Async XLA Ops:
  0.0 0.9 %copy-start = (f32[9,20,256]{2,1,0:T(8,128)S(1)}, f32[9,20,256]{2,1,0:T(8,128)}, u32[]{:S(2)}) copy-start(f32[9,20,256]{2,1,0:T(8,128)} %dof_ref.5) | copy-start | bytes 552964
  0.0 0.9 %copy-start.2 = (f32[3,20,20]{2,1,0:T(8,128)S(1)}, f32[3,20,20]{2,1,0:T(8,128)}, u32[]{:S(2)}) copy-start(f32[3,20,20]{2,1,0:T(8,128)} %kstiff_ref.3) | copy-start | bytes 14404
  0.0 1.0 %copy-start.1 = (bf16[3,9,9,256]{3,0,2,1:T(4,128)(2,1)S(1)}, bf16[3,9,9,256]{3,0,2,1:T(4,128)(2,1)}, u32[]{:S(2)}) copy-start(bf16[3,9,9,256]{3,0,2,1:T(4,128)(2,1)} %param.18) | copy-start | bytes 373252
  0.0 1.0 %copy-start.3 = (s32[1,4,64]{2,1,0:T(4,128)S(1)}, s32[1,4,64]{2,1,0:T(4,128)}, u32[]{:S(2)}) copy-start(s32[1,4,64]{2,1,0:T(4,128)} %send_ref.1) | copy-start | bytes 3076
  1.0 8.0 %copy-start.6 = (f32[4,4,20,20]{3,1,2,0:T(4,128)S(1)}, f32[4,4,20,20]{3,1,2,0:T(4,128)}, u32[]{:S(2)}) copy-start(f32[4,4,20,20]{3,1,2,0:T(4,128)} %param.23) | copy-start | bytes 76804
  1.0 8.1 %copy-start.9 = (f32[20,20]{1,0:T(8,128)S(1)}, f32[20,20]{1,0:T(8,128)}, u32[]{:S(2)}) copy-start(f32[20,20]{1,0:T(8,128)} %to_ref.1) | copy-start | bytes 4804
  1.1 8.1 %copy-start.10 = (f32[20,20]{1,0:T(8,128)S(1)}, f32[20,20]{1,0:T(8,128)}, u32[]{:S(2)}) copy-start(f32[20,20]{1,0:T(8,128)} %from_ref.1) | copy-start | bytes 4804
  1.1 8.1 %copy-start.11 = (s32[4,256]{1,0:T(4,128)S(1)}, s32[4,256]{1,0:T(4,128)}, u32[]{:S(2)}) copy-start(s32[4,256]{1,0:T(4,128)} %index_ref.1) | copy-start | bytes 12292
  1.1 8.1 %copy-start.12 = (s32[4,256]{1,0:T(4,128)S(1)}, s32[4,256]{1,0:T(4,128)}, u32[]{:S(2)}) copy-start(s32[4,256]{1,0:T(4,128)} %face_ref.1) | copy-start | bytes 12292
  1.1 8.1 %copy-start.14 = (s32[1,256]{1,0:T(1,128)S(1)}, s32[1,256]{1,0:T(1,128)}, u32[]{:S(2)}) copy-start(s32[1,256]{1,0:T(1,128)} %damage_ref.1) | copy-start | bytes 3076
  1.1 8.1 %copy-start.15 = (f32[256]{0:T(256)S(1)}, f32[256]{0:T(256)}, u32[]{:S(2)}) copy-start(f32[256]{0:T(256)} %param.31) | copy-start | bytes 3076
  2.8 1.4 %collective-permute-start = (f32[180,128]{1,0:T(8,128)S(1)}, f32[180,128]{1,0:T(8,128)S(1)}, u32[]{:S(2)}, u32[]{:S(2)}) collective-permute-start(f32[180,128]{1,0:T(8,128)S(1)} %get-tuple-element.32), channel_id=1, source_target_pairs={{0,1},{1,0},{2,3},{3,2},{4,5},{5,4},{6,7},{7,6},{8,9},{9,8},{10,11... | collective-permute-start | bytes 276488 | tf_op jit(solution)/shard_map/ppermute | solution.py:391
  4.2 5.0 %copy-start.4 = (bf16[4,9,9,256]{3,0,2,1:T(4,128)(2,1)S(1)}, bf16[4,9,9,256]{3,0,2,1:T(4,128)(2,1)}, u32[]{:S(2)}) copy-start(bf16[4,9,9,256]{3,0,2,1:T(4,128)(2,1)} %param.19) | copy-start | bytes 497668
  4.2 5.0 %copy-start.5 = (bf16[4,9,9,256]{3,0,2,1:T(4,128)(2,1)S(1)}, bf16[4,9,9,256]{3,0,2,1:T(4,128)(2,1)}, u32[]{:S(2)}) copy-start(bf16[4,9,9,256]{3,0,2,1:T(4,128)(2,1)} %param.20) | copy-start | bytes 497668
  4.2 5.0 %copy-start.7 = (f32[4,20,20]{2,0,1:T(4,128)S(1)}, f32[4,20,20]{2,0,1:T(4,128)}, u32[]{:S(2)}) copy-start(f32[4,20,20]{2,0,1:T(4,128)} %param.22) | copy-start | bytes 19204
  4.2 5.0 %copy-start.8 = (s32[20,256]{1,0:T(8,128)S(1)}, s32[20,256]{1,0:T(8,128)}, u32[]{:S(2)}) copy-start(s32[20,256]{1,0:T(8,128)} %yield_ref.1) | copy-start | bytes 61444
  4.2 9.1 %collective-permute-start.1 = (f32[180,128]{1,0:T(8,128)S(1)}, f32[180,128]{1,0:T(8,128)S(1)}, u32[]{:S(2)}, u32[]{:S(2)}) collective-permute-start(f32[180,128]{1,0:T(8,128)S(1)} %get-tuple-element.37), channel_id=1, source_target_pairs={{0,2},{1,3},{2,0},{3,1},{4,6},{5,7},{6,4},{7,5},{8,10},{9,11},{10,... | collective-permute-start | bytes 276488 | tf_op jit(solution)/shard_map/ppermute | solution.py:396
  5.8 8.3 %collective-permute-start.2 = (f32[180,128]{1,0:T(8,128)S(1)}, f32[180,128]{1,0:T(8,128)S(1)}, u32[]{:S(2)}, u32[]{:S(2)}) collective-permute-start(f32[180,128]{1,0:T(8,128)S(1)} %get-tuple-element.38), channel_id=1, source_target_pairs={{0,0},{1,1},{30,30},{31,31},{2,4},{4,2},{3,5},{5,3},{6,8},{8,6},{7... | collective-permute-start | bytes 276488 | tf_op jit(solution)/shard_map/ppermute | solution.py:397
  9.1 0.7 %copy-start.13 = (s32[256]{0:T(256)S(1)}, s32[256]{0:T(256)}, u32[]{:S(2)}) copy-start(s32[256]{0:T(256)} %param.26) | copy-start | bytes 3076
  17.0 1.4 %collective-permute-start.3 = (f32[180,128]{1,0:T(8,128)S(1)}, f32[180,128]{1,0:T(8,128)S(1)}, u32[]{:S(2)}, u32[]{:S(2)}) collective-permute-start(f32[180,128]{1,0:T(8,128)S(1)} %get-tuple-element.46), channel_id=1, source_target_pairs={{0,1},{1,0},{2,3},{3,2},{4,5},{5,4},{6,7},{7,6},{8,9},{9,8},{10,11... | collective-permute-start | bytes 276488 | tf_op jit(solution)/shard_map/ppermute | solution.py:391
  18.4 7.1 %collective-permute-start.4 = (f32[180,128]{1,0:T(8,128)S(1)}, f32[180,128]{1,0:T(8,128)S(1)}, u32[]{:S(2)}, u32[]{:S(2)}) collective-permute-start(f32[180,128]{1,0:T(8,128)S(1)} %get-tuple-element.50), channel_id=1, source_target_pairs={{0,2},{1,3},{2,0},{3,1},{4,6},{5,7},{6,4},{7,5},{8,10},{9,11},{10,... | collective-permute-start | bytes 276488 | tf_op jit(solution)/shard_map/ppermute | solution.py:396
  19.3 8.3 %collective-permute-start.5 = (f32[180,128]{1,0:T(8,128)S(1)}, f32[180,128]{1,0:T(8,128)S(1)}, u32[]{:S(2)}, u32[]{:S(2)}) collective-permute-start(f32[180,128]{1,0:T(8,128)S(1)} %get-tuple-element.51), channel_id=1, source_target_pairs={{0,0},{1,1},{30,30},{31,31},{2,4},{4,2},{3,5},{5,3},{6,8},{8,6},{7... | collective-permute-start | bytes 276488 | tf_op jit(solution)/shard_map/ppermute | solution.py:397

commit v4 on v3

--- a/solution.py
+++ b/solution.py
@@ -56,39 +56,78 @@
         body(pl.ds(start, LANES))
 
 
-def taylor_buffer(x_ref, first_ref, y_ref, m_ref, wk, weights_at, out_ref):
-    elements = x_ref.shape[-1]
-    basis_products(wk, x_ref, y_ref, 3)
-
-    def first(lanes):
-        acc = star_sum(y_ref, [m_ref], lanes, [jnp.zeros((R, LANES), F32)] * NQ)
-        for p in range(NQ):
-            first_ref[p, :, lanes] = acc[p]
-
-    each_half(elements, first)
-    basis_products(wk, first_ref, y_ref, 3)
-
-    def second(lanes):
-        acc = star_sum(y_ref, [m_ref], lanes, [jnp.zeros((R, LANES), F32)] * NQ)
-        w1, w2 = weights_at(lanes)
-        for p in range(NQ):
-            out_ref[p, :, lanes] = x_ref[p, :, lanes] + (w1 * first_ref[p, :, lanes] + w2 * acc[p])
-
-    each_half(elements, second)
-
-
-def send_blocks(b_ref, send, near_ref, far_ref):
+def in_turns(one, two, stages):
+    for now, before in zip(stages + [0], [0] + stages):
+        done = 0
+        for step in range(now):
+            next(one, None)
+            while done * now < (step + 1) * before:
+                next(two, None)
+                done += 1
+        while done < before:
+            next(two, None)
+            done += 1
+    next(one, None)
+    next(two, None)
+
+
+def star_steps(acc, ys, m_ref, lanes):
+    for q in range(NQ):
+        for k in range(m_ref.shape[1]):
+            y = ys.pop((k, q))
+            for p in range(NQ):
+                acc[p] = acc[p] + y * m_ref[q * NQ + p, k : k + 1, lanes]
+            yield
+
+
+def far_steps(ys, both, index, face, w_ref):
+    size = NQ * R
+    gathered = both
+    for f in range(4):
+        yield
+    for q in range(NQ):
+        for f in range(4):
+            kind = jnp.broadcast_to(face[f : f + 1], (R, LANES))
+            w = w_ref[W_FAR + 4 * f * R : W_FAR + 4 * (f + 1) * R]
+            high_rows = gathered[f][q * R : (q + 1) * R]
+            low_rows = gathered[f][size + q * R : size + (q + 1) * R]
+            out = dot(w, jnp.concatenate([high_rows, low_rows, high_rows], axis=0).astype(BF16))
+            ys[f, q] = jnp.where(
+                kind < 2,
+                jnp.where(kind == 0, out[:R], out[R : 2 * R]),
+                jnp.where(kind == 2, out[2 * R : 3 * R], out[3 * R :]),
+            )
+            yield
+
+
+def derivative_steps(x, following, wk, m_ref, lanes):
+    ys = {}
+    for q in range(NQ):
+        out = dot(wk, stack_values(x[q]))
+        for k in range(3):
+            ys[k, q] = out[k * R : (k + 1) * R]
+        yield
+    yield from star_steps(following, ys, m_ref, lanes)
+
+
+def taylor_steps(x, wk, m_ref, lanes, w1, w2, out_ref):
+    first = [jnp.zeros((R, LANES), F32)] * NQ
+    yield from derivative_steps(x, first, wk, m_ref, lanes)
+    second = [jnp.zeros((R, LANES), F32)] * NQ
+    yield from derivative_steps(first, second, wk, m_ref, lanes)
+    for p in range(NQ):
+        out_ref[p, :, lanes] = x[p] + (w1 * first[p] + w2 * second[p])
+
+
+def pick_columns(b_ref, send, out_ref):
     elements = b_ref.shape[-1]
-    columns = send.shape[-1]
-    b = b_ref[...].reshape(NQ * R, elements)
-    high = b.astype(BF16)
-    low = (b - high.astype(F32)).astype(BF16)
-    rows = lax.broadcasted_iota(jnp.int32, (elements, columns), 0).astype(F32)
+    both = split_rows(b_ref[...].reshape(NQ * R, elements))
+    rows = lax.broadcasted_iota(jnp.int32, (elements, send.shape[-1]), 0).astype(F32)
     hot = jnp.where(rows == send, 1.0, 0.0).astype(BF16)
-    out = dot(high, hot) + dot(low, hot)
-    for q in range(NQ):
-        near_ref[q * NB : (q + 1) * NB] = out[q * R : q * R + NB, : columns // 2]
-        far_ref[q * NB : (q + 1) * NB] = out[q * R : q * R + NB, columns // 2 :]
+    out = dot(both, hot)
+    out = out[: NQ * R] + out[NQ * R :]
+    for q in range(NQ):
+        out_ref[q * NB : (q + 1) * NB] = out[q * R : q * R + NB]
 
 
 def far_sides(source, index, face, w_ref, y_ref, base):
@@ -179,20 +218,26 @@
 ROWS = 40
 
 
-def predict_kernel(
-    dof_ref, star_ref, kstiff_ref, send_ref, twice_ref, once_ref,
-    b_ref, near_ref, far_ref, m_ref, wk_ref, send_out,
-    w_ref, x_ref, first_ref, y_ref,
-):
+def setup_kernel(kstiff_ref, send_ref, twice_ref, once_ref, wk_ref, send_out, w_ref):
     fill_stiffness(w_ref, kstiff_ref)
     wk_ref[...] = place_weights(w_ref[...], twice_ref, once_ref)
-    x_ref[:, NB:, :] = jnp.zeros((NQ, R - NB, x_ref.shape[-1]), F32)
-    x_ref[:, :NB, :] = dof_ref[...]
+    send_out[...] = send_columns(send_ref.at[0])
+
+
+def far_kernel(b_ref, send_ref, out_ref):
+    pick_columns(b_ref, send_ref[:, send_ref.shape[-1] // 2 :], out_ref)
+
+
+def predict_kernel(dof_ref, star_ref, wk_ref, send_ref, b_ref, near_ref, m_ref):
     widen(star_ref, m_ref)
-    taylor_buffer(x_ref, first_ref, y_ref, m_ref, wk_ref[...], lambda lanes: (0.5, 1.0 / 6.0), b_ref)
-    send = send_columns(send_ref.at[0])
-    send_out[...] = send
-    send_blocks(b_ref, send, near_ref, far_ref)
+    wk = wk_ref[...]
+
+    def half(lanes):
+        x = [padded(dof_ref, p, lanes) for p in range(NQ)]
+        yield from taylor_steps(x, wk, m_ref, lanes, 0.5, 1.0 / 6.0, b_ref)
+
+    in_turns(half(pl.ds(0, LANES)), half(pl.ds(LANES, LANES)), [NQ, 3 * NQ] * 2)
+    pick_columns(b_ref, send_ref[:, : send_ref.shape[-1] // 2], near_ref)
 
 
 NEIGHBOUR, FACE, CLUSTER, DAMAGE, COHESION, YIELD = 0, 4, 8, 9, 10, 16
@@ -279,74 +324,102 @@
     return jnp.concatenate([piece for q in range(NQ) for piece in (both[q * NB : (q + 1) * NB], pad)], axis=0)
 
 
-def ghost_part(near_ref, even_ref, odd_ref, w_ref, table_ref, y_ref):
-    elements = table_ref.shape[-1]
-    ghosts = near_ref.shape[-1] // 2
-    index = table_ref[NEIGHBOUR : NEIGHBOUR + 4] - elements
+def gather_all(both, index):
+    rows = lax.broadcasted_iota(jnp.int32, (both.shape[1], index.shape[1]), 0).astype(F32)
+    gathered = []
+    for f in range(4):
+        hot = jnp.where(rows == index[f : f + 1], 1.0, 0.0).astype(BF16)
+        gathered.append(dot(both, hot))
+    return gathered
+
+
+def ghost_index(table_ref, ghosts):
+    index = table_ref[NEIGHBOUR : NEIGHBOUR + 4] - table_ref.shape[-1]
     last = jnp.where(index >= 3 * ghosts, index - ghosts, index + ghosts)
-    index = jnp.where(index >= 2 * ghosts, last, index)
-    source = ghost_source(near_ref, even_ref, odd_ref)
-    far_sides(source, index, table_ref[FACE : FACE + 4], w_ref, y_ref, 0)
+    return jnp.where(index >= 2 * ghosts, last, index)
+
+
+def split_rows(source):
+    high = source.astype(BF16)
+    return jnp.concatenate([high, (source - high.astype(F32)).astype(BF16)], axis=0)
 
 
 def second_kernel(
     v_ref, dof_ref, near_ref, even_ref, odd_ref, wk_ref, send_ref, w_ref, table_ref, ms_ref, mn_ref,
-    state_ref, b_ref, near_out, far_out,
-    x_ref, first_ref, y_ref,
+    state_ref, b_ref, near_out,
 ):
-    elements = v_ref.shape[-1]
-    ghost_part(near_ref, even_ref, odd_ref, w_ref, table_ref, y_ref)
-
-    def body(lanes):
-        acc = star_sum(y_ref, [mn_ref], lanes, [v_ref[p, :, lanes] for p in range(NQ)])
+    both = split_rows(ghost_source(near_ref, even_ref, odd_ref))
+    index = ghost_index(table_ref, near_ref.shape[-1] // 2)
+    both = gather_all(both, index)
+    wk = wk_ref[...]
+
+    def half(at):
+        lanes = pl.ds(at, LANES)
+        ys = {}
+        yield from far_steps(ys, [one[:, at : at + LANES] for one in both], index[:, at : at + LANES], table_ref[FACE : FACE + 4, lanes], w_ref)
+        acc = [v_ref[p, :, lanes] for p in range(NQ)]
+        yield from star_steps(acc, ys, mn_ref, lanes)
         fine = table_ref[CLUSTER : CLUSTER + 1, lanes] < 0.5
+        x = []
         for p in range(NQ):
             state_ref[p, :, lanes] = acc[p]
-            x_ref[p, :, lanes] = jnp.where(fine, acc[p], padded(dof_ref, p, lanes))
-
-    each_half(elements, body)
-
-    def weights_at(lanes):
-        fine = table_ref[CLUSTER : CLUSTER + 1, lanes] < 0.5
-        return jnp.where(fine, 0.5, 1.5), jnp.where(fine, 1.0 / 6.0, 7.0 / 6.0)
-
-    taylor_buffer(x_ref, first_ref, y_ref, ms_ref, wk_ref[...], weights_at, b_ref)
-    send_blocks(b_ref, send_ref[...], near_out, far_out)
+            x.append(jnp.where(fine, acc[p], padded(dof_ref, p, lanes)))
+        w1, w2 = jnp.where(fine, 0.5, 1.5), jnp.where(fine, 1.0 / 6.0, 7.0 / 6.0)
+        yield from taylor_steps(x, wk, ms_ref, lanes, w1, w2, b_ref)
+
+    in_turns(half(0), half(LANES), [4 + 4 * NQ, 4 * NQ] + [NQ, 3 * NQ] * 2)
+    pick_columns(b_ref, send_ref[:, : send_ref.shape[-1] // 2], near_out)
 
 
 def last_kernel(
     v_ref, near_ref, even_ref, odd_ref, w_ref, table_ref, mn_ref, mask_ref,
     result_ref,
-    x_ref, y_ref, out_ref, sems,
+    out_ref, sems,
 ):
-    writes = [pltpu.make_async_copy(out_ref.at[q], result_ref.at[q], sems.at[q]) for q in range(NQ)]
-    elements = v_ref.shape[-1]
-    ghost_part(near_ref, even_ref, odd_ref, w_ref, table_ref, y_ref)
-
-    def body(lanes):
-        acc = star_sum(y_ref, [mn_ref], lanes, [v_ref[p, :, lanes] for p in range(NQ)])
-        for p in range(NQ):
-            x_ref[p, :, lanes] = acc[p]
-
-    each_half(elements, body)
-
-    for q in range(6, NQ):
-        out_ref[q] = x_ref[q, :NB, :]
-        writes[q].start()
-    points = [dot(w_ref[W_POINTS : W_POINTS + R], stack_values(x_ref[q])) for q in range(6)]
-    pressure = (points[0] + points[1] + points[2]) / 3.0
-    normal = [points[q] - pressure for q in range(3)]
-    normal_sum = normal[0] * normal[0] + normal[1] * normal[1] + normal[2] * normal[2]
-    shear_sum = points[3] * points[3] + points[4] * points[4] + points[5] * points[5]
-    tau = jnp.sqrt(0.5 * normal_sum + shear_sum)
-    strength = table_ref[COHESION : COHESION + 1]
-    limit = jnp.maximum(strength - FRICTION * pressure, 0.5 * strength)
-    rate = jnp.where(mask_ref[...] > 0.5, RELAXATION * (limit / jnp.maximum(tau, limit) - 1.0), 0.0)
-    deviation = normal + points[3:]
-    for q in range(6):
-        change = dot(w_ref[W_POINTS + R : W_ROWS], stack_values(rate * deviation[q]))
-        out_ref[q] = (x_ref[q] + change)[:NB]
-        writes[q].start()
+    both = split_rows(ghost_source(near_ref, even_ref, odd_ref))
+    index = ghost_index(table_ref, near_ref.shape[-1] // 2)
+    both = gather_all(both, index)
+    writes = []
+
+    def send_out(quantities, lanes):
+        write = pltpu.make_async_copy(
+            out_ref.at[quantities, :, lanes], result_ref.at[quantities, :, lanes], sems.at[len(writes)]
+        )
+        write.start()
+        writes.append(write)
+
+    def half(at):
+        lanes = pl.ds(at, LANES)
+        ys = {}
+        yield from far_steps(ys, [one[:, at : at + LANES] for one in both], index[:, at : at + LANES], table_ref[FACE : FACE + 4, lanes], w_ref)
+        state = [v_ref[p, :, lanes] for p in range(NQ)]
+        yield from star_steps(state, ys, mn_ref, lanes)
+        for q in range(6, NQ):
+            out_ref[q, :, lanes] = state[q][:NB]
+        send_out(pl.ds(6, 3), lanes)
+        points = []
+        for q in range(6):
+            points.append(dot(w_ref[W_POINTS : W_POINTS + R], stack_values(state[q])))
+            yield
+        pressure = (points[0] + points[1] + points[2]) / 3.0
+        normal = [points[q] - pressure for q in range(3)]
+        normal_sum = normal[0] * normal[0] + normal[1] * normal[1] + normal[2] * normal[2]
+        shear_sum = points[3] * points[3] + points[4] * points[4] + points[5] * points[5]
+        tau = jnp.sqrt(0.5 * normal_sum + shear_sum)
+        strength = table_ref[COHESION : COHESION + 1, lanes]
+        limit = jnp.maximum(strength - FRICTION * pressure, 0.5 * strength)
+        yield
+        rate = RELAXATION * (limit / jnp.maximum(tau, limit) - 1.0)
+        rate = jnp.where(mask_ref[:, lanes] > 0.5, rate, 0.0)
+        yield
+        deviation = normal + points[3:]
+        for q in range(6):
+            change = dot(w_ref[W_POINTS + R : W_ROWS], stack_values(rate * deviation[q]))
+            out_ref[q, :, lanes] = (state[q] + change)[:NB]
+            yield
+        send_out(pl.ds(0, 6), lanes)
+
+    in_turns(half(0), half(LANES), [4 + 4 * NQ, 4 * NQ, 14])
     for write in writes:
         write.wait()
 
@@ -387,15 +460,16 @@
     return route
 
 
-def exchange(near, far, me, total, beside):
+def exchange(near, buffer, send, me, total):
     got = lax.ppermute(near, "dom", core_swap(total))
+    far = call(far_kernel, [buffer, send], spec(near.shape), [], cost=500_000_000)
     left = lax.broadcasted_iota(jnp.int32, got.shape, 1) < got.shape[1] // 2
     forward = left == ((me // 2) % 2 == 0)
     to_even, to_odd = jnp.where(forward, got, far), jnp.where(forward, far, got)
-    beside, to_even, to_odd = lax.optimization_barrier((beside, to_even, to_odd))
+    buffer, to_even, to_odd = lax.optimization_barrier((buffer, to_even, to_odd))
     even = lax.ppermute(to_even, "dom", even_chip_swap(total))
     odd = lax.ppermute(to_odd, "dom", odd_chip_swap(total))
-    return got, even, odd, beside
+    return got, even, odd, buffer
 
 
 def per_device(
@@ -424,7 +498,6 @@
 
     field = spec((NQ, R, elements))
     block = spec((NQ * NB, 2 * ghosts))
-    x_s = (field.shape, F32)
 
     def y_s(blocks):
         return ((blocks, NQ, R, elements), F32)
@@ -440,13 +513,14 @@
 
     place = spec((LANES, K3), BF16)
     twice, once = call(place_kernel, [], (place, place), [], cost=4_000_000_000)
-    buffer_one, near, far, ms, wk, send = call(
-        predict_kernel,
-        [dof_values, star, kstiff, send_list, twice, once],
-        (field, block, block, m_o(3), spec((3 * R, K3), BF16), spec((1, 4 * ghosts))),
-        [((3 * R, LANES), F32), x_s, x_s, y_s(3)],
-    )
-    near, even, odd, buffer_one = exchange(near, far, me, total, buffer_one)
+    wk, send = call(
+        setup_kernel,
+        [kstiff, send_list, twice, once],
+        (spec((3 * R, K3), BF16), spec((1, 4 * ghosts))),
+        [((3 * R, LANES), F32)],
+    )
+    buffer_one, near, ms = call(predict_kernel, [dof_values, star, wk, send], (field, block, m_o(3)), [])
+    near, even, odd, buffer_one = exchange(near, buffer_one, send, me, total)
     started, ml, mn, mask, table, weights = call(
         local_kernel,
         [
@@ -458,13 +532,13 @@
         [((W_ROWS, LANES), F32), y_s(11)],
         cost=1_000_000_000,
     )
-    updated, buffer_two, near, far = call(
+    updated, buffer_two, near = call(
         second_kernel,
         [started, dof_values, near, even, odd, wk, send, weights, table, ms, mn],
-        (field, field, block, block),
-        [x_s, x_s, y_s(4)],
-    )
-    near, even, odd, buffer_two = exchange(near, far, me, total, buffer_two)
+        (field, field, block),
+        [],
+    )
+    near, even, odd, buffer_two = exchange(near, buffer_two, send, me, total)
     started = call(
         again_kernel,
         [updated, buffer_two, weights, table, ms, ml, mn],
@@ -476,7 +550,7 @@
         last_kernel,
         [started, near, even, odd, weights, table, mn, mask],
         spec(dof_values.shape),
-        [x_s, y_s(4), (dof_values.shape, F32), pltpu.SemaphoreType.DMA((NQ,))],
+        [(dof_values.shape, F32), pltpu.SemaphoreType.DMA((4,))],
         out_space=HBM,
     )
 

time: 30.5 us -> 29.8 us (0.977)
  waiting for transfers between devices: 4.66 us -> 4.09 us
    ppermute x2, waiting for transfers between devices: 1.87 us -> 1.29 us  [exchange(): got = lax.ppermute(near, 'dom', core_swap(total))]
    pallas_call x6 -> x9, Pallas kernels: 13.8 us -> 13.8 us  [call(): pl.pallas_call(kernel, out_shape=outputs, in_specs=[VMEM] * len(inputs),...]
  transfers between devices with their start and end apart: 6 -> 6, of which waited for: 4 -> 4; matrix products, arithmetic and copies ran while one was open for 0% -> 0% of each run, Pallas kernels for 22% -> 24%
where the time goes in v4:
time: 29.8 us; the launch traced here: 29.6 us
  Pallas kernels  13.8 us (46%)
  starting transfers between devices  9.08 us (30%)
  waiting for transfers between devices  4.09 us (14%)
  local copies, waits for them, and re-layouts  1.48 us (5%)
  between operations  1.16 us (4%)
    pallas_call x9, Pallas kernels, call(): pl.pallas_call(kernel, out_shape=outputs, in_specs=[VMEM] * len(inputs),...  13.8 us
    ppermute x2, starting transfers between devices, exchange(): odd = lax.ppermute(to_odd, 'dom', odd_chip_swap(total))  6.4 us
    ppermute x2, waiting for transfers between devices, exchange(): odd = lax.ppermute(to_odd, 'dom', odd_chip_swap(total))  2.79 us
    ppermute x2, starting transfers between devices, exchange(): even = lax.ppermute(to_even, 'dom', even_chip_swap(total))  2.54 us
    unnamed x32, local copies, waits for them, and re-layouts  1.48 us
    ppermute x2, waiting for transfers between devices, exchange(): got = lax.ppermute(near, 'dom', core_swap(total))  1.29 us
  transfers between devices with their start and end apart: 6, of which 4 were waited for; matrix products, arithmetic and copies ran while one was open for 0% of the time, Pallas kernels for 24%

profile of v4, /device:TPU:24, one launch (start us, length us, event | category | flops | bytes accessed | tf_op | source)
XLA Modules:
  0.0 29.6 jit_solution(17279066835190538685)
XLA Ops:
  0.1 0.7 %copy-done.2 = f32[3,20,20]{2,1,0:T(8,128)S(1)} copy-done((f32[3,20,20]{2,1,0:T(8,128)S(1)}, f32[3,20,20]{2,1,0:T(8,128)}, u32[]{:S(2)}) %copy-start.2) | copy-done | bytes 4824
  0.8 0.0 copy-done.3
  0.8 0.2 shard_map.164
  1.0 0.0 copy-done
  1.0 0.1 copy-done.1
  1.1 1.4 %shard_map.165 = (f32[9,24,256]{2,1,0:T(8,128)S(1)}, f32[180,128]{1,0:T(8,128)S(1)}, f32[81,3,256]{2,1,0:T(4,128)S(1)}) custom-call(f32[9,20,256]{2,1,0:T(8,128)S(1)} %copy-done, bf16[9,9,3,256]{3,2,1,0:T(4,128)(2,1)S(1)} %bitcast.9, bf16[72,72]{1,0:T(8,128)(2,1)S(1)} %get-tuple-element.29.wk_ref, f32[1,256]{1,0:T(1,128)S(1)} %get-tuple-element.30.send_ref), custom_call_target="tpu_custom_call" | custom-call | bytes 1048576 | tf_op jit(solution)/shard_map/pallas_call | solution.py:436
  2.5 0.1 collective-permute-start
  3.2 0.0 copy-start.6
  3.3 0.2 shard_map.166
  3.6 0.2 collective-permute-done.near_ref
  3.9 1.6 %collective-permute-start.1 = (f32[180,128]{1,0:T(8,128)S(1)}, f32[180,128]{1,0:T(8,128)S(1)}, u32[]{:S(2)}, u32[]{:S(2)}) collective-permute-start(f32[180,128]{1,0:T(8,128)S(1)} %get-tuple-element.36), channel_id=1, source_target_pairs={{0,2},{1,3},{2,0},{3,1},{4,6},{5,7},{6,4},{7,5},{8,10},{9,11},{10,... | collective-permute-start | bytes 276488 | tf_op jit(solution)/shard_map/ppermute | solution.py:470
  5.4 3.3 %collective-permute-start.2 = (f32[180,128]{1,0:T(8,128)S(1)}, f32[180,128]{1,0:T(8,128)S(1)}, u32[]{:S(2)}, u32[]{:S(2)}) collective-permute-start(f32[180,128]{1,0:T(8,128)S(1)} %get-tuple-element.37), channel_id=1, source_target_pairs={{0,0},{1,1},{30,30},{31,31},{2,4},{4,2},{3,5},{5,3},{6,8},{8,6},{7... | collective-permute-start | bytes 276488 | tf_op jit(solution)/shard_map/ppermute | solution.py:471
  8.8 0.6 %copy-done.13 = s32[256]{0:T(256)S(1)} copy-done((s32[256]{0:T(256)S(1)}, s32[256]{0:T(256)}, u32[]{:S(2)}) %copy-start.13) | copy-done | bytes 1048
  9.4 3.6 %shard_map.167 = (f32[9,24,256]{2,1,0:T(8,128)S(1)}, f32[81,4,256]{2,1,0:T(4,128)S(1)}, f32[81,4,256]{2,1,0:T(4,128)S(1)}, f32[24,256]{1,0:T(8,128)S(1)}, f32[40...) custom-call(f32[9,20,256]{2,1,0:T(8,128)S(1)} %copy-done, f32[9,24,256]{2,1,0:T(8,128)S(1)} %get-tuple-element.33.b_ref, ...), custom_call_target="tpu_custom_call" | custom-call | flops 1000000000 | bytes 1048576 | tf_op jit(solution)/shard_map/pallas_call | solution.py:436
  13.0 0.7 %collective-permute-done.2.odd_ref = f32[180,128]{1,0:T(8,128)S(1)} collective-permute-done((f32[180,128]{1,0:T(8,128)S(1)}, f32[180,128]{1,0:T(8,128)S(1)}, u32[]{:S(2)}, u32[]{:S(2)}) %collective-permute-start.2) | collective-permute-done | bytes 92192 | tf_op jit(solution)/shard_map/ppermute | solution.py:471
  13.7 2.7 %shard_map.168 = (f32[9,24,256]{2,1,0:T(8,128)S(1)}, f32[9,24,256]{2,1,0:T(8,128)S(1)}, f32[180,128]{1,0:T(8,128)S(1)}) custom-call(f32[9,24,256]{2,1,0:T(8,128)S(1)} %get-tuple-element.35.v_ref, f32[9,20,256]{2,1,0:T(8,128)S(1)} %copy-done, f32[180,128]{1,0:T(8,128)S(1)} %collective-permute-done.near_ref, f32[180,128]{1,0:T(8,128)S(1)} %collective-permute-done.1.even_ref, ...), custom_call_target="tpu_custom_call" | custom-call | bytes 1048576 | tf_op jit(solution)/shard_map/pallas_call | solution.py:436
  16.4 0.1 collective-permute-start.3
  16.5 0.2 shard_map.169
  16.7 1.1 %collective-permute-done.3.near_ref = f32[180,128]{1,0:T(8,128)S(1)} collective-permute-done((f32[180,128]{1,0:T(8,128)S(1)}, f32[180,128]{1,0:T(8,128)S(1)}, u32[]{:S(2)}, u32[]{:S(2)}) %collective-permute-start.3) | collective-permute-done | bytes 92192 | tf_op jit(solution)/shard_map/ppermute | solution.py:464
  17.8 1.0 %collective-permute-start.4 = (f32[180,128]{1,0:T(8,128)S(1)}, f32[180,128]{1,0:T(8,128)S(1)}, u32[]{:S(2)}, u32[]{:S(2)}) collective-permute-start(f32[180,128]{1,0:T(8,128)S(1)} %get-tuple-element.46), channel_id=1, source_target_pairs={{0,2},{1,3},{2,0},{3,1},{4,6},{5,7},{6,4},{7,5},{8,10},{9,11},{10,... | collective-permute-start | bytes 276488 | tf_op jit(solution)/shard_map/ppermute | solution.py:470
  18.8 3.1 %collective-permute-start.5 = (f32[180,128]{1,0:T(8,128)S(1)}, f32[180,128]{1,0:T(8,128)S(1)}, u32[]{:S(2)}, u32[]{:S(2)}) collective-permute-start(f32[180,128]{1,0:T(8,128)S(1)} %get-tuple-element.47), channel_id=1, source_target_pairs={{0,0},{1,1},{30,30},{31,31},{2,4},{4,2},{3,5},{5,3},{6,8},{8,6},{7... | collective-permute-start | bytes 276488 | tf_op jit(solution)/shard_map/ppermute | solution.py:471
  21.9 3.0 %shard_map.170.v_ref = f32[9,24,256]{2,1,0:T(8,128)S(1)} custom-call(f32[9,24,256]{2,1,0:T(8,128)S(1)} %get-tuple-element.41.base_ref, f32[9,24,256]{2,1,0:T(8,128)S(1)} %get-tuple-element.44.b_ref, bf16[600,72]{1,0:T(8,128)(2,1)S(1)} %get-tuple-element.38.w_ref, f32[40,256]{1,0:T(8,128)S(1)} %get-tuple-element.39.table_ref, ...), custom_call_target="tpu_custom_call" | custom-call | flops 1000000000 | bytes 1048576 | tf_op jit(solution)/shard_map/pallas_call | solution.py:436
  24.9 2.1 %collective-permute-done.5.odd_ref = f32[180,128]{1,0:T(8,128)S(1)} collective-permute-done((f32[180,128]{1,0:T(8,128)S(1)}, f32[180,128]{1,0:T(8,128)S(1)}, u32[]{:S(2)}, u32[]{:S(2)}) %collective-permute-start.5) | collective-permute-done | bytes 92192 | tf_op jit(solution)/shard_map/ppermute | solution.py:471
  27.0 2.4 %shard_map.171 = f32[9,20,256]{2,1,0:T(8,128)} custom-call(f32[9,24,256]{2,1,0:T(8,128)S(1)} %shard_map.170.v_ref, f32[180,128]{1,0:T(8,128)S(1)} %collective-permute-done.3.near_ref, f32[180,128]{1,0:T(8,128)S(1)} %collective-permute-done.4.even_ref, f32[180,128]{1,0:T(8,128)S(1)} %collective-permute-done.5.odd_ref, ...), custom_call_target="tpu_custom_call" | custom-call | bytes 1048576 | tf_op jit(solution)/shard_map/pallas_call | solution.py:436
  (32 shorter events, 0.1 us)
Async XLA Ops:
  0.0 0.8 %copy-start.2 = (f32[3,20,20]{2,1,0:T(8,128)S(1)}, f32[3,20,20]{2,1,0:T(8,128)}, u32[]{:S(2)}) copy-start(f32[3,20,20]{2,1,0:T(8,128)} %kstiff_ref.3) | copy-start | bytes 14404
  0.0 1.0 %copy-start = (f32[9,20,256]{2,1,0:T(8,128)S(1)}, f32[9,20,256]{2,1,0:T(8,128)}, u32[]{:S(2)}) copy-start(f32[9,20,256]{2,1,0:T(8,128)} %dof_ref.5) | copy-start | bytes 552964
  0.0 1.1 %copy-start.1 = (bf16[3,9,9,256]{3,0,2,1:T(4,128)(2,1)S(1)}, bf16[3,9,9,256]{3,0,2,1:T(4,128)(2,1)}, u32[]{:S(2)}) copy-start(bf16[3,9,9,256]{3,0,2,1:T(4,128)(2,1)} %param.18) | copy-start | bytes 373252
  0.0 0.7 %copy-start.3 = (s32[1,4,64]{2,1,0:T(4,128)S(1)}, s32[1,4,64]{2,1,0:T(4,128)}, u32[]{:S(2)}) copy-start(s32[1,4,64]{2,1,0:T(4,128)} %send_ref.1) | copy-start | bytes 3076
  2.5 1.4 %collective-permute-start = (f32[180,128]{1,0:T(8,128)S(1)}, f32[180,128]{1,0:T(8,128)S(1)}, u32[]{:S(2)}, u32[]{:S(2)}) collective-permute-start(f32[180,128]{1,0:T(8,128)S(1)} %get-tuple-element.32), channel_id=1, source_target_pairs={{0,1},{1,0},{2,3},{3,2},{4,5},{5,4},{6,7},{7,6},{8,9},{9,8},{10,11... | collective-permute-start | bytes 276488 | tf_op jit(solution)/shard_map/ppermute | solution.py:464
  3.2 5.5 %copy-start.6 = (f32[4,4,20,20]{3,1,2,0:T(4,128)S(1)}, f32[4,4,20,20]{3,1,2,0:T(4,128)}, u32[]{:S(2)}) copy-start(f32[4,4,20,20]{3,1,2,0:T(4,128)} %param.23) | copy-start | bytes 76804
  3.3 5.5 %copy-start.9 = (f32[20,20]{1,0:T(8,128)S(1)}, f32[20,20]{1,0:T(8,128)}, u32[]{:S(2)}) copy-start(f32[20,20]{1,0:T(8,128)} %to_ref.1) | copy-start | bytes 4804
  3.3 5.5 %copy-start.10 = (f32[20,20]{1,0:T(8,128)S(1)}, f32[20,20]{1,0:T(8,128)}, u32[]{:S(2)}) copy-start(f32[20,20]{1,0:T(8,128)} %from_ref.1) | copy-start | bytes 4804
  3.3 5.5 %copy-start.11 = (s32[4,256]{1,0:T(4,128)S(1)}, s32[4,256]{1,0:T(4,128)}, u32[]{:S(2)}) copy-start(s32[4,256]{1,0:T(4,128)} %index_ref.1) | copy-start | bytes 12292
  3.3 5.5 %copy-start.12 = (s32[4,256]{1,0:T(4,128)S(1)}, s32[4,256]{1,0:T(4,128)}, u32[]{:S(2)}) copy-start(s32[4,256]{1,0:T(4,128)} %face_ref.1) | copy-start | bytes 12292
  3.3 5.5 %copy-start.14 = (s32[1,256]{1,0:T(1,128)S(1)}, s32[1,256]{1,0:T(1,128)}, u32[]{:S(2)}) copy-start(s32[1,256]{1,0:T(1,128)} %damage_ref.1) | copy-start | bytes 3076
  3.3 5.5 %copy-start.15 = (f32[256]{0:T(256)S(1)}, f32[256]{0:T(256)}, u32[]{:S(2)}) copy-start(f32[256]{0:T(256)} %param.31) | copy-start | bytes 3076
  3.6 5.2 %copy-start.8 = (s32[20,256]{1,0:T(8,128)S(1)}, s32[20,256]{1,0:T(8,128)}, u32[]{:S(2)}) copy-start(s32[20,256]{1,0:T(8,128)} %yield_ref.1) | copy-start | bytes 61444
  3.6 5.2 %copy-start.4 = (bf16[4,9,9,256]{3,0,2,1:T(4,128)(2,1)S(1)}, bf16[4,9,9,256]{3,0,2,1:T(4,128)(2,1)}, u32[]{:S(2)}) copy-start(bf16[4,9,9,256]{3,0,2,1:T(4,128)(2,1)} %param.19) | copy-start | bytes 497668
  3.6 5.2 %copy-start.5 = (bf16[4,9,9,256]{3,0,2,1:T(4,128)(2,1)S(1)}, bf16[4,9,9,256]{3,0,2,1:T(4,128)(2,1)}, u32[]{:S(2)}) copy-start(bf16[4,9,9,256]{3,0,2,1:T(4,128)(2,1)} %param.20) | copy-start | bytes 497668
  3.6 5.2 %copy-start.7 = (f32[4,20,20]{2,0,1:T(4,128)S(1)}, f32[4,20,20]{2,0,1:T(4,128)}, u32[]{:S(2)}) copy-start(f32[4,20,20]{2,0,1:T(4,128)} %param.22) | copy-start | bytes 19204
  3.9 9.1 %collective-permute-start.1 = (f32[180,128]{1,0:T(8,128)S(1)}, f32[180,128]{1,0:T(8,128)S(1)}, u32[]{:S(2)}, u32[]{:S(2)}) collective-permute-start(f32[180,128]{1,0:T(8,128)S(1)} %get-tuple-element.36), channel_id=1, source_target_pairs={{0,2},{1,3},{2,0},{3,1},{4,6},{5,7},{6,4},{7,5},{8,10},{9,11},{10,... | collective-permute-start | bytes 276488 | tf_op jit(solution)/shard_map/ppermute | solution.py:470
  5.4 8.3 %collective-permute-start.2 = (f32[180,128]{1,0:T(8,128)S(1)}, f32[180,128]{1,0:T(8,128)S(1)}, u32[]{:S(2)}, u32[]{:S(2)}) collective-permute-start(f32[180,128]{1,0:T(8,128)S(1)} %get-tuple-element.37), channel_id=1, source_target_pairs={{0,0},{1,1},{30,30},{31,31},{2,4},{4,2},{3,5},{5,3},{6,8},{8,6},{7... | collective-permute-start | bytes 276488 | tf_op jit(solution)/shard_map/ppermute | solution.py:471
  8.7 0.7 %copy-start.13 = (s32[256]{0:T(256)S(1)}, s32[256]{0:T(256)}, u32[]{:S(2)}) copy-start(s32[256]{0:T(256)} %param.26) | copy-start | bytes 3076
  16.4 1.4 %collective-permute-start.3 = (f32[180,128]{1,0:T(8,128)S(1)}, f32[180,128]{1,0:T(8,128)S(1)}, u32[]{:S(2)}, u32[]{:S(2)}) collective-permute-start(f32[180,128]{1,0:T(8,128)S(1)} %get-tuple-element.43), channel_id=1, source_target_pairs={{0,1},{1,0},{2,3},{3,2},{4,5},{5,4},{6,7},{7,6},{8,9},{9,8},{10,11... | collective-permute-start | bytes 276488 | tf_op jit(solution)/shard_map/ppermute | solution.py:464
  17.8 7.1 %collective-permute-start.4 = (f32[180,128]{1,0:T(8,128)S(1)}, f32[180,128]{1,0:T(8,128)S(1)}, u32[]{:S(2)}, u32[]{:S(2)}) collective-permute-start(f32[180,128]{1,0:T(8,128)S(1)} %get-tuple-element.46), channel_id=1, source_target_pairs={{0,2},{1,3},{2,0},{3,1},{4,6},{5,7},{6,4},{7,5},{8,10},{9,11},{10,... | collective-permute-start | bytes 276488 | tf_op jit(solution)/shard_map/ppermute | solution.py:470
  18.8 8.3 %collective-permute-start.5 = (f32[180,128]{1,0:T(8,128)S(1)}, f32[180,128]{1,0:T(8,128)S(1)}, u32[]{:S(2)}, u32[]{:S(2)}) collective-permute-start(f32[180,128]{1,0:T(8,128)S(1)} %get-tuple-element.47), channel_id=1, source_target_pairs={{0,0},{1,1},{30,30},{31,31},{2,4},{4,2},{3,5},{5,3},{6,8},{8,6},{7... | collective-permute-start | bytes 276488 | tf_op jit(solution)/shard_map/ppermute | solution.py:471

commit v5 on v4

--- a/solution.py
+++ b/solution.py
@@ -57,18 +57,20 @@
 
 
 def in_turns(one, two, stages):
-    for now, before in zip(stages + [0], [0] + stages):
-        done = 0
-        for step in range(now):
-            next(one, None)
-            while done * now < (step + 1) * before:
-                next(two, None)
-                done += 1
-        while done < before:
-            next(two, None)
-            done += 1
+    for now, before in zip(stages + [[]], [[]] + stages):
+        order = []
+        for steps, weights in ((one, now), (two, before)):
+            done = 0
+            for weight in weights:
+                order.append((done / sum(weights), steps))
+                done += weight
+        for _, steps in sorted(order, key=lambda entry: entry[0]):
+            next(steps, None)
     next(one, None)
     next(two, None)
+
+
+FAR = [0.01] * 4 + [1] * 4 * NQ
 
 
 def star_steps(acc, ys, m_ref, lanes):
@@ -214,18 +216,20 @@
     return jnp.where(slot < 2, first, second)
 
 
-NEIGHBOUR, FACE, CLUSTER, DAMAGE, COUNT, COHESION, SEND, YIELD = 0, 4, 8, 9, 10, 11, 12, 16
-ROWS = 40
-
-
 def setup_kernel(kstiff_ref, send_ref, twice_ref, once_ref, wk_ref, send_out, w_ref):
     fill_stiffness(w_ref, kstiff_ref)
     wk_ref[...] = place_weights(w_ref[...], twice_ref, once_ref)
     send_out[...] = send_columns(send_ref.at[0])
 
 
-def far_kernel(b_ref, send_ref, out_ref):
-    pick_columns(b_ref, send_ref[:, send_ref.shape[-1] // 2 :], out_ref)
+def far_kernel(b_ref, send_ref, near_ref, far_ref, even_ref, flag_ref):
+    pick_columns(b_ref, send_ref[:, send_ref.shape[-1] // 2 :], far_ref)
+    chip = (lax.axis_index("dom") // 2) % 2
+    half = near_ref.shape[1] // 2
+    side = lax.broadcasted_iota(jnp.int32, near_ref.shape, 1) // half
+    even_ref[...] = jnp.where(side == chip, near_ref[...], far_ref[...])
+    lane = lax.broadcasted_iota(jnp.int32, flag_ref.shape, 1) // half
+    flag_ref[...] = jnp.where(lane == chip, 1.0, 0.0)
 
 
 def predict_kernel(dof_ref, star_ref, wk_ref, send_ref, b_ref, near_ref, m_ref):
@@ -236,7 +240,7 @@
         x = [padded(dof_ref, p, lanes) for p in range(NQ)]
         yield from taylor_steps(x, wk, m_ref, lanes, 0.5, 1.0 / 6.0, b_ref)
 
-    in_turns(half(pl.ds(0, LANES)), half(pl.ds(LANES, LANES)), [NQ, 3 * NQ] * 2)
+    in_turns(half(pl.ds(0, LANES)), half(pl.ds(LANES, LANES)), [[1] * NQ, [1] * 3 * NQ] * 2)
     pick_columns(b_ref, send_ref[:, : send_ref.shape[-1] // 2], near_ref)
 
 
@@ -305,7 +309,7 @@
     local_part(b_ref, w_ref, table_ref, ms_ref, ml_ref, mn_ref, out_ref, y_ref, lambda p, lanes: base_ref[p, :, lanes])
 
 
-def ghost_source(near_ref, even_ref, odd_ref):
+def ghost_source(near_ref, even_ref, odd_ref, cross_ref):
     me, total = lax.axis_index("dom"), lax.axis_size("dom")
     core = me % 2
     chip = (me // 2) % 2 == 0
@@ -314,7 +318,7 @@
     down = jnp.where(chip, odd, even)
     half = near.shape[1] // 2
     side = lax.broadcasted_iota(jnp.int32, near.shape, 1) // half
-    across = jnp.where(core == 0, down, up)
+    across = jnp.where((me // 2) % 2 == core, odd, cross_ref[...])
     one = jnp.where(side == core, across, near)
     two = jnp.where(side == 0, up, down)
     one = jnp.where(jnp.where(side == 0, me - 1, total - 2 - me) >= 0, one, 0.0)
@@ -345,10 +349,10 @@
 
 
 def second_kernel(
-    v_ref, dof_ref, near_ref, even_ref, odd_ref, wk_ref, send_ref, w_ref, table_ref, ms_ref, mn_ref,
+    v_ref, dof_ref, near_ref, even_ref, odd_ref, cross_ref, wk_ref, send_ref, w_ref, table_ref, ms_ref, mn_ref,
     state_ref, b_ref, near_out,
 ):
-    both = split_rows(ghost_source(near_ref, even_ref, odd_ref))
+    both = split_rows(ghost_source(near_ref, even_ref, odd_ref, cross_ref))
     index = ghost_index(table_ref, near_ref.shape[-1] // 2)
     both = gather_all(both, index)
     wk = wk_ref[...]
@@ -367,16 +371,16 @@
         w1, w2 = jnp.where(fine, 0.5, 1.5), jnp.where(fine, 1.0 / 6.0, 7.0 / 6.0)
         yield from taylor_steps(x, wk, ms_ref, lanes, w1, w2, b_ref)
 
-    in_turns(half(0), half(LANES), [4 + 4 * NQ, 4 * NQ] + [NQ, 3 * NQ] * 2)
+    in_turns(half(0), half(LANES), [FAR, [1] * 4 * NQ] + [[1] * NQ, [1] * 3 * NQ] * 2)
     pick_columns(b_ref, send_ref[:, : send_ref.shape[-1] // 2], near_out)
 
 
 def last_kernel(
-    v_ref, near_ref, even_ref, odd_ref, w_ref, table_ref, mn_ref, mask_ref,
+    v_ref, near_ref, even_ref, odd_ref, cross_ref, w_ref, table_ref, mn_ref, mask_ref,
     result_ref,
     out_ref, sems,
 ):
-    both = split_rows(ghost_source(near_ref, even_ref, odd_ref))
+    both = split_rows(ghost_source(near_ref, even_ref, odd_ref, cross_ref))
     index = ghost_index(table_ref, near_ref.shape[-1] // 2)
     both = gather_all(both, index)
     writes = []
@@ -419,7 +423,7 @@
             yield
         send_out(pl.ds(0, 6), lanes)
 
-    in_turns(half(0), half(LANES), [4 + 4 * NQ, 4 * NQ, 14])
+    in_turns(half(0), half(LANES), [FAR, [1] * 4 * NQ, [1] * 14])
     for write in writes:
         write.wait()
 
@@ -460,16 +464,17 @@
     return route
 
 
-def exchange(near, buffer, send, me, total):
+def exchange(near, buffer, send, total):
     got = lax.ppermute(near, "dom", core_swap(total))
-    far = call(far_kernel, [buffer, send], spec(near.shape), [], cost=500_000_000)
-    left = lax.broadcasted_iota(jnp.int32, got.shape, 1) < got.shape[1] // 2
-    forward = left == ((me // 2) % 2 == 0)
-    to_even, to_odd = jnp.where(forward, got, far), jnp.where(forward, far, got)
-    buffer, to_even, to_odd = lax.optimization_barrier((buffer, to_even, to_odd))
+    far, to_even, flag = call(
+        far_kernel, [buffer, send, near], (spec(near.shape), spec(near.shape), spec((8, near.shape[1]))), [], cost=0
+    )
     even = lax.ppermute(to_even, "dom", even_chip_swap(total))
+    to_odd = jnp.where(flag[:1] > 0.5, far, got)
     odd = lax.ppermute(to_odd, "dom", odd_chip_swap(total))
-    return got, even, odd, buffer
+    buffer, even, to_odd = lax.optimization_barrier((buffer, even, to_odd))
+    cross = lax.ppermute(even, "dom", core_swap(total))
+    return got, even, odd, cross, buffer
 
 
 def per_device(
@@ -493,7 +498,6 @@
 ):
     elements = dof_values.shape[-1]
     total = lax.axis_size("dom")
-    me = lax.axis_index("dom")
     ghosts = send_list.shape[-1]
 
     field = spec((NQ, R, elements))
@@ -520,7 +524,7 @@
         [((3 * R, LANES), F32)],
     )
     buffer_one, near, ms = call(predict_kernel, [dof_values, star, wk, send], (field, block, m_o(3)), [])
-    near, even, odd, buffer_one = exchange(near, buffer_one, send, me, total)
+    near, even, odd, cross, buffer_one = exchange(near, buffer_one, send, total)
     started, ml, mn, mask, table, weights = call(
         local_kernel,
         [
@@ -534,11 +538,11 @@
     )
     updated, buffer_two, near = call(
         second_kernel,
-        [started, dof_values, near, even, odd, wk, send, weights, table, ms, mn],
+        [started, dof_values, near, even, odd, cross, wk, send, weights, table, ms, mn],
         (field, field, block),
         [],
     )
-    near, even, odd, buffer_two = exchange(near, buffer_two, send, me, total)
+    near, even, odd, cross, buffer_two = exchange(near, buffer_two, send, total)
     started = call(
         again_kernel,
         [updated, buffer_two, weights, table, ms, ml, mn],
@@ -548,7 +552,7 @@
     )
     return call(
         last_kernel,
-        [started, near, even, odd, weights, table, mn, mask],
+        [started, near, even, odd, cross, weights, table, mn, mask],
         spec(dof_values.shape),
         [(dof_values.shape, F32), pltpu.SemaphoreType.DMA((4,))],
         out_space=HBM,

time: 29.8 us -> 29.2 us (0.980)
  waiting for transfers between devices: 4.09 us -> 2.62 us
  starting transfers between devices: 9.08 us -> 10 us
    ppermute x2, waiting for transfers between devices: 1.29 us -> 0.01 us  [exchange(): got = lax.ppermute(near, 'dom', core_swap(total))]
    ppermute x2, starting transfers between devices: 6.4 us -> 7 us  [exchange(): odd = lax.ppermute(to_odd, 'dom', odd_chip_swap(total))]
    ppermute x2, waiting for transfers between devices: 2.79 us -> 2.29 us  [exchange(): odd = lax.ppermute(to_odd, 'dom', odd_chip_swap(total))]
    ppermute x2, waiting for transfers between devices: 0.01 us -> 0.32 us  [exchange(): even = lax.ppermute(to_even, 'dom', even_chip_swap(total))]
  transfers between devices with their start and end apart: 6 -> 8, of which waited for: 4 -> 3; matrix products, arithmetic and copies ran while one was open for 0% -> 0% of each run, Pallas kernels for 24% -> 24%
where the time goes in v5:
time: 29.2 us; the launch traced here: 28.9 us
  Pallas kernels  13.6 us (47%)
  starting transfers between devices  10 us (34%)
  waiting for transfers between devices  2.62 us (9%)
  local copies, waits for them, and re-layouts  1.48 us (5%)
  between operations  1.14 us (4%)
    pallas_call x9, Pallas kernels, call(): pl.pallas_call(kernel, out_shape=outputs, in_specs=[VMEM] * len(inputs),...  13.6 us
    ppermute x2, starting transfers between devices, exchange(): odd = lax.ppermute(to_odd, 'dom', odd_chip_swap(total))  7 us
    ppermute x2, starting transfers between devices, exchange(): even = lax.ppermute(to_even, 'dom', even_chip_swap(total))  2.81 us
    ppermute x2, waiting for transfers between devices, exchange(): odd = lax.ppermute(to_odd, 'dom', odd_chip_swap(total))  2.29 us
    unnamed x32, local copies, waits for them, and re-layouts  1.48 us
  transfers between devices with their start and end apart: 8, of which 3 were waited for; matrix products, arithmetic and copies ran while one was open for 0% of the time, Pallas kernels for 24%

profile of v5, /device:TPU:24, one launch (start us, length us, event | category | flops | bytes accessed | tf_op | source)
XLA Modules:
  0.0 28.9 jit_solution(11162212703476357028)
XLA Ops:
  0.1 0.7 %copy-done.2 = f32[3,20,20]{2,1,0:T(8,128)S(1)} copy-done((f32[3,20,20]{2,1,0:T(8,128)S(1)}, f32[3,20,20]{2,1,0:T(8,128)}, u32[]{:S(2)}) %copy-start.2) | copy-done | bytes 4824
  0.8 0.0 copy-done.3
  0.8 0.2 shard_map.164
  1.0 0.0 copy-done
  1.0 0.1 copy-done.1
  1.1 1.4 %shard_map.165 = (f32[9,24,256]{2,1,0:T(8,128)S(1)}, f32[180,128]{1,0:T(8,128)S(1)}, f32[81,3,256]{2,1,0:T(4,128)S(1)}) custom-call(f32[9,20,256]{2,1,0:T(8,128)S(1)} %copy-done, bf16[9,9,3,256]{3,2,1,0:T(4,128)(2,1)S(1)} %bitcast.13, bf16[72,72]{1,0:T(8,128)(2,1)S(1)} %get-tuple-element.33.wk_ref, f32[1,256]{1,0:T(1,128)S(1)} %get-tuple-element.34.send_ref), custom_call_target="tpu_custom_call" | custom-call | bytes 1048576 | tf_op jit(solution)/shard_map/pallas_call | solution.py:440
  2.4 0.1 collective-permute-start.1
  2.5 0.0 copy-start.6
  2.5 0.2 shard_map.166
  2.8 1.6 %collective-permute-start = (f32[180,128]{1,0:T(8,128)S(1)}, f32[180,128]{1,0:T(8,128)S(1)}, u32[]{:S(2)}, u32[]{:S(2)}) collective-permute-start(f32[180,128]{1,0:T(8,128)S(1)} %get-tuple-element.37), channel_id=1, source_target_pairs={{0,2},{1,3},{2,0},{3,1},{4,6},{5,7},{6,4},{7,5},{8,10},{9,11},{10,... | collective-permute-start | bytes 276488 | tf_op jit(solution)/shard_map/ppermute | solution.py:472
  5.1 3.4 %collective-permute-start.2 = (f32[180,128]{1,0:T(8,128)S(1)}, f32[180,128]{1,0:T(8,128)S(1)}, u32[]{:S(2)}, u32[]{:S(2)}) collective-permute-start(f32[180,128]{1,0:T(8,128)S(1)} %broadcast_select_fusion.1), channel_id=1, source_target_pairs={{0,0},{1,1},{30,30},{31,31},{2,4},{4,2},{3,5},{5,3},{6,8},{8,6},{7... | collective-permute-start | bytes 276488 | tf_op jit(solution)/shard_map/ppermute | solution.py:474
  8.6 0.1 collective-permute-start.3
  8.8 0.6 %copy-done.13 = s32[256]{0:T(256)S(1)} copy-done((s32[256]{0:T(256)S(1)}, s32[256]{0:T(256)}, u32[]{:S(2)}) %copy-start.13) | copy-done | bytes 1048
  9.3 3.5 %shard_map.167 = (f32[9,24,256]{2,1,0:T(8,128)S(1)}, f32[81,4,256]{2,1,0:T(4,128)S(1)}, f32[81,4,256]{2,1,0:T(4,128)S(1)}, f32[24,256]{1,0:T(8,128)S(1)}, f32[40...) custom-call(f32[9,20,256]{2,1,0:T(8,128)S(1)} %copy-done, f32[9,24,256]{2,1,0:T(8,128)S(1)} %get-tuple-element.40.b_ref, ...), custom_call_target="tpu_custom_call" | custom-call | flops 1000000000 | bytes 1048576 | tf_op jit(solution)/shard_map/pallas_call | solution.py:440
  12.8 0.9 %collective-permute-done.2.odd_ref = f32[180,128]{1,0:T(8,128)S(1)} collective-permute-done((f32[180,128]{1,0:T(8,128)S(1)}, f32[180,128]{1,0:T(8,128)S(1)}, u32[]{:S(2)}, u32[]{:S(2)}) %collective-permute-start.2) | collective-permute-done | bytes 92192 | tf_op jit(solution)/shard_map/ppermute | solution.py:474
  13.8 2.7 %shard_map.168 = (f32[9,24,256]{2,1,0:T(8,128)S(1)}, f32[9,24,256]{2,1,0:T(8,128)S(1)}, f32[180,128]{1,0:T(8,128)S(1)}) custom-call(f32[9,24,256]{2,1,0:T(8,128)S(1)} %get-tuple-element.42.v_ref, f32[9,20,256]{2,1,0:T(8,128)S(1)} %copy-done, f32[180,128]{1,0:T(8,128)S(1)} %collective-permute-done.1.near_ref, f32[180,128]{1,0:T(8,128)S(1)} %collective-permute-done.even_ref, ...), custom_call_target="tpu_custom_call" | custom-call | bytes 1048576 | tf_op jit(solution)/shard_map/pallas_call | solution.py:440
  16.4 0.1 collective-permute-start.5
  16.5 0.2 shard_map.169
  16.8 1.2 %collective-permute-start.4 = (f32[180,128]{1,0:T(8,128)S(1)}, f32[180,128]{1,0:T(8,128)S(1)}, u32[]{:S(2)}, u32[]{:S(2)}) collective-permute-start(f32[180,128]{1,0:T(8,128)S(1)} %get-tuple-element.50), channel_id=1, source_target_pairs={{0,2},{1,3},{2,0},{3,1},{4,6},{5,7},{6,4},{7,5},{8,10},{9,11},{10,... | collective-permute-start | bytes 276488 | tf_op jit(solution)/shard_map/ppermute | solution.py:472
  18.0 3.6 %collective-permute-start.6 = (f32[180,128]{1,0:T(8,128)S(1)}, f32[180,128]{1,0:T(8,128)S(1)}, u32[]{:S(2)}, u32[]{:S(2)}) collective-permute-start(f32[180,128]{1,0:T(8,128)S(1)} %broadcast_select_fusion), channel_id=1, source_target_pairs={{0,0},{1,1},{30,30},{31,31},{2,4},{4,2},{3,5},{5,3},{6,8},{8,6},{7... | collective-permute-start | bytes 276488 | tf_op jit(solution)/shard_map/ppermute | solution.py:474
  21.6 0.3 %collective-permute-done.4.even_ref = f32[180,128]{1,0:T(8,128)S(1)} collective-permute-done((f32[180,128]{1,0:T(8,128)S(1)}, f32[180,128]{1,0:T(8,128)S(1)}, u32[]{:S(2)}, u32[]{:S(2)}) %collective-permute-start.4) | collective-permute-done | bytes 92192 | tf_op jit(solution)/shard_map/ppermute | solution.py:472
  22.0 3.0 %shard_map.170.v_ref = f32[9,24,256]{2,1,0:T(8,128)S(1)} custom-call(f32[9,24,256]{2,1,0:T(8,128)S(1)} %get-tuple-element.47.base_ref, f32[9,24,256]{2,1,0:T(8,128)S(1)} %get-tuple-element.53.b_ref, bf16[600,72]{1,0:T(8,128)(2,1)S(1)} %get-tuple-element.44.w_ref, f32[40,256]{1,0:T(8,128)S(1)} %get-tuple-element.45.table_ref, ...), custom_call_target="tpu_custom_call" | custom-call | flops 1000000000 | bytes 1048576 | tf_op jit(solution)/shard_map/pallas_call | solution.py:440
  24.9 1.4 %collective-permute-done.6.odd_ref = f32[180,128]{1,0:T(8,128)S(1)} collective-permute-done((f32[180,128]{1,0:T(8,128)S(1)}, f32[180,128]{1,0:T(8,128)S(1)}, u32[]{:S(2)}, u32[]{:S(2)}) %collective-permute-start.6) | collective-permute-done | bytes 92192 | tf_op jit(solution)/shard_map/ppermute | solution.py:474
  26.3 2.4 %shard_map.171 = f32[9,20,256]{2,1,0:T(8,128)} custom-call(f32[9,24,256]{2,1,0:T(8,128)S(1)} %shard_map.170.v_ref, f32[180,128]{1,0:T(8,128)S(1)} %collective-permute-done.5.near_ref, f32[180,128]{1,0:T(8,128)S(1)} %collective-permute-done.4.even_ref, f32[180,128]{1,0:T(8,128)S(1)} %collective-permute-done.6.odd_ref, ...), custom_call_target="tpu_custom_call" | custom-call | bytes 1048576 | tf_op jit(solution)/shard_map/pallas_call | solution.py:440
  (37 shorter events, 0.2 us)
Async XLA Ops:
  0.0 0.8 %copy-start.2 = (f32[3,20,20]{2,1,0:T(8,128)S(1)}, f32[3,20,20]{2,1,0:T(8,128)}, u32[]{:S(2)}) copy-start(f32[3,20,20]{2,1,0:T(8,128)} %kstiff_ref.3) | copy-start | bytes 14404
  0.0 1.0 %copy-start = (f32[9,20,256]{2,1,0:T(8,128)S(1)}, f32[9,20,256]{2,1,0:T(8,128)}, u32[]{:S(2)}) copy-start(f32[9,20,256]{2,1,0:T(8,128)} %dof_ref.5) | copy-start | bytes 552964
  0.0 1.1 %copy-start.1 = (bf16[3,9,9,256]{3,0,2,1:T(4,128)(2,1)S(1)}, bf16[3,9,9,256]{3,0,2,1:T(4,128)(2,1)}, u32[]{:S(2)}) copy-start(bf16[3,9,9,256]{3,0,2,1:T(4,128)(2,1)} %param.18) | copy-start | bytes 373252
  0.0 0.7 %copy-start.3 = (s32[1,4,64]{2,1,0:T(4,128)S(1)}, s32[1,4,64]{2,1,0:T(4,128)}, u32[]{:S(2)}) copy-start(s32[1,4,64]{2,1,0:T(4,128)} %send_ref.1) | copy-start | bytes 3076
  2.4 2.6 %collective-permute-start.1 = (f32[180,128]{1,0:T(8,128)S(1)}, f32[180,128]{1,0:T(8,128)S(1)}, u32[]{:S(2)}, u32[]{:S(2)}) collective-permute-start(f32[180,128]{1,0:T(8,128)S(1)} %get-tuple-element.36.near_ref), channel_id=1, source_target_pairs={{0,1},{1,0},{2,3},{3,2},{4,5},{5,4},{6,7},{7,6},{8,9},{9,8},{10,11... | collective-permute-start | bytes 276488 | tf_op jit(solution)/shard_map/ppermute | solution.py:468
  2.5 6.1 %copy-start.5 = (bf16[4,9,9,256]{3,0,2,1:T(4,128)(2,1)S(1)}, bf16[4,9,9,256]{3,0,2,1:T(4,128)(2,1)}, u32[]{:S(2)}) copy-start(bf16[4,9,9,256]{3,0,2,1:T(4,128)(2,1)} %param.20) | copy-start | bytes 497668
  2.5 6.1 %copy-start.6 = (f32[4,4,20,20]{3,1,2,0:T(4,128)S(1)}, f32[4,4,20,20]{3,1,2,0:T(4,128)}, u32[]{:S(2)}) copy-start(f32[4,4,20,20]{3,1,2,0:T(4,128)} %param.23) | copy-start | bytes 76804
  2.8 5.9 %copy-start.4 = (bf16[4,9,9,256]{3,0,2,1:T(4,128)(2,1)S(1)}, bf16[4,9,9,256]{3,0,2,1:T(4,128)(2,1)}, u32[]{:S(2)}) copy-start(bf16[4,9,9,256]{3,0,2,1:T(4,128)(2,1)} %param.19) | copy-start | bytes 497668
  2.8 5.8 %collective-permute-start = (f32[180,128]{1,0:T(8,128)S(1)}, f32[180,128]{1,0:T(8,128)S(1)}, u32[]{:S(2)}, u32[]{:S(2)}) collective-permute-start(f32[180,128]{1,0:T(8,128)S(1)} %get-tuple-element.37), channel_id=1, source_target_pairs={{0,2},{1,3},{2,0},{3,1},{4,6},{5,7},{6,4},{7,5},{8,10},{9,11},{10,... | collective-permute-start | bytes 276488 | tf_op jit(solution)/shard_map/ppermute | solution.py:472
  5.0 3.7 %copy-start.7 = (f32[4,20,20]{2,0,1:T(4,128)S(1)}, f32[4,20,20]{2,0,1:T(4,128)}, u32[]{:S(2)}) copy-start(f32[4,20,20]{2,0,1:T(4,128)} %param.22) | copy-start | bytes 19204
  5.0 3.7 %copy-start.8 = (s32[20,256]{1,0:T(8,128)S(1)}, s32[20,256]{1,0:T(8,128)}, u32[]{:S(2)}) copy-start(s32[20,256]{1,0:T(8,128)} %yield_ref.1) | copy-start | bytes 61444
  5.0 3.7 %copy-start.10 = (f32[20,20]{1,0:T(8,128)S(1)}, f32[20,20]{1,0:T(8,128)}, u32[]{:S(2)}) copy-start(f32[20,20]{1,0:T(8,128)} %from_ref.1) | copy-start | bytes 4804
  5.0 3.7 %copy-start.11 = (s32[4,256]{1,0:T(4,128)S(1)}, s32[4,256]{1,0:T(4,128)}, u32[]{:S(2)}) copy-start(s32[4,256]{1,0:T(4,128)} %index_ref.1) | copy-start | bytes 12292
  5.1 3.7 %copy-start.12 = (s32[4,256]{1,0:T(4,128)S(1)}, s32[4,256]{1,0:T(4,128)}, u32[]{:S(2)}) copy-start(s32[4,256]{1,0:T(4,128)} %face_ref.1) | copy-start | bytes 12292
  5.1 3.7 %copy-start.14 = (s32[1,256]{1,0:T(1,128)S(1)}, s32[1,256]{1,0:T(1,128)}, u32[]{:S(2)}) copy-start(s32[1,256]{1,0:T(1,128)} %damage_ref.1) | copy-start | bytes 3076
  5.1 3.7 %copy-start.15 = (f32[256]{0:T(256)S(1)}, f32[256]{0:T(256)}, u32[]{:S(2)}) copy-start(f32[256]{0:T(256)} %param.31) | copy-start | bytes 3076
  5.1 3.6 %copy-start.9 = (f32[20,20]{1,0:T(8,128)S(1)}, f32[20,20]{1,0:T(8,128)}, u32[]{:S(2)}) copy-start(f32[20,20]{1,0:T(8,128)} %to_ref.1) | copy-start | bytes 4804
  5.1 8.6 %collective-permute-start.2 = (f32[180,128]{1,0:T(8,128)S(1)}, f32[180,128]{1,0:T(8,128)S(1)}, u32[]{:S(2)}, u32[]{:S(2)}) collective-permute-start(f32[180,128]{1,0:T(8,128)S(1)} %broadcast_select_fusion.1), channel_id=1, source_target_pairs={{0,0},{1,1},{30,30},{31,31},{2,4},{4,2},{3,5},{5,3},{6,8},{8,6},{7... | collective-permute-start | bytes 276488 | tf_op jit(solution)/shard_map/ppermute | solution.py:474
  8.6 5.2 %collective-permute-start.3 = (f32[180,128]{1,0:T(8,128)S(1)}, f32[180,128]{1,0:T(8,128)S(1)}, u32[]{:S(2)}, u32[]{:S(2)}) collective-permute-start(f32[180,128]{1,0:T(8,128)S(1)} %collective-permute-done.even_ref), channel_id=1, source_target_pairs={{0,1},{1,0},{2,3},{3,2},{4,5},{5,4},{6,7},{7,6},{8,9},{9,8},{10,11... | collective-permute-start | bytes 276488 | tf_op jit(solution)/shard_map/ppermute | solution.py:476
  8.6 0.7 %copy-start.13 = (s32[256]{0:T(256)S(1)}, s32[256]{0:T(256)}, u32[]{:S(2)}) copy-start(s32[256]{0:T(256)} %param.26) | copy-start | bytes 3076
  16.4 1.6 %collective-permute-start.5 = (f32[180,128]{1,0:T(8,128)S(1)}, f32[180,128]{1,0:T(8,128)S(1)}, u32[]{:S(2)}, u32[]{:S(2)}) collective-permute-start(f32[180,128]{1,0:T(8,128)S(1)} %get-tuple-element.49.near_ref), channel_id=1, source_target_pairs={{0,1},{1,0},{2,3},{3,2},{4,5},{5,4},{6,7},{7,6},{8,9},{9,8},{10,11... | collective-permute-start | bytes 276488 | tf_op jit(solution)/shard_map/ppermute | solution.py:468
  16.8 5.2 %collective-permute-start.4 = (f32[180,128]{1,0:T(8,128)S(1)}, f32[180,128]{1,0:T(8,128)S(1)}, u32[]{:S(2)}, u32[]{:S(2)}) collective-permute-start(f32[180,128]{1,0:T(8,128)S(1)} %get-tuple-element.50), channel_id=1, source_target_pairs={{0,2},{1,3},{2,0},{3,1},{4,6},{5,7},{6,4},{7,5},{8,10},{9,11},{10,... | collective-permute-start | bytes 276488 | tf_op jit(solution)/shard_map/ppermute | solution.py:472
  18.0 8.3 %collective-permute-start.6 = (f32[180,128]{1,0:T(8,128)S(1)}, f32[180,128]{1,0:T(8,128)S(1)}, u32[]{:S(2)}, u32[]{:S(2)}) collective-permute-start(f32[180,128]{1,0:T(8,128)S(1)} %broadcast_select_fusion), channel_id=1, source_target_pairs={{0,0},{1,1},{30,30},{31,31},{2,4},{4,2},{3,5},{5,3},{6,8},{8,6},{7... | collective-permute-start | bytes 276488 | tf_op jit(solution)/shard_map/ppermute | solution.py:474
  21.9 4.4 %collective-permute-start.7 = (f32[180,128]{1,0:T(8,128)S(1)}, f32[180,128]{1,0:T(8,128)S(1)}, u32[]{:S(2)}, u32[]{:S(2)}) collective-permute-start(f32[180,128]{1,0:T(8,128)S(1)} %collective-permute-done.4.even_ref), channel_id=1, source_target_pairs={{0,1},{1,0},{2,3},{3,2},{4,5},{5,4},{6,7},{7,6},{8,9},{9,8},{10,11... | collective-permute-start | bytes 276488 | tf_op jit(solution)/shard_map/ppermute | solution.py:476

commit v6 on v5

--- a/solution.py
+++ b/solution.py
@@ -216,10 +216,20 @@
     return jnp.where(slot < 2, first, second)
 
 
-def setup_kernel(kstiff_ref, send_ref, twice_ref, once_ref, wk_ref, send_out, w_ref):
+NEIGHBOUR, FACE, CLUSTER, COHESION, LIVE, YIELD = 0, 4, 8, 9, 10, 16
+ROWS = 40
+
+
+def setup_kernel(kstiff_ref, count_ref, twice_ref, once_ref, wk_ref, count_out, w_ref):
     fill_stiffness(w_ref, kstiff_ref)
     wk_ref[...] = place_weights(w_ref[...], twice_ref, once_ref)
-    send_out[...] = send_columns(send_ref.at[0])
+    count_out[...] = jnp.broadcast_to(count_ref[...], count_out.shape).astype(F32)
+
+
+def near_kernel(b_ref, lists_ref, near_ref, send_ref):
+    send = send_columns(lists_ref.at[0])
+    send_ref[...] = send
+    pick_columns(b_ref, send[:, : send.shape[-1] // 2], near_ref)
 
 
 def far_kernel(b_ref, send_ref, near_ref, far_ref, even_ref, flag_ref):
@@ -232,7 +242,7 @@
     flag_ref[...] = jnp.where(lane == chip, 1.0, 0.0)
 
 
-def predict_kernel(dof_ref, star_ref, wk_ref, send_ref, b_ref, near_ref, m_ref):
+def predict_kernel(dof_ref, star_ref, wk_ref, b_ref, m_ref):
     widen(star_ref, m_ref)
     wk = wk_ref[...]
 
@@ -241,23 +251,16 @@
         yield from taylor_steps(x, wk, m_ref, lanes, 0.5, 1.0 / 6.0, b_ref)
 
     in_turns(half(pl.ds(0, LANES)), half(pl.ds(LANES, LANES)), [[1] * NQ, [1] * 3 * NQ] * 2)
-    pick_columns(b_ref, send_ref[:, : send_ref.shape[-1] // 2], near_ref)
-
-
-NEIGHBOUR, FACE, CLUSTER, DAMAGE, COHESION, YIELD = 0, 4, 8, 9, 10, 16
-ROWS = 40
-
-
-def fill_table(table_ref, index_ref, face_ref, cluster_ref, damage_ref, count_ref, cohesion_ref, yield_ref):
-    elements = table_ref.shape[-1]
+
+
+def fill_table(table_ref, index_ref, face_ref, cluster_ref, cohesion_ref, damage_ref, count_ref, yield_ref):
     table_ref[...] = jnp.zeros(table_ref.shape, F32)
     table_ref[NEIGHBOUR : NEIGHBOUR + 4, :] = index_ref[...].astype(F32)
     table_ref[FACE : FACE + 4, :] = face_ref[...].astype(F32)
     table_ref[CLUSTER : CLUSTER + 1, :] = cluster_ref[...].astype(F32)
-    slot = lax.broadcasted_iota(jnp.int32, (1, elements), 1)
-    count = jnp.broadcast_to(count_ref[...], (1, elements))
-    table_ref[DAMAGE : DAMAGE + 1, :] = jnp.where(slot < count, damage_ref[...], -1).astype(F32)
     table_ref[COHESION : COHESION + 1, :] = cohesion_ref[...]
+    slot = lax.broadcasted_iota(jnp.int32, damage_ref.shape, 1).astype(F32)
+    table_ref[LIVE : LIVE + 1, :] = jnp.where(slot < count_ref[...], damage_ref[...].astype(F32), -1.0)
     table_ref[YIELD : YIELD + NB, :] = yield_ref[...].astype(F32)
 
 
@@ -282,31 +285,33 @@
 def local_kernel(
     dof_ref, b_ref, ms_ref, local_ref, neigh_ref,
     kstiff_ref, minus_ref, plus_ref, to_ref, from_ref, twice_ref, once_ref,
-    index_ref, face_ref, cluster_ref, damage_ref, count_ref, cohesion_ref, yield_ref,
-    out_ref, ml_ref, mn_ref, mask_ref, table_ref, weights_ref,
+    index_ref, face_ref, cluster_ref, cohesion_ref, damage_ref, count_ref, yield_ref,
+    out_ref, ml_ref, mn_ref, table_ref, weights_ref,
     w_ref, y_ref,
 ):
     fill_weights(w_ref, kstiff_ref, minus_ref, plus_ref, to_ref, from_ref)
     weights_ref[...] = place_weights(w_ref[...], twice_ref, once_ref)
-    fill_table(table_ref, index_ref, face_ref, cluster_ref, damage_ref, count_ref, cohesion_ref, yield_ref)
+    fill_table(table_ref, index_ref, face_ref, cluster_ref, cohesion_ref, damage_ref, count_ref, yield_ref)
     widen(local_ref, ml_ref)
     widen(neigh_ref, mn_ref)
     local_part(
         b_ref, weights_ref, table_ref, ms_ref, ml_ref, mn_ref, out_ref, y_ref, lambda p, lanes: padded(dof_ref, p, lanes)
     )
+
+
+def again_kernel(
+    base_ref, b_ref, w_ref, table_ref, ms_ref, ml_ref, mn_ref, out_ref, mask_ref, y_ref
+):
+    local_part(b_ref, w_ref, table_ref, ms_ref, ml_ref, mn_ref, out_ref, y_ref, lambda p, lanes: base_ref[p, :, lanes])
     elements = out_ref.shape[-1]
     rows = lax.broadcasted_iota(jnp.int32, (elements, elements), 0).astype(F32)
     listed = lax.dot_general(
         jnp.ones((8, elements), BF16),
-        jnp.where(rows == table_ref[DAMAGE : DAMAGE + 1], 1.0, 0.0).astype(BF16),
+        jnp.where(rows == table_ref[LIVE : LIVE + 1], 1.0, 0.0).astype(BF16),
         (((1,), (1,)), ((), ())),
         preferred_element_type=F32,
     )[0:1]
     mask_ref[...] = jnp.where(listed > 0.5, table_ref[YIELD : YIELD + R], 0.0)
-
-
-def again_kernel(base_ref, b_ref, w_ref, table_ref, ms_ref, ml_ref, mn_ref, out_ref, y_ref):
-    local_part(b_ref, w_ref, table_ref, ms_ref, ml_ref, mn_ref, out_ref, y_ref, lambda p, lanes: base_ref[p, :, lanes])
 
 
 def ghost_source(near_ref, even_ref, odd_ref, cross_ref):
@@ -517,22 +522,23 @@
 
     place = spec((LANES, K3), BF16)
     twice, once = call(place_kernel, [], (place, place), [], cost=4_000_000_000)
-    wk, send = call(
+    wk, count = call(
         setup_kernel,
-        [kstiff, send_list, twice, once],
-        (spec((3 * R, K3), BF16), spec((1, 4 * ghosts))),
+        [kstiff, damage_count[None], twice, once],
+        (spec((3 * R, K3), BF16), spec((1, elements))),
         [((3 * R, LANES), F32)],
     )
-    buffer_one, near, ms = call(predict_kernel, [dof_values, star, wk, send], (field, block, m_o(3)), [])
+    buffer_one, ms = call(predict_kernel, [dof_values, star, wk], (field, m_o(3)), [])
+    near, send = call(near_kernel, [buffer_one, send_list], (block, spec((1, 4 * ghosts))), [])
     near, even, odd, cross, buffer_one = exchange(near, buffer_one, send, total)
-    started, ml, mn, mask, table, weights = call(
+    started, ml, mn, table, weights = call(
         local_kernel,
         [
             dof_values, buffer_one, ms, own, other,
             kstiff, minus, plus, to_points, from_points, twice, once,
-            neighbour, neigh_face, cluster[None], damage_list, damage_count[None], cohesion[None], yield_mask,
+            neighbour, neigh_face, cluster[None], cohesion[None], damage_list, count, yield_mask,
         ],
-        (field, m_o(4), m_o(4), spec((R, elements)), spec((ROWS, elements)), spec((W_ROWS, K3), BF16)),
+        (field, m_o(4), m_o(4), spec((ROWS, elements)), spec((W_ROWS, K3), BF16)),
         [((W_ROWS, LANES), F32), y_s(11)],
         cost=1_000_000_000,
     )
@@ -543,10 +549,10 @@
         [],
     )
     near, even, odd, cross, buffer_two = exchange(near, buffer_two, send, total)
-    started = call(
+    started, mask = call(
         again_kernel,
         [updated, buffer_two, weights, table, ms, ml, mn],
-        field,
+        (field, spec((R, elements))),
         [y_s(11)],
         cost=1_000_000_000,
     )

time: 29.2 us -> 28.7 us (0.983)
  local copies, waits for them, and re-layouts: 1.48 us -> 0.81 us
  waiting for transfers between devices: 2.62 us -> 2.07 us
  starting transfers between devices: 10 us -> 10.5 us
  Pallas kernels: 13.6 us -> 13.9 us
    unnamed x32, local copies, waits for them, and re-layouts: 1.48 us -> 0.81 us
    ppermute x2, waiting for transfers between devices: 2.29 us -> 1.85 us  [exchange(): odd = lax.ppermute(to_odd, 'dom', odd_chip_swap(total))]
    ppermute x2, starting transfers between devices: 7 us -> 7.34 us  [exchange(): odd = lax.ppermute(to_odd, 'dom', odd_chip_swap(total))]
    pallas_call x9 -> x10, Pallas kernels: 13.6 us -> 13.9 us  [call(): pl.pallas_call(kernel, out_shape=outputs, in_specs=[VMEM] * len(inputs),...]
  transfers between devices with their start and end apart: 8 -> 8, of which waited for: 3 -> 3; matrix products, arithmetic and copies ran while one was open for 0% -> 0% of each run, Pallas kernels for 24% -> 25%
where the time goes in v6:
time: 28.7 us; the launch traced here: 28.5 us
  Pallas kernels  13.9 us (48%)
  starting transfers between devices  10.5 us (37%)
  waiting for transfers between devices  2.07 us (7%)
  between operations  1.17 us (4%)
  local copies, waits for them, and re-layouts  0.81 us (3%)
    pallas_call x10, Pallas kernels, call(): pl.pallas_call(kernel, out_shape=outputs, in_specs=[VMEM] * len(inputs),...  13.9 us
    ppermute x2, starting transfers between devices, exchange(): odd = lax.ppermute(to_odd, 'dom', odd_chip_swap(total))  7.34 us
    ppermute x2, starting transfers between devices, exchange(): even = lax.ppermute(to_even, 'dom', even_chip_swap(total))  2.87 us
    ppermute x2, waiting for transfers between devices, exchange(): odd = lax.ppermute(to_odd, 'dom', odd_chip_swap(total))  1.85 us
    unnamed x32, local copies, waits for them, and re-layouts  0.81 us
  transfers between devices with their start and end apart: 8, of which 3 were waited for; matrix products, arithmetic and copies ran while one was open for 0% of the time, Pallas kernels for 25%

profile of v6, /device:TPU:24, one launch (start us, length us, event | category | flops | bytes accessed | tf_op | source)
XLA Modules:
  0.0 28.5 jit_solution(418723688378581670)
XLA Ops:
  0.7 0.0 copy-done.2
  0.8 0.2 shard_map.164
  0.9 0.1 copy-done
  1.0 0.1 copy-done.1
  1.1 1.2 %shard_map.165 = (f32[9,24,256]{2,1,0:T(8,128)S(1)}, f32[81,3,256]{2,1,0:T(4,128)S(1)}) custom-call(f32[9,20,256]{2,1,0:T(8,128)S(1)} %copy-done, bf16[9,9,3,256]{3,2,1,0:T(4,128)(2,1)S(1)} %bitcast.13, bf16[72,72]{1,0:T(8,128)(2,1)S(1)} %get-tuple-element.35.wk_ref), custom_call_target="tpu_custom_call" | custom-call | bytes 1048576 | tf_op jit(solution)/shard_map/pallas_call | solution.py:445
  2.3 0.4 %shard_map.166 = (f32[180,128]{1,0:T(8,128)S(1)}, f32[1,256]{1,0:T(1,128)S(1)}) custom-call(f32[9,24,256]{2,1,0:T(8,128)S(1)} %get-tuple-element.42.b_ref, s32[1,4,64]{2,1,0:T(4,128)S(1)} %copy-done.3), custom_call_target="tpu_custom_call" | custom-call | bytes 1048576 | tf_op jit(solution)/shard_map/pallas_call | solution.py:445
  2.7 0.1 collective-permute-start.1
  2.7 0.0 copy-start.6
  2.8 0.2 shard_map.167
  3.0 1.6 %collective-permute-start = (f32[180,128]{1,0:T(8,128)S(1)}, f32[180,128]{1,0:T(8,128)S(1)}, u32[]{:S(2)}, u32[]{:S(2)}) collective-permute-start(f32[180,128]{1,0:T(8,128)S(1)} %get-tuple-element.39), channel_id=1, source_target_pairs={{0,2},{1,3},{2,0},{3,1},{4,6},{5,7},{6,4},{7,5},{8,10},{9,11},{10,... | collective-permute-start | bytes 276488 | tf_op jit(solution)/shard_map/ppermute | solution.py:477
  4.7 3.8 %collective-permute-start.2 = (f32[180,128]{1,0:T(8,128)S(1)}, f32[180,128]{1,0:T(8,128)S(1)}, u32[]{:S(2)}, u32[]{:S(2)}) collective-permute-start(f32[180,128]{1,0:T(8,128)S(1)} %broadcast_select_fusion.1), channel_id=1, source_target_pairs={{0,0},{1,1},{30,30},{31,31},{2,4},{4,2},{3,5},{5,3},{6,8},{8,6},{7... | collective-permute-start | bytes 276488 | tf_op jit(solution)/shard_map/ppermute | solution.py:479
  8.5 0.1 collective-permute-start.3
  8.7 0.6 %copy-done.13 = s32[256]{0:T(256)S(1)} copy-done((s32[256]{0:T(256)S(1)}, s32[256]{0:T(256)}, u32[]{:S(2)}) %copy-start.13) | copy-done | bytes 1048
  9.2 3.6 %shard_map.168 = (f32[9,24,256]{2,1,0:T(8,128)S(1)}, f32[81,4,256]{2,1,0:T(4,128)S(1)}, f32[81,4,256]{2,1,0:T(4,128)S(1)}, f32[40,256]{1,0:T(8,128)S(1)}, bf16[600,72]{1,0:T(8,128)(2,1)S(1)}) custom-call(f32[9,20,256]{2,1,0:T(8,128)S(1)} %copy-done, f32[9,24,256]{2,1,0:T(8,128)S(1)} %get-tuple-element.42.b_ref, f32[81,3,256]{2,1,0:T(4,128)S(1)} %get-tuple-element.43.ms_ref, ...), custom_call_target="tpu_custom_call" | custom-call | flops 1000000000 | bytes 1048576 | tf_op jit(solution)/shard_map/pallas_call | solution.py:445
  12.9 0.4 %collective-permute-done.2.odd_ref = f32[180,128]{1,0:T(8,128)S(1)} collective-permute-done((f32[180,128]{1,0:T(8,128)S(1)}, f32[180,128]{1,0:T(8,128)S(1)}, u32[]{:S(2)}, u32[]{:S(2)}) %collective-permute-start.2) | collective-permute-done | bytes 92192 | tf_op jit(solution)/shard_map/ppermute | solution.py:479
  13.3 2.7 %shard_map.169 = (f32[9,24,256]{2,1,0:T(8,128)S(1)}, f32[9,24,256]{2,1,0:T(8,128)S(1)}, f32[180,128]{1,0:T(8,128)S(1)}) custom-call(f32[9,24,256]{2,1,0:T(8,128)S(1)} %get-tuple-element.45.v_ref, f32[9,20,256]{2,1,0:T(8,128)S(1)} %copy-done, f32[180,128]{1,0:T(8,128)S(1)} %collective-permute-done.1.near_ref, f32[180,128]{1,0:T(8,128)S(1)} %collective-permute-done.even_ref, ...), custom_call_target="tpu_custom_call" | custom-call | bytes 1048576 | tf_op jit(solution)/shard_map/pallas_call | solution.py:445
  16.0 0.2 collective-permute-start.5
  16.2 0.2 shard_map.170
  16.4 1.3 %collective-permute-start.4 = (f32[180,128]{1,0:T(8,128)S(1)}, f32[180,128]{1,0:T(8,128)S(1)}, u32[]{:S(2)}, u32[]{:S(2)}) collective-permute-start(f32[180,128]{1,0:T(8,128)S(1)} %get-tuple-element.53), channel_id=1, source_target_pairs={{0,2},{1,3},{2,0},{3,1},{4,6},{5,7},{6,4},{7,5},{8,10},{9,11},{10,... | collective-permute-start | bytes 276488 | tf_op jit(solution)/shard_map/ppermute | solution.py:477
  17.7 3.6 %collective-permute-start.6 = (f32[180,128]{1,0:T(8,128)S(1)}, f32[180,128]{1,0:T(8,128)S(1)}, u32[]{:S(2)}, u32[]{:S(2)}) collective-permute-start(f32[180,128]{1,0:T(8,128)S(1)} %broadcast_select_fusion), channel_id=1, source_target_pairs={{0,0},{1,1},{30,30},{31,31},{2,4},{4,2},{3,5},{5,3},{6,8},{8,6},{7... | collective-permute-start | bytes 276488 | tf_op jit(solution)/shard_map/ppermute | solution.py:479
  21.3 0.2 collective-permute-done.4.even_ref
  21.5 3.0 %shard_map.171 = (f32[9,24,256]{2,1,0:T(8,128)S(1)}, f32[24,256]{1,0:T(8,128)S(1)}) custom-call(f32[9,24,256]{2,1,0:T(8,128)S(1)} %get-tuple-element.50.base_ref, f32[9,24,256]{2,1,0:T(8,128)S(1)} %get-tuple-element.56.b_ref, bf16[600,72]{1,0:T(8,128)(2,1)S(1)} %get-tuple-element.47.w_ref, f32[40,256]{1,0:T(8,128)S(1)} %get-tuple-element.48.table_ref, ...), custom_call_target="tpu_custom_call" | custom-call | flops 1000000000 | bytes 1048576 | tf_op jit(solution)/shard_map/pallas_call | solution.py:445
  24.6 1.4 %collective-permute-done.6.odd_ref = f32[180,128]{1,0:T(8,128)S(1)} collective-permute-done((f32[180,128]{1,0:T(8,128)S(1)}, f32[180,128]{1,0:T(8,128)S(1)}, u32[]{:S(2)}, u32[]{:S(2)}) %collective-permute-start.6) | collective-permute-done | bytes 92192 | tf_op jit(solution)/shard_map/ppermute | solution.py:479
  26.0 2.4 %shard_map.172 = f32[9,20,256]{2,1,0:T(8,128)} custom-call(f32[9,24,256]{2,1,0:T(8,128)S(1)} %get-tuple-element.58.v_ref, f32[180,128]{1,0:T(8,128)S(1)} %collective-permute-done.5.near_ref, f32[180,128]{1,0:T(8,128)S(1)} %collective-permute-done.4.even_ref, f32[180,128]{1,0:T(8,128)S(1)} %collective-permute-done.6.odd_ref, ...), custom_call_target="tpu_custom_call" | custom-call | bytes 1048576 | tf_op jit(solution)/shard_map/pallas_call | solution.py:445
  (38 shorter events, 0.2 us)
Async XLA Ops:
  0.0 0.8 %copy-start.2 = (f32[3,20,20]{2,1,0:T(8,128)S(1)}, f32[3,20,20]{2,1,0:T(8,128)}, u32[]{:S(2)}) copy-start(f32[3,20,20]{2,1,0:T(8,128)} %kstiff_ref.3) | copy-start | bytes 14404
  0.0 1.0 %copy-start = (f32[9,20,256]{2,1,0:T(8,128)S(1)}, f32[9,20,256]{2,1,0:T(8,128)}, u32[]{:S(2)}) copy-start(f32[9,20,256]{2,1,0:T(8,128)} %dof_ref.5) | copy-start | bytes 552964
  0.0 1.1 %copy-start.1 = (bf16[3,9,9,256]{3,0,2,1:T(4,128)(2,1)S(1)}, bf16[3,9,9,256]{3,0,2,1:T(4,128)(2,1)}, u32[]{:S(2)}) copy-start(bf16[3,9,9,256]{3,0,2,1:T(4,128)(2,1)} %param.18) | copy-start | bytes 373252
  1.1 1.2 %copy-start.3 = (s32[1,4,64]{2,1,0:T(4,128)S(1)}, s32[1,4,64]{2,1,0:T(4,128)}, u32[]{:S(2)}) copy-start(s32[1,4,64]{2,1,0:T(4,128)} %lists_ref.1) | copy-start | bytes 3076
  2.7 1.9 %collective-permute-start.1 = (f32[180,128]{1,0:T(8,128)S(1)}, f32[180,128]{1,0:T(8,128)S(1)}, u32[]{:S(2)}, u32[]{:S(2)}) collective-permute-start(f32[180,128]{1,0:T(8,128)S(1)} %get-tuple-element.38.near_ref), channel_id=1, source_target_pairs={{0,1},{1,0},{2,3},{3,2},{4,5},{5,4},{6,7},{7,6},{8,9},{9,8},{10,11... | collective-permute-start | bytes 276488 | tf_op jit(solution)/shard_map/ppermute | solution.py:473
  2.7 5.8 %copy-start.5 = (bf16[4,9,9,256]{3,0,2,1:T(4,128)(2,1)S(1)}, bf16[4,9,9,256]{3,0,2,1:T(4,128)(2,1)}, u32[]{:S(2)}) copy-start(bf16[4,9,9,256]{3,0,2,1:T(4,128)(2,1)} %param.20) | copy-start | bytes 497668
  2.7 5.8 %copy-start.6 = (f32[4,4,20,20]{3,1,2,0:T(4,128)S(1)}, f32[4,4,20,20]{3,1,2,0:T(4,128)}, u32[]{:S(2)}) copy-start(f32[4,4,20,20]{3,1,2,0:T(4,128)} %param.23) | copy-start | bytes 76804
  3.0 5.6 %copy-start.4 = (bf16[4,9,9,256]{3,0,2,1:T(4,128)(2,1)S(1)}, bf16[4,9,9,256]{3,0,2,1:T(4,128)(2,1)}, u32[]{:S(2)}) copy-start(bf16[4,9,9,256]{3,0,2,1:T(4,128)(2,1)} %param.19) | copy-start | bytes 497668
  3.0 5.5 %collective-permute-start = (f32[180,128]{1,0:T(8,128)S(1)}, f32[180,128]{1,0:T(8,128)S(1)}, u32[]{:S(2)}, u32[]{:S(2)}) collective-permute-start(f32[180,128]{1,0:T(8,128)S(1)} %get-tuple-element.39), channel_id=1, source_target_pairs={{0,2},{1,3},{2,0},{3,1},{4,6},{5,7},{6,4},{7,5},{8,10},{9,11},{10,... | collective-permute-start | bytes 276488 | tf_op jit(solution)/shard_map/ppermute | solution.py:477
  4.6 4.0 %copy-start.7 = (f32[4,20,20]{2,0,1:T(4,128)S(1)}, f32[4,20,20]{2,0,1:T(4,128)}, u32[]{:S(2)}) copy-start(f32[4,20,20]{2,0,1:T(4,128)} %param.22) | copy-start | bytes 19204
  4.6 4.0 %copy-start.8 = (s32[20,256]{1,0:T(8,128)S(1)}, s32[20,256]{1,0:T(8,128)}, u32[]{:S(2)}) copy-start(s32[20,256]{1,0:T(8,128)} %yield_ref.1) | copy-start | bytes 61444
  4.6 4.0 %copy-start.10 = (f32[20,20]{1,0:T(8,128)S(1)}, f32[20,20]{1,0:T(8,128)}, u32[]{:S(2)}) copy-start(f32[20,20]{1,0:T(8,128)} %from_ref.1) | copy-start | bytes 4804
  4.6 4.0 %copy-start.11 = (s32[4,256]{1,0:T(4,128)S(1)}, s32[4,256]{1,0:T(4,128)}, u32[]{:S(2)}) copy-start(s32[4,256]{1,0:T(4,128)} %index_ref.1) | copy-start | bytes 12292
  4.6 4.0 %copy-start.12 = (s32[4,256]{1,0:T(4,128)S(1)}, s32[4,256]{1,0:T(4,128)}, u32[]{:S(2)}) copy-start(s32[4,256]{1,0:T(4,128)} %face_ref.1) | copy-start | bytes 12292
  4.6 4.0 %copy-start.14 = (f32[256]{0:T(256)S(1)}, f32[256]{0:T(256)}, u32[]{:S(2)}) copy-start(f32[256]{0:T(256)} %param.31) | copy-start | bytes 3076
  4.6 4.0 %copy-start.15 = (s32[1,256]{1,0:T(1,128)S(1)}, s32[1,256]{1,0:T(1,128)}, u32[]{:S(2)}) copy-start(s32[1,256]{1,0:T(1,128)} %damage_ref.1) | copy-start | bytes 3076
  4.7 4.0 %copy-start.9 = (f32[20,20]{1,0:T(8,128)S(1)}, f32[20,20]{1,0:T(8,128)}, u32[]{:S(2)}) copy-start(f32[20,20]{1,0:T(8,128)} %to_ref.1) | copy-start | bytes 4804
  4.7 8.6 %collective-permute-start.2 = (f32[180,128]{1,0:T(8,128)S(1)}, f32[180,128]{1,0:T(8,128)S(1)}, u32[]{:S(2)}, u32[]{:S(2)}) collective-permute-start(f32[180,128]{1,0:T(8,128)S(1)} %broadcast_select_fusion.1), channel_id=1, source_target_pairs={{0,0},{1,1},{30,30},{31,31},{2,4},{4,2},{3,5},{5,3},{6,8},{8,6},{7... | collective-permute-start | bytes 276488 | tf_op jit(solution)/shard_map/ppermute | solution.py:479
  8.5 4.8 %collective-permute-start.3 = (f32[180,128]{1,0:T(8,128)S(1)}, f32[180,128]{1,0:T(8,128)S(1)}, u32[]{:S(2)}, u32[]{:S(2)}) collective-permute-start(f32[180,128]{1,0:T(8,128)S(1)} %collective-permute-done.even_ref), channel_id=1, source_target_pairs={{0,1},{1,0},{2,3},{3,2},{4,5},{5,4},{6,7},{7,6},{8,9},{9,8},{10,11... | collective-permute-start | bytes 276488 | tf_op jit(solution)/shard_map/ppermute | solution.py:481
  8.6 0.7 %copy-start.13 = (s32[256]{0:T(256)S(1)}, s32[256]{0:T(256)}, u32[]{:S(2)}) copy-start(s32[256]{0:T(256)} %param.26) | copy-start | bytes 3076
  16.0 1.7 %collective-permute-start.5 = (f32[180,128]{1,0:T(8,128)S(1)}, f32[180,128]{1,0:T(8,128)S(1)}, u32[]{:S(2)}, u32[]{:S(2)}) collective-permute-start(f32[180,128]{1,0:T(8,128)S(1)} %get-tuple-element.52.near_ref), channel_id=1, source_target_pairs={{0,1},{1,0},{2,3},{3,2},{4,5},{5,4},{6,7},{7,6},{8,9},{9,8},{10,11... | collective-permute-start | bytes 276488 | tf_op jit(solution)/shard_map/ppermute | solution.py:473
  16.4 5.1 %collective-permute-start.4 = (f32[180,128]{1,0:T(8,128)S(1)}, f32[180,128]{1,0:T(8,128)S(1)}, u32[]{:S(2)}, u32[]{:S(2)}) collective-permute-start(f32[180,128]{1,0:T(8,128)S(1)} %get-tuple-element.53), channel_id=1, source_target_pairs={{0,2},{1,3},{2,0},{3,1},{4,6},{5,7},{6,4},{7,5},{8,10},{9,11},{10,... | collective-permute-start | bytes 276488 | tf_op jit(solution)/shard_map/ppermute | solution.py:477
  17.7 8.3 %collective-permute-start.6 = (f32[180,128]{1,0:T(8,128)S(1)}, f32[180,128]{1,0:T(8,128)S(1)}, u32[]{:S(2)}, u32[]{:S(2)}) collective-permute-start(f32[180,128]{1,0:T(8,128)S(1)} %broadcast_select_fusion), channel_id=1, source_target_pairs={{0,0},{1,1},{30,30},{31,31},{2,4},{4,2},{3,5},{5,3},{6,8},{8,6},{7... | collective-permute-start | bytes 276488 | tf_op jit(solution)/shard_map/ppermute | solution.py:479
  21.5 4.5 %collective-permute-start.7 = (f32[180,128]{1,0:T(8,128)S(1)}, f32[180,128]{1,0:T(8,128)S(1)}, u32[]{:S(2)}, u32[]{:S(2)}) collective-permute-start(f32[180,128]{1,0:T(8,128)S(1)} %collective-permute-done.4.even_ref), channel_id=1, source_target_pairs={{0,1},{1,0},{2,3},{3,2},{4,5},{5,4},{6,7},{7,6},{8,9},{9,8},{10,11... | collective-permute-start | bytes 276488 | tf_op jit(solution)/shard_map/ppermute | solution.py:481

commit v7 on v6

--- a/solution.py
+++ b/solution.py
@@ -121,15 +121,17 @@
         out_ref[p, :, lanes] = x[p] + (w1 * first[p] + w2 * second[p])
 
 
-def pick_columns(b_ref, send, out_ref):
+def pick_columns(b_ref, send, near_ref, far_ref):
     elements = b_ref.shape[-1]
     both = split_rows(b_ref[...].reshape(NQ * R, elements))
     rows = lax.broadcasted_iota(jnp.int32, (elements, send.shape[-1]), 0).astype(F32)
     hot = jnp.where(rows == send, 1.0, 0.0).astype(BF16)
     out = dot(both, hot)
     out = out[: NQ * R] + out[NQ * R :]
-    for q in range(NQ):
-        out_ref[q * NB : (q + 1) * NB] = out[q * R : q * R + NB]
+    half = send.shape[-1] // 2
+    for q in range(NQ):
+        near_ref[q * NB : (q + 1) * NB] = out[q * R : q * R + NB, :half]
+        far_ref[q * NB : (q + 1) * NB] = out[q * R : q * R + NB, half:]
 
 
 def far_sides(source, index, face, w_ref, y_ref, base):
@@ -226,14 +228,13 @@
     count_out[...] = jnp.broadcast_to(count_ref[...], count_out.shape).astype(F32)
 
 
-def near_kernel(b_ref, lists_ref, near_ref, send_ref):
+def pick_kernel(b_ref, lists_ref, near_ref, far_ref, send_ref):
     send = send_columns(lists_ref.at[0])
     send_ref[...] = send
-    pick_columns(b_ref, send[:, : send.shape[-1] // 2], near_ref)
-
-
-def far_kernel(b_ref, send_ref, near_ref, far_ref, even_ref, flag_ref):
-    pick_columns(b_ref, send_ref[:, send_ref.shape[-1] // 2 :], far_ref)
+    pick_columns(b_ref, send, near_ref, far_ref)
+
+
+def route_kernel(near_ref, far_ref, even_ref, flag_ref):
     chip = (lax.axis_index("dom") // 2) % 2
     half = near_ref.shape[1] // 2
     side = lax.broadcasted_iota(jnp.int32, near_ref.shape, 1) // half
@@ -355,7 +356,7 @@
 
 def second_kernel(
     v_ref, dof_ref, near_ref, even_ref, odd_ref, cross_ref, wk_ref, send_ref, w_ref, table_ref, ms_ref, mn_ref,
-    state_ref, b_ref, near_out,
+    state_ref, b_ref, near_out, far_out,
 ):
     both = split_rows(ghost_source(near_ref, even_ref, odd_ref, cross_ref))
     index = ghost_index(table_ref, near_ref.shape[-1] // 2)
@@ -377,7 +378,7 @@
         yield from taylor_steps(x, wk, ms_ref, lanes, w1, w2, b_ref)
 
     in_turns(half(0), half(LANES), [FAR, [1] * 4 * NQ] + [[1] * NQ, [1] * 3 * NQ] * 2)
-    pick_columns(b_ref, send_ref[:, : send_ref.shape[-1] // 2], near_out)
+    pick_columns(b_ref, send_ref[...], near_out, far_out)
 
 
 def last_kernel(
@@ -469,11 +470,9 @@
     return route
 
 
-def exchange(near, buffer, send, total):
+def exchange(near, far, buffer, total):
     got = lax.ppermute(near, "dom", core_swap(total))
-    far, to_even, flag = call(
-        far_kernel, [buffer, send, near], (spec(near.shape), spec(near.shape), spec((8, near.shape[1]))), [], cost=0
-    )
+    to_even, flag = call(route_kernel, [near, far], (spec(near.shape), spec((8, near.shape[1]))), [])
     even = lax.ppermute(to_even, "dom", even_chip_swap(total))
     to_odd = jnp.where(flag[:1] > 0.5, far, got)
     odd = lax.ppermute(to_odd, "dom", odd_chip_swap(total))
@@ -529,8 +528,8 @@
         [((3 * R, LANES), F32)],
     )
     buffer_one, ms = call(predict_kernel, [dof_values, star, wk], (field, m_o(3)), [])
-    near, send = call(near_kernel, [buffer_one, send_list], (block, spec((1, 4 * ghosts))), [])
-    near, even, odd, cross, buffer_one = exchange(near, buffer_one, send, total)
+    near, far, send = call(pick_kernel, [buffer_one, send_list], (block, block, spec((1, 4 * ghosts))), [])
+    near, even, odd, cross, buffer_one = exchange(near, far, buffer_one, total)
     started, ml, mn, table, weights = call(
         local_kernel,
         [
@@ -542,13 +541,13 @@
         [((W_ROWS, LANES), F32), y_s(11)],
         cost=1_000_000_000,
     )
-    updated, buffer_two, near = call(
+    updated, buffer_two, near, far = call(
         second_kernel,
         [started, dof_values, near, even, odd, cross, wk, send, weights, table, ms, mn],
-        (field, field, block),
+        (field, field, block, block),
         [],
     )
-    near, even, odd, cross, buffer_two = exchange(near, buffer_two, send, total)
+    near, even, odd, cross, buffer_two = exchange(near, far, buffer_two, total)
     started, mask = call(
         again_kernel,
         [updated, buffer_two, weights, table, ms, ml, mn],

time: 28.7 us -> 28.4 us (0.990)
  starting transfers between devices: 10.5 us -> 11.1 us
  waiting for transfers between devices: 2.07 us -> 1.63 us
  Pallas kernels: 13.9 us -> 13.5 us
    pallas_call x10, Pallas kernels: 13.9 us -> 13.5 us  [call(): pl.pallas_call(kernel, out_shape=outputs, in_specs=[VMEM] * len(inputs),...]
    ppermute x2, starting transfers between devices: 7.34 us -> 7.71 us  [exchange(): odd = lax.ppermute(to_odd, 'dom', odd_chip_swap(total))]
  transfers between devices with their start and end apart: 8 -> 8, of which waited for: 3 -> 2; matrix products, arithmetic and copies ran while one was open for 0% -> 0% of each run, Pallas kernels for 25% -> 24%
where the time goes in v7:
time: 28.4 us; the launch traced here: 28.2 us
  Pallas kernels  13.5 us (48%)
  starting transfers between devices  11.1 us (39%)
  waiting for transfers between devices  1.63 us (6%)
  between operations  1.2 us (4%)
  local copies, waits for them, and re-layouts  0.81 us (3%)
    pallas_call x10, Pallas kernels, call(): pl.pallas_call(kernel, out_shape=outputs, in_specs=[VMEM] * len(inputs),...  13.5 us
    ppermute x2, starting transfers between devices, exchange(): odd = lax.ppermute(to_odd, 'dom', odd_chip_swap(total))  7.71 us
    ppermute x2, starting transfers between devices, exchange(): even = lax.ppermute(to_even, 'dom', even_chip_swap(total))  2.69 us
    ppermute x2, waiting for transfers between devices, exchange(): odd = lax.ppermute(to_odd, 'dom', odd_chip_swap(total))  1.61 us
    unnamed x32, local copies, waits for them, and re-layouts  0.81 us
  transfers between devices with their start and end apart: 8, of which 2 were waited for; matrix products, arithmetic and copies ran while one was open for 0% of the time, Pallas kernels for 24%

profile of v7, /device:TPU:24, one launch (start us, length us, event | category | flops | bytes accessed | tf_op | source)
XLA Modules:
  0.0 28.2 jit_solution(18039316243587449992)
XLA Ops:
  0.7 0.0 copy-done.2
  0.8 0.2 shard_map.164
  0.9 0.1 copy-done
  1.0 0.1 copy-done.1
  1.1 1.2 %shard_map.165 = (f32[9,24,256]{2,1,0:T(8,128)S(1)}, f32[81,3,256]{2,1,0:T(4,128)S(1)}) custom-call(f32[9,20,256]{2,1,0:T(8,128)S(1)} %copy-done, bf16[9,9,3,256]{3,2,1,0:T(4,128)(2,1)S(1)} %bitcast.13, bf16[72,72]{1,0:T(8,128)(2,1)S(1)} %get-tuple-element.35.wk_ref), custom_call_target="tpu_custom_call" | custom-call | bytes 1048576 | tf_op jit(solution)/shard_map/pallas_call | solution.py:446
  2.3 0.0 copy-start.7
  2.3 0.0 copy-start.9
  2.3 0.0 copy-start.10
  2.4 0.4 %shard_map.166 = (f32[180,128]{1,0:T(8,128)S(1)}, f32[180,128]{1,0:T(8,128)S(1)}, f32[1,256]{1,0:T(1,128)S(1)}) custom-call(f32[9,24,256]{2,1,0:T(8,128)S(1)} %get-tuple-element.41.b_ref, s32[1,4,64]{2,1,0:T(4,128)S(1)} %copy-done.3), custom_call_target="tpu_custom_call" | custom-call | bytes 1048576 | tf_op jit(solution)/shard_map/pallas_call | solution.py:446
  2.8 0.1 collective-permute-start.1
  2.9 1.6 %collective-permute-start = (f32[180,128]{1,0:T(8,128)S(1)}, f32[180,128]{1,0:T(8,128)S(1)}, u32[]{:S(2)}, u32[]{:S(2)}) collective-permute-start(f32[180,128]{1,0:T(8,128)S(1)} %get-tuple-element.39), channel_id=1, source_target_pairs={{0,2},{1,3},{2,0},{3,1},{4,6},{5,7},{6,4},{7,5},{8,10},{9,11},{10,... | collective-permute-start | bytes 276488 | tf_op jit(solution)/shard_map/ppermute | solution.py:476
  4.5 3.9 %collective-permute-start.2 = (f32[180,128]{1,0:T(8,128)S(1)}, f32[180,128]{1,0:T(8,128)S(1)}, u32[]{:S(2)}, u32[]{:S(2)}) collective-permute-start(f32[180,128]{1,0:T(8,128)S(1)} %broadcast_select_fusion.1), channel_id=1, source_target_pairs={{0,0},{1,1},{30,30},{31,31},{2,4},{4,2},{3,5},{5,3},{6,8},{8,6},{7... | collective-permute-start | bytes 276488 | tf_op jit(solution)/shard_map/ppermute | solution.py:478
  8.4 0.1 collective-permute-start.3
  8.6 0.6 %copy-done.13 = s32[256]{0:T(256)S(1)} copy-done((s32[256]{0:T(256)S(1)}, s32[256]{0:T(256)}, u32[]{:S(2)}) %copy-start.13) | copy-done | bytes 1048
  9.2 3.6 %shard_map.168 = (f32[9,24,256]{2,1,0:T(8,128)S(1)}, f32[81,4,256]{2,1,0:T(4,128)S(1)}, f32[81,4,256]{2,1,0:T(4,128)S(1)}, f32[40,256]{1,0:T(8,128)S(1)}, bf16[600,72]{1,0:T(8,128)(2,1)S(1)}) custom-call(f32[9,20,256]{2,1,0:T(8,128)S(1)} %copy-done, f32[9,24,256]{2,1,0:T(8,128)S(1)} %get-tuple-element.41.b_ref, f32[81,3,256]{2,1,0:T(4,128)S(1)} %get-tuple-element.42.ms_ref, ...), custom_call_target="tpu_custom_call" | custom-call | flops 1000000000 | bytes 1048576 | tf_op jit(solution)/shard_map/pallas_call | solution.py:446
  12.8 0.2 collective-permute-done.2.odd_ref
  13.0 2.7 %shard_map.169 = (f32[9,24,256]{2,1,0:T(8,128)S(1)}, f32[9,24,256]{2,1,0:T(8,128)S(1)}, f32[180,128]{1,0:T(8,128)S(1)}, f32[180,128]{1,0:T(8,128)S(1)}) custom-call(f32[9,24,256]{2,1,0:T(8,128)S(1)} %get-tuple-element.44.v_ref, f32[9,20,256]{2,1,0:T(8,128)S(1)} %copy-done, f32[180,128]{1,0:T(8,128)S(1)} %collective-permute-done.1.near_ref, ...), custom_call_target="tpu_custom_call" | custom-call | bytes 1048576 | tf_op jit(solution)/shard_map/pallas_call | solution.py:446
  15.7 0.4 %collective-permute-start.5 = (f32[180,128]{1,0:T(8,128)S(1)}, f32[180,128]{1,0:T(8,128)S(1)}, u32[]{:S(2)}, u32[]{:S(2)}) collective-permute-start(f32[180,128]{1,0:T(8,128)S(1)} %get-tuple-element.52.near_ref), channel_id=1, source_target_pairs={{0,1},{1,0},{2,3},{3,2},{4,5},{5,4},{6,7},{7,6},{8,9},{9,8},{10,11... | collective-permute-start | bytes 276488 | tf_op jit(solution)/shard_map/ppermute | solution.py:474
  16.1 1.1 %collective-permute-start.4 = (f32[180,128]{1,0:T(8,128)S(1)}, f32[180,128]{1,0:T(8,128)S(1)}, u32[]{:S(2)}, u32[]{:S(2)}) collective-permute-start(f32[180,128]{1,0:T(8,128)S(1)} %get-tuple-element.54), channel_id=1, source_target_pairs={{0,2},{1,3},{2,0},{3,1},{4,6},{5,7},{6,4},{7,5},{8,10},{9,11},{10,... | collective-permute-start | bytes 276488 | tf_op jit(solution)/shard_map/ppermute | solution.py:476
  17.3 3.8 %collective-permute-start.6 = (f32[180,128]{1,0:T(8,128)S(1)}, f32[180,128]{1,0:T(8,128)S(1)}, u32[]{:S(2)}, u32[]{:S(2)}) collective-permute-start(f32[180,128]{1,0:T(8,128)S(1)} %broadcast_select_fusion), channel_id=1, source_target_pairs={{0,0},{1,1},{30,30},{31,31},{2,4},{4,2},{3,5},{5,3},{6,8},{8,6},{7... | collective-permute-start | bytes 276488 | tf_op jit(solution)/shard_map/ppermute | solution.py:478
  21.1 0.1 collective-permute-start.7
  21.2 3.0 %shard_map.171 = (f32[9,24,256]{2,1,0:T(8,128)S(1)}, f32[24,256]{1,0:T(8,128)S(1)}) custom-call(f32[9,24,256]{2,1,0:T(8,128)S(1)} %get-tuple-element.50.base_ref, f32[9,24,256]{2,1,0:T(8,128)S(1)} %get-tuple-element.56.b_ref, bf16[600,72]{1,0:T(8,128)(2,1)S(1)} %get-tuple-element.47.w_ref, f32[40,256]{1,0:T(8,128)S(1)} %get-tuple-element.48.table_ref, ...), custom_call_target="tpu_custom_call" | custom-call | flops 1000000000 | bytes 1048576 | tf_op jit(solution)/shard_map/pallas_call | solution.py:446
  24.3 1.4 %collective-permute-done.6.odd_ref = f32[180,128]{1,0:T(8,128)S(1)} collective-permute-done((f32[180,128]{1,0:T(8,128)S(1)}, f32[180,128]{1,0:T(8,128)S(1)}, u32[]{:S(2)}, u32[]{:S(2)}) %collective-permute-start.6) | collective-permute-done | bytes 92192 | tf_op jit(solution)/shard_map/ppermute | solution.py:478
  25.7 2.4 %shard_map.172 = f32[9,20,256]{2,1,0:T(8,128)} custom-call(f32[9,24,256]{2,1,0:T(8,128)S(1)} %get-tuple-element.58.v_ref, f32[180,128]{1,0:T(8,128)S(1)} %collective-permute-done.5.near_ref, f32[180,128]{1,0:T(8,128)S(1)} %collective-permute-done.4.even_ref, f32[180,128]{1,0:T(8,128)S(1)} %collective-permute-done.6.odd_ref, ...), custom_call_target="tpu_custom_call" | custom-call | bytes 1048576 | tf_op jit(solution)/shard_map/pallas_call | solution.py:446
  (38 shorter events, 0.2 us)
Async XLA Ops:
  0.0 0.8 %copy-start.2 = (f32[3,20,20]{2,1,0:T(8,128)S(1)}, f32[3,20,20]{2,1,0:T(8,128)}, u32[]{:S(2)}) copy-start(f32[3,20,20]{2,1,0:T(8,128)} %kstiff_ref.3) | copy-start | bytes 14404
  0.0 1.0 %copy-start = (f32[9,20,256]{2,1,0:T(8,128)S(1)}, f32[9,20,256]{2,1,0:T(8,128)}, u32[]{:S(2)}) copy-start(f32[9,20,256]{2,1,0:T(8,128)} %dof_ref.5) | copy-start | bytes 552964
  0.0 1.1 %copy-start.1 = (bf16[3,9,9,256]{3,0,2,1:T(4,128)(2,1)S(1)}, bf16[3,9,9,256]{3,0,2,1:T(4,128)(2,1)}, u32[]{:S(2)}) copy-start(bf16[3,9,9,256]{3,0,2,1:T(4,128)(2,1)} %param.18) | copy-start | bytes 373252
  1.1 1.2 %copy-start.3 = (s32[1,4,64]{2,1,0:T(4,128)S(1)}, s32[1,4,64]{2,1,0:T(4,128)}, u32[]{:S(2)}) copy-start(s32[1,4,64]{2,1,0:T(4,128)} %lists_ref.1) | copy-start | bytes 3076
  2.3 6.2 %copy-start.7 = (f32[4,20,20]{2,0,1:T(4,128)S(1)}, f32[4,20,20]{2,0,1:T(4,128)}, u32[]{:S(2)}) copy-start(f32[4,20,20]{2,0,1:T(4,128)} %param.22) | copy-start | bytes 19204
  2.3 6.2 %copy-start.8 = (s32[20,256]{1,0:T(8,128)S(1)}, s32[20,256]{1,0:T(8,128)}, u32[]{:S(2)}) copy-start(s32[20,256]{1,0:T(8,128)} %yield_ref.1) | copy-start | bytes 61444
  2.3 6.2 %copy-start.9 = (f32[20,20]{1,0:T(8,128)S(1)}, f32[20,20]{1,0:T(8,128)}, u32[]{:S(2)}) copy-start(f32[20,20]{1,0:T(8,128)} %to_ref.1) | copy-start | bytes 4804
  2.3 6.2 %copy-start.10 = (f32[20,20]{1,0:T(8,128)S(1)}, f32[20,20]{1,0:T(8,128)}, u32[]{:S(2)}) copy-start(f32[20,20]{1,0:T(8,128)} %from_ref.1) | copy-start | bytes 4804
  2.3 6.2 %copy-start.11 = (s32[4,256]{1,0:T(4,128)S(1)}, s32[4,256]{1,0:T(4,128)}, u32[]{:S(2)}) copy-start(s32[4,256]{1,0:T(4,128)} %index_ref.1) | copy-start | bytes 12292
  2.4 6.2 %copy-start.12 = (s32[4,256]{1,0:T(4,128)S(1)}, s32[4,256]{1,0:T(4,128)}, u32[]{:S(2)}) copy-start(s32[4,256]{1,0:T(4,128)} %face_ref.1) | copy-start | bytes 12292
  2.4 6.2 %copy-start.14 = (f32[256]{0:T(256)S(1)}, f32[256]{0:T(256)}, u32[]{:S(2)}) copy-start(f32[256]{0:T(256)} %param.31) | copy-start | bytes 3076
  2.4 6.2 %copy-start.15 = (s32[1,256]{1,0:T(1,128)S(1)}, s32[1,256]{1,0:T(1,128)}, u32[]{:S(2)}) copy-start(s32[1,256]{1,0:T(1,128)} %damage_ref.1) | copy-start | bytes 3076
  2.8 5.8 %copy-start.6 = (f32[4,4,20,20]{3,1,2,0:T(4,128)S(1)}, f32[4,4,20,20]{3,1,2,0:T(4,128)}, u32[]{:S(2)}) copy-start(f32[4,4,20,20]{3,1,2,0:T(4,128)} %param.23) | copy-start | bytes 76804
  2.8 1.7 %collective-permute-start.1 = (f32[180,128]{1,0:T(8,128)S(1)}, f32[180,128]{1,0:T(8,128)S(1)}, u32[]{:S(2)}, u32[]{:S(2)}) collective-permute-start(f32[180,128]{1,0:T(8,128)S(1)} %get-tuple-element.37.near_ref), channel_id=1, source_target_pairs={{0,1},{1,0},{2,3},{3,2},{4,5},{5,4},{6,7},{7,6},{8,9},{9,8},{10,11... | collective-permute-start | bytes 276488 | tf_op jit(solution)/shard_map/ppermute | solution.py:474
  2.9 5.7 %copy-start.5 = (bf16[4,9,9,256]{3,0,2,1:T(4,128)(2,1)S(1)}, bf16[4,9,9,256]{3,0,2,1:T(4,128)(2,1)}, u32[]{:S(2)}) copy-start(bf16[4,9,9,256]{3,0,2,1:T(4,128)(2,1)} %param.20) | copy-start | bytes 497668
  2.9 5.7 %copy-start.4 = (bf16[4,9,9,256]{3,0,2,1:T(4,128)(2,1)S(1)}, bf16[4,9,9,256]{3,0,2,1:T(4,128)(2,1)}, u32[]{:S(2)}) copy-start(bf16[4,9,9,256]{3,0,2,1:T(4,128)(2,1)} %param.19) | copy-start | bytes 497668
  2.9 5.5 %collective-permute-start = (f32[180,128]{1,0:T(8,128)S(1)}, f32[180,128]{1,0:T(8,128)S(1)}, u32[]{:S(2)}, u32[]{:S(2)}) collective-permute-start(f32[180,128]{1,0:T(8,128)S(1)} %get-tuple-element.39), channel_id=1, source_target_pairs={{0,2},{1,3},{2,0},{3,1},{4,6},{5,7},{6,4},{7,5},{8,10},{9,11},{10,... | collective-permute-start | bytes 276488 | tf_op jit(solution)/shard_map/ppermute | solution.py:476
  4.5 8.5 %collective-permute-start.2 = (f32[180,128]{1,0:T(8,128)S(1)}, f32[180,128]{1,0:T(8,128)S(1)}, u32[]{:S(2)}, u32[]{:S(2)}) collective-permute-start(f32[180,128]{1,0:T(8,128)S(1)} %broadcast_select_fusion.1), channel_id=1, source_target_pairs={{0,0},{1,1},{30,30},{31,31},{2,4},{4,2},{3,5},{5,3},{6,8},{8,6},{7... | collective-permute-start | bytes 276488 | tf_op jit(solution)/shard_map/ppermute | solution.py:478
  8.4 4.4 %collective-permute-start.3 = (f32[180,128]{1,0:T(8,128)S(1)}, f32[180,128]{1,0:T(8,128)S(1)}, u32[]{:S(2)}, u32[]{:S(2)}) collective-permute-start(f32[180,128]{1,0:T(8,128)S(1)} %collective-permute-done.even_ref), channel_id=1, source_target_pairs={{0,1},{1,0},{2,3},{3,2},{4,5},{5,4},{6,7},{7,6},{8,9},{9,8},{10,11... | collective-permute-start | bytes 276488 | tf_op jit(solution)/shard_map/ppermute | solution.py:480
  8.5 0.7 %copy-start.13 = (s32[256]{0:T(256)S(1)}, s32[256]{0:T(256)}, u32[]{:S(2)}) copy-start(s32[256]{0:T(256)} %param.26) | copy-start | bytes 3076
  15.7 1.6 %collective-permute-start.5 = (f32[180,128]{1,0:T(8,128)S(1)}, f32[180,128]{1,0:T(8,128)S(1)}, u32[]{:S(2)}, u32[]{:S(2)}) collective-permute-start(f32[180,128]{1,0:T(8,128)S(1)} %get-tuple-element.52.near_ref), channel_id=1, source_target_pairs={{0,1},{1,0},{2,3},{3,2},{4,5},{5,4},{6,7},{7,6},{8,9},{9,8},{10,11... | collective-permute-start | bytes 276488 | tf_op jit(solution)/shard_map/ppermute | solution.py:474
  16.1 5.0 %collective-permute-start.4 = (f32[180,128]{1,0:T(8,128)S(1)}, f32[180,128]{1,0:T(8,128)S(1)}, u32[]{:S(2)}, u32[]{:S(2)}) collective-permute-start(f32[180,128]{1,0:T(8,128)S(1)} %get-tuple-element.54), channel_id=1, source_target_pairs={{0,2},{1,3},{2,0},{3,1},{4,6},{5,7},{6,4},{7,5},{8,10},{9,11},{10,... | collective-permute-start | bytes 276488 | tf_op jit(solution)/shard_map/ppermute | solution.py:476
  17.3 8.4 %collective-permute-start.6 = (f32[180,128]{1,0:T(8,128)S(1)}, f32[180,128]{1,0:T(8,128)S(1)}, u32[]{:S(2)}, u32[]{:S(2)}) collective-permute-start(f32[180,128]{1,0:T(8,128)S(1)} %broadcast_select_fusion), channel_id=1, source_target_pairs={{0,0},{1,1},{30,30},{31,31},{2,4},{4,2},{3,5},{5,3},{6,8},{8,6},{7... | collective-permute-start | bytes 276488 | tf_op jit(solution)/shard_map/ppermute | solution.py:478
  21.1 3.1 %collective-permute-start.7 = (f32[180,128]{1,0:T(8,128)S(1)}, f32[180,128]{1,0:T(8,128)S(1)}, u32[]{:S(2)}, u32[]{:S(2)}) collective-permute-start(f32[180,128]{1,0:T(8,128)S(1)} %collective-permute-done.4.even_ref), channel_id=1, source_target_pairs={{0,1},{1,0},{2,3},{3,2},{4,5},{5,4},{6,7},{7,6},{8,9},{9,8},{10,11... | collective-permute-start | bytes 276488 | tf_op jit(solution)/shard_map/ppermute | solution.py:480

commit v8 on v7

--- a/solution.py
+++ b/solution.py
@@ -38,22 +38,13 @@
             y_ref[base + k, q] = out[k * R : (k + 1) * R]
 
 
-def star_sum(y_ref, m_refs, lanes, start):
-    acc = list(start)
-    for q in range(NQ):
-        k = 0
-        for m_ref in m_refs:
-            for row in range(m_ref.shape[1]):
-                y = y_ref[k, q, :, lanes]
-                for p in range(NQ):
-                    acc[p] = acc[p] + y * m_ref[q * NQ + p, row : row + 1, lanes]
-                k += 1
+def star_add(acc, y_ref, k, m_ref, row, lanes):
+    acc = list(acc)
+    for q in range(NQ):
+        y = y_ref[k, q, :, lanes]
+        for p in range(NQ):
+            acc[p] = acc[p] + y * m_ref[q * NQ + p, row : row + 1, lanes]
     return acc
-
-
-def each_half(elements, body):
-    for start in range(0, elements, LANES):
-        body(pl.ds(start, LANES))
 
 
 def in_turns(one, two, stages):
@@ -134,7 +125,7 @@
         far_ref[q * NB : (q + 1) * NB] = out[q * R : q * R + NB, half:]
 
 
-def far_sides(source, index, face, w_ref, y_ref, base):
+def far_sides(source, index, face, w_ref, y_ref, base, between):
     high = source.astype(BF16)
     low = (source - high.astype(F32)).astype(BF16)
     both = jnp.concatenate([high, low], axis=0)
@@ -157,6 +148,7 @@
                 jnp.where(kind == 0, out[:R], out[R : 2 * R]),
                 jnp.where(kind == 2, out[2 * R : 3 * R], out[3 * R :]),
             )
+        between(f)
 
 
 def place_kernel(twice_ref, once_ref):
@@ -269,14 +261,23 @@
     elements = b_ref.shape[-1]
     basis_products(w_ref[W_OWN:W_FAR], b_ref, y_ref, 7)
     source = b_ref[...].reshape(NQ * R, elements)
-    far_sides(source, table_ref[NEIGHBOUR : NEIGHBOUR + 4], table_ref[FACE : FACE + 4], w_ref, y_ref, 7)
-
-    def body(lanes):
-        acc = star_sum(y_ref, [ms_ref, ml_ref, mn_ref], lanes, [start(p, lanes) for p in range(NQ)])
+    halves = [pl.ds(at, LANES) for at in range(0, elements, LANES)]
+    acc = [[start(p, lanes) for p in range(NQ)] for lanes in halves]
+
+    def add(k, m_ref, row):
+        for i, lanes in enumerate(halves):
+            acc[i] = star_add(acc[i], y_ref, k, m_ref, row, lanes)
+
+    def between(f):
+        for k in ((0, 1), (2, 3), (4, 5), (6,))[f]:
+            add(k, ms_ref if k < 3 else ml_ref, k if k < 3 else k - 3)
+
+    far_sides(source, table_ref[NEIGHBOUR : NEIGHBOUR + 4], table_ref[FACE : FACE + 4], w_ref, y_ref, 7, between)
+    for f in range(4):
+        add(7 + f, mn_ref, f)
+    for i, lanes in enumerate(halves):
         for p in range(NQ):
-            out_ref[p, :, lanes] = acc[p]
-
-    each_half(elements, body)
+            out_ref[p, :, lanes] = acc[i][p]
 
 
 def padded(ref, p, lanes):

time: 28.4 us -> 28.2 us (level)
  Pallas kernels: 13.5 us -> 13.2 us
    pallas_call x10, Pallas kernels: 13.5 us -> 13.2 us  [call(): pl.pallas_call(kernel, out_shape=outputs, in_specs=[VMEM] * len(inputs),...]
  transfers between devices with their start and end apart: 8 -> 8, of which waited for: 2 -> 2; matrix products, arithmetic and copies ran while one was open for 0% -> 0% of each run, Pallas kernels for 24% -> 23%
where the time goes in v8:
time: 28.2 us; the launch traced here: 28.1 us
  Pallas kernels  13.2 us (47%)
  starting transfers between devices  11 us (39%)
  waiting for transfers between devices  1.81 us (6%)
  between operations  1.2 us (4%)
  local copies, waits for them, and re-layouts  0.81 us (3%)
    pallas_call x10, Pallas kernels, call(): pl.pallas_call(kernel, out_shape=outputs, in_specs=[VMEM] * len(inputs),...  13.2 us
    ppermute x2, starting transfers between devices, exchange(): odd = lax.ppermute(to_odd, 'dom', odd_chip_swap(total))  7.87 us
    ppermute x2, starting transfers between devices, exchange(): even = lax.ppermute(to_even, 'dom', even_chip_swap(total))  2.7 us
    ppermute x2, waiting for transfers between devices, exchange(): odd = lax.ppermute(to_odd, 'dom', odd_chip_swap(total))  1.79 us
    unnamed x32, local copies, waits for them, and re-layouts  0.81 us
  transfers between devices with their start and end apart: 8, of which 2 were waited for; matrix products, arithmetic and copies ran while one was open for 0% of the time, Pallas kernels for 23%

profile of v8, /device:TPU:24, one launch (start us, length us, event | category | flops | bytes accessed | tf_op | source)
XLA Modules:
  0.0 28.1 jit_solution(8727582951982876929)
XLA Ops:
  0.7 0.0 copy-done.2
  0.8 0.2 shard_map.164
  0.9 0.1 copy-done
  1.0 0.1 copy-done.1
  1.1 1.2 %shard_map.165 = (f32[9,24,256]{2,1,0:T(8,128)S(1)}, f32[81,3,256]{2,1,0:T(4,128)S(1)}) custom-call(f32[9,20,256]{2,1,0:T(8,128)S(1)} %copy-done, bf16[9,9,3,256]{3,2,1,0:T(4,128)(2,1)S(1)} %bitcast.13, bf16[72,72]{1,0:T(8,128)(2,1)S(1)} %get-tuple-element.35.wk_ref), custom_call_target="tpu_custom_call" | custom-call | bytes 1048576 | tf_op jit(solution)/shard_map/pallas_call | solution.py:447
  2.3 0.0 copy-start.7
  2.3 0.0 copy-start.8
  2.3 0.0 copy-start.11
  2.4 0.4 %shard_map.166 = (f32[180,128]{1,0:T(8,128)S(1)}, f32[180,128]{1,0:T(8,128)S(1)}, f32[1,256]{1,0:T(1,128)S(1)}) custom-call(f32[9,24,256]{2,1,0:T(8,128)S(1)} %get-tuple-element.41.b_ref, s32[1,4,64]{2,1,0:T(4,128)S(1)} %copy-done.3), custom_call_target="tpu_custom_call" | custom-call | bytes 1048576 | tf_op jit(solution)/shard_map/pallas_call | solution.py:447
  2.8 0.1 collective-permute-start.1
  2.9 1.6 %collective-permute-start = (f32[180,128]{1,0:T(8,128)S(1)}, f32[180,128]{1,0:T(8,128)S(1)}, u32[]{:S(2)}, u32[]{:S(2)}) collective-permute-start(f32[180,128]{1,0:T(8,128)S(1)} %get-tuple-element.39), channel_id=1, source_target_pairs={{0,2},{1,3},{2,0},{3,1},{4,6},{5,7},{6,4},{7,5},{8,10},{9,11},{10,... | collective-permute-start | bytes 276488 | tf_op jit(solution)/shard_map/ppermute | solution.py:477
  4.5 3.9 %collective-permute-start.2 = (f32[180,128]{1,0:T(8,128)S(1)}, f32[180,128]{1,0:T(8,128)S(1)}, u32[]{:S(2)}, u32[]{:S(2)}) collective-permute-start(f32[180,128]{1,0:T(8,128)S(1)} %broadcast_select_fusion.1), channel_id=1, source_target_pairs={{0,0},{1,1},{30,30},{31,31},{2,4},{4,2},{3,5},{5,3},{6,8},{8,6},{7... | collective-permute-start | bytes 276488 | tf_op jit(solution)/shard_map/ppermute | solution.py:479
  8.4 0.1 collective-permute-start.3
  8.6 0.6 %copy-done.13 = s32[256]{0:T(256)S(1)} copy-done((s32[256]{0:T(256)S(1)}, s32[256]{0:T(256)}, u32[]{:S(2)}) %copy-start.13) | copy-done | bytes 1048
  9.2 3.5 %shard_map.168 = (f32[9,24,256]{2,1,0:T(8,128)S(1)}, f32[81,4,256]{2,1,0:T(4,128)S(1)}, f32[81,4,256]{2,1,0:T(4,128)S(1)}, f32[40,256]{1,0:T(8,128)S(1)}, bf16[600,72]{1,0:T(8,128)(2,1)S(1)}) custom-call(f32[9,20,256]{2,1,0:T(8,128)S(1)} %copy-done, f32[9,24,256]{2,1,0:T(8,128)S(1)} %get-tuple-element.41.b_ref, f32[81,3,256]{2,1,0:T(4,128)S(1)} %get-tuple-element.42.ms_ref, ...), custom_call_target="tpu_custom_call" | custom-call | flops 1000000000 | bytes 1048576 | tf_op jit(solution)/shard_map/pallas_call | solution.py:447
  12.7 0.3 %collective-permute-done.2.odd_ref = f32[180,128]{1,0:T(8,128)S(1)} collective-permute-done((f32[180,128]{1,0:T(8,128)S(1)}, f32[180,128]{1,0:T(8,128)S(1)}, u32[]{:S(2)}, u32[]{:S(2)}) %collective-permute-start.2) | collective-permute-done | bytes 92192 | tf_op jit(solution)/shard_map/ppermute | solution.py:479
  13.0 2.7 %shard_map.169 = (f32[9,24,256]{2,1,0:T(8,128)S(1)}, f32[9,24,256]{2,1,0:T(8,128)S(1)}, f32[180,128]{1,0:T(8,128)S(1)}, f32[180,128]{1,0:T(8,128)S(1)}) custom-call(f32[9,24,256]{2,1,0:T(8,128)S(1)} %get-tuple-element.44.v_ref, f32[9,20,256]{2,1,0:T(8,128)S(1)} %copy-done, f32[180,128]{1,0:T(8,128)S(1)} %collective-permute-done.1.near_ref, ...), custom_call_target="tpu_custom_call" | custom-call | bytes 1048576 | tf_op jit(solution)/shard_map/pallas_call | solution.py:447
  15.7 0.2 collective-permute-start.5
  16.0 1.1 %collective-permute-start.4 = (f32[180,128]{1,0:T(8,128)S(1)}, f32[180,128]{1,0:T(8,128)S(1)}, u32[]{:S(2)}, u32[]{:S(2)}) collective-permute-start(f32[180,128]{1,0:T(8,128)S(1)} %get-tuple-element.54), channel_id=1, source_target_pairs={{0,2},{1,3},{2,0},{3,1},{4,6},{5,7},{6,4},{7,5},{8,10},{9,11},{10,... | collective-permute-start | bytes 276488 | tf_op jit(solution)/shard_map/ppermute | solution.py:477
  17.1 4.0 %collective-permute-start.6 = (f32[180,128]{1,0:T(8,128)S(1)}, f32[180,128]{1,0:T(8,128)S(1)}, u32[]{:S(2)}, u32[]{:S(2)}) collective-permute-start(f32[180,128]{1,0:T(8,128)S(1)} %broadcast_select_fusion), channel_id=1, source_target_pairs={{0,0},{1,1},{30,30},{31,31},{2,4},{4,2},{3,5},{5,3},{6,8},{8,6},{7... | collective-permute-start | bytes 276488 | tf_op jit(solution)/shard_map/ppermute | solution.py:479
  21.1 0.1 collective-permute-start.7
  21.2 2.9 %shard_map.171 = (f32[9,24,256]{2,1,0:T(8,128)S(1)}, f32[24,256]{1,0:T(8,128)S(1)}) custom-call(f32[9,24,256]{2,1,0:T(8,128)S(1)} %get-tuple-element.50.base_ref, f32[9,24,256]{2,1,0:T(8,128)S(1)} %get-tuple-element.56.b_ref, bf16[600,72]{1,0:T(8,128)(2,1)S(1)} %get-tuple-element.47.w_ref, f32[40,256]{1,0:T(8,128)S(1)} %get-tuple-element.48.table_ref, ...), custom_call_target="tpu_custom_call" | custom-call | flops 1000000000 | bytes 1048576 | tf_op jit(solution)/shard_map/pallas_call | solution.py:447
  24.1 1.5 %collective-permute-done.6.odd_ref = f32[180,128]{1,0:T(8,128)S(1)} collective-permute-done((f32[180,128]{1,0:T(8,128)S(1)}, f32[180,128]{1,0:T(8,128)S(1)}, u32[]{:S(2)}, u32[]{:S(2)}) %collective-permute-start.6) | collective-permute-done | bytes 92192 | tf_op jit(solution)/shard_map/ppermute | solution.py:479
  25.5 2.4 %shard_map.172 = f32[9,20,256]{2,1,0:T(8,128)} custom-call(f32[9,24,256]{2,1,0:T(8,128)S(1)} %get-tuple-element.58.v_ref, f32[180,128]{1,0:T(8,128)S(1)} %collective-permute-done.5.near_ref, f32[180,128]{1,0:T(8,128)S(1)} %collective-permute-done.4.even_ref, f32[180,128]{1,0:T(8,128)S(1)} %collective-permute-done.6.odd_ref, ...), custom_call_target="tpu_custom_call" | custom-call | bytes 1048576 | tf_op jit(solution)/shard_map/pallas_call | solution.py:447
  (38 shorter events, 0.2 us)
Async XLA Ops:
  0.0 0.8 %copy-start.2 = (f32[3,20,20]{2,1,0:T(8,128)S(1)}, f32[3,20,20]{2,1,0:T(8,128)}, u32[]{:S(2)}) copy-start(f32[3,20,20]{2,1,0:T(8,128)} %kstiff_ref.3) | copy-start | bytes 14404
  0.0 1.0 %copy-start = (f32[9,20,256]{2,1,0:T(8,128)S(1)}, f32[9,20,256]{2,1,0:T(8,128)}, u32[]{:S(2)}) copy-start(f32[9,20,256]{2,1,0:T(8,128)} %dof_ref.5) | copy-start | bytes 552964
  0.0 1.1 %copy-start.1 = (bf16[3,9,9,256]{3,0,2,1:T(4,128)(2,1)S(1)}, bf16[3,9,9,256]{3,0,2,1:T(4,128)(2,1)}, u32[]{:S(2)}) copy-start(bf16[3,9,9,256]{3,0,2,1:T(4,128)(2,1)} %param.18) | copy-start | bytes 373252
  1.1 1.2 %copy-start.3 = (s32[1,4,64]{2,1,0:T(4,128)S(1)}, s32[1,4,64]{2,1,0:T(4,128)}, u32[]{:S(2)}) copy-start(s32[1,4,64]{2,1,0:T(4,128)} %lists_ref.1) | copy-start | bytes 3076
  2.3 6.2 %copy-start.7 = (f32[4,20,20]{2,0,1:T(4,128)S(1)}, f32[4,20,20]{2,0,1:T(4,128)}, u32[]{:S(2)}) copy-start(f32[4,20,20]{2,0,1:T(4,128)} %param.22) | copy-start | bytes 19204
  2.3 6.2 %copy-start.8 = (s32[20,256]{1,0:T(8,128)S(1)}, s32[20,256]{1,0:T(8,128)}, u32[]{:S(2)}) copy-start(s32[20,256]{1,0:T(8,128)} %yield_ref.1) | copy-start | bytes 61444
  2.3 6.2 %copy-start.9 = (f32[20,20]{1,0:T(8,128)S(1)}, f32[20,20]{1,0:T(8,128)}, u32[]{:S(2)}) copy-start(f32[20,20]{1,0:T(8,128)} %to_ref.1) | copy-start | bytes 4804
  2.3 6.2 %copy-start.10 = (f32[20,20]{1,0:T(8,128)S(1)}, f32[20,20]{1,0:T(8,128)}, u32[]{:S(2)}) copy-start(f32[20,20]{1,0:T(8,128)} %from_ref.1) | copy-start | bytes 4804
  2.3 6.2 %copy-start.11 = (s32[4,256]{1,0:T(4,128)S(1)}, s32[4,256]{1,0:T(4,128)}, u32[]{:S(2)}) copy-start(s32[4,256]{1,0:T(4,128)} %index_ref.1) | copy-start | bytes 12292
  2.4 6.2 %copy-start.12 = (s32[4,256]{1,0:T(4,128)S(1)}, s32[4,256]{1,0:T(4,128)}, u32[]{:S(2)}) copy-start(s32[4,256]{1,0:T(4,128)} %face_ref.1) | copy-start | bytes 12292
  2.4 6.2 %copy-start.14 = (f32[256]{0:T(256)S(1)}, f32[256]{0:T(256)}, u32[]{:S(2)}) copy-start(f32[256]{0:T(256)} %param.31) | copy-start | bytes 3076
  2.4 6.2 %copy-start.15 = (s32[1,256]{1,0:T(1,128)S(1)}, s32[1,256]{1,0:T(1,128)}, u32[]{:S(2)}) copy-start(s32[1,256]{1,0:T(1,128)} %damage_ref.1) | copy-start | bytes 3076
  2.8 5.8 %copy-start.6 = (f32[4,4,20,20]{3,1,2,0:T(4,128)S(1)}, f32[4,4,20,20]{3,1,2,0:T(4,128)}, u32[]{:S(2)}) copy-start(f32[4,4,20,20]{3,1,2,0:T(4,128)} %param.23) | copy-start | bytes 76804
  2.8 1.7 %collective-permute-start.1 = (f32[180,128]{1,0:T(8,128)S(1)}, f32[180,128]{1,0:T(8,128)S(1)}, u32[]{:S(2)}, u32[]{:S(2)}) collective-permute-start(f32[180,128]{1,0:T(8,128)S(1)} %get-tuple-element.37.near_ref), channel_id=1, source_target_pairs={{0,1},{1,0},{2,3},{3,2},{4,5},{5,4},{6,7},{7,6},{8,9},{9,8},{10,11... | collective-permute-start | bytes 276488 | tf_op jit(solution)/shard_map/ppermute | solution.py:475
  2.9 5.7 %copy-start.5 = (bf16[4,9,9,256]{3,0,2,1:T(4,128)(2,1)S(1)}, bf16[4,9,9,256]{3,0,2,1:T(4,128)(2,1)}, u32[]{:S(2)}) copy-start(bf16[4,9,9,256]{3,0,2,1:T(4,128)(2,1)} %param.20) | copy-start | bytes 497668
  2.9 5.7 %copy-start.4 = (bf16[4,9,9,256]{3,0,2,1:T(4,128)(2,1)S(1)}, bf16[4,9,9,256]{3,0,2,1:T(4,128)(2,1)}, u32[]{:S(2)}) copy-start(bf16[4,9,9,256]{3,0,2,1:T(4,128)(2,1)} %param.19) | copy-start | bytes 497668
  2.9 5.5 %collective-permute-start = (f32[180,128]{1,0:T(8,128)S(1)}, f32[180,128]{1,0:T(8,128)S(1)}, u32[]{:S(2)}, u32[]{:S(2)}) collective-permute-start(f32[180,128]{1,0:T(8,128)S(1)} %get-tuple-element.39), channel_id=1, source_target_pairs={{0,2},{1,3},{2,0},{3,1},{4,6},{5,7},{6,4},{7,5},{8,10},{9,11},{10,... | collective-permute-start | bytes 276488 | tf_op jit(solution)/shard_map/ppermute | solution.py:477
  4.5 8.5 %collective-permute-start.2 = (f32[180,128]{1,0:T(8,128)S(1)}, f32[180,128]{1,0:T(8,128)S(1)}, u32[]{:S(2)}, u32[]{:S(2)}) collective-permute-start(f32[180,128]{1,0:T(8,128)S(1)} %broadcast_select_fusion.1), channel_id=1, source_target_pairs={{0,0},{1,1},{30,30},{31,31},{2,4},{4,2},{3,5},{5,3},{6,8},{8,6},{7... | collective-permute-start | bytes 276488 | tf_op jit(solution)/shard_map/ppermute | solution.py:479
  8.4 4.2 %collective-permute-start.3 = (f32[180,128]{1,0:T(8,128)S(1)}, f32[180,128]{1,0:T(8,128)S(1)}, u32[]{:S(2)}, u32[]{:S(2)}) collective-permute-start(f32[180,128]{1,0:T(8,128)S(1)} %collective-permute-done.even_ref), channel_id=1, source_target_pairs={{0,1},{1,0},{2,3},{3,2},{4,5},{5,4},{6,7},{7,6},{8,9},{9,8},{10,11... | collective-permute-start | bytes 276488 | tf_op jit(solution)/shard_map/ppermute | solution.py:481
  8.5 0.7 %copy-start.13 = (s32[256]{0:T(256)S(1)}, s32[256]{0:T(256)}, u32[]{:S(2)}) copy-start(s32[256]{0:T(256)} %param.26) | copy-start | bytes 3076
  15.7 1.4 %collective-permute-start.5 = (f32[180,128]{1,0:T(8,128)S(1)}, f32[180,128]{1,0:T(8,128)S(1)}, u32[]{:S(2)}, u32[]{:S(2)}) collective-permute-start(f32[180,128]{1,0:T(8,128)S(1)} %get-tuple-element.52.near_ref), channel_id=1, source_target_pairs={{0,1},{1,0},{2,3},{3,2},{4,5},{5,4},{6,7},{7,6},{8,9},{9,8},{10,11... | collective-permute-start | bytes 276488 | tf_op jit(solution)/shard_map/ppermute | solution.py:475
  16.0 5.1 %collective-permute-start.4 = (f32[180,128]{1,0:T(8,128)S(1)}, f32[180,128]{1,0:T(8,128)S(1)}, u32[]{:S(2)}, u32[]{:S(2)}) collective-permute-start(f32[180,128]{1,0:T(8,128)S(1)} %get-tuple-element.54), channel_id=1, source_target_pairs={{0,2},{1,3},{2,0},{3,1},{4,6},{5,7},{6,4},{7,5},{8,10},{9,11},{10,... | collective-permute-start | bytes 276488 | tf_op jit(solution)/shard_map/ppermute | solution.py:477
  17.1 8.4 %collective-permute-start.6 = (f32[180,128]{1,0:T(8,128)S(1)}, f32[180,128]{1,0:T(8,128)S(1)}, u32[]{:S(2)}, u32[]{:S(2)}) collective-permute-start(f32[180,128]{1,0:T(8,128)S(1)} %broadcast_select_fusion), channel_id=1, source_target_pairs={{0,0},{1,1},{30,30},{31,31},{2,4},{4,2},{3,5},{5,3},{6,8},{8,6},{7... | collective-permute-start | bytes 276488 | tf_op jit(solution)/shard_map/ppermute | solution.py:479
  21.1 3.0 %collective-permute-start.7 = (f32[180,128]{1,0:T(8,128)S(1)}, f32[180,128]{1,0:T(8,128)S(1)}, u32[]{:S(2)}, u32[]{:S(2)}) collective-permute-start(f32[180,128]{1,0:T(8,128)S(1)} %collective-permute-done.4.even_ref), channel_id=1, source_target_pairs={{0,1},{1,0},{2,3},{3,2},{4,5},{5,4},{6,7},{7,6},{8,9},{9,8},{10,11... | collective-permute-start | bytes 276488 | tf_op jit(solution)/shard_map/ppermute | solution.py:481
